TPU v7x, 256 devices: a whole 4x4x8 slice. The times are simulated.
256 devices in a mesh: owner: 16 (over y_lo, z), blk: 16 (over y_hi, x, core).
Axes of the slice: x: 4, y: 4 (y_hi: 2, y_lo: 2; y = y_hi * 2 + y_lo), z: 8, core: 2. Of those that a mesh axis runs over, the one named last changes fastest.
Arguments:
- rhs_pivot: bfloat16 [16, 8192, 2048], P(None, 'owner', 'blk'), may hold values from -6 to 6
- block_pattern: int32 [16, 16, 16], P(None, 'owner', 'blk'), may hold values 0 or 1
- diag_inverse: bfloat16 [16, 8192, 512], P('blk', 'owner'), may hold values from -0.25 to 0.25
- right_factor: bfloat16 [16, 8192, 1024], P('blk', 'owner'), may hold values from -0.25 to 0.25
- left_factor: bfloat16 [16, 8192, 1024], P('blk', 'owner'), may hold values from -0.1875 to 0.1875
- tile_ranks: int32 [16, 16, 16], P('blk'), may hold values from 9 to 64
- contrib_rhs: bfloat16 [16, 8192, 2048], P('blk', 'owner'), may hold values from -6 to 6
- parent_map: int32 [16, 8192], replicated, may hold values from 0 to 8191, as said below
Outputs:
- pivot_solution: bfloat16 [16, 8192, 2048], P('blk', 'owner')
- parent_update: float32 [8192, 2048], P('owner', 'blk')
Inputs may be any that keep to these rules, and one draw needn't show every extreme that they name: Each front's row of parent_map names every parent row exactly once; of the 512 rows of one contribution tile at most 64 go to any one parent tile of 512 rows, and in every front some tile sends exactly 64 rows to some parent tile.
All inputs are finite; a program needn't handle non-finite values. No bound on the sum of `block_pattern` on one device may be relied on, other than what follows from the above.
Results may differ from a plain program's by a relative error of at most 0.0022.
Values may be sent and summed in bfloat16 or wider, within the bound.
No kernel may reach another device: no remote copies, remote signals or barrier semaphores. Data moves between devices by JAX's collectives and lax.ppermute only.
A program may use at most 192 MiB of HBM per device.

v0:
```python
import jax
import jax.numpy as jnp
from jax import lax
from jax.sharding import PartitionSpec as P

RK = 64


def per_device(
    rhs_pivot,
    block_pattern,
    diag_inverse,
    right_factor,
    left_factor,
    tile_ranks,
    contrib_rhs,
    parent_map,
):
    owner_index = lax.axis_index("owner")
    owner_count = lax.axis_size("owner")
    tile_rows = diag_inverse.shape[1]
    ranks_width = RK
    local_cols = rhs_pivot.shape[2]
    block_width = local_cols // block_pattern.shape[2]
    expand = jnp.repeat(block_pattern, block_width, axis=2).astype(jnp.bfloat16)
    masked = rhs_pivot * expand
    front_rhs = lax.all_to_all(masked, "blk", split_axis=0, concat_axis=2, tiled=True)
    fronts_here = front_rhs.shape[0]
    solved = jnp.einsum(
        "fst,ftc->fsc", diag_inverse, front_rhs, preferred_element_type=jnp.float32
    ).astype(jnp.bfloat16)
    rank_index = jnp.arange(ranks_width, dtype=jnp.int32)
    projected = jnp.einsum("ftq,ftc->fqc", right_factor, solved, preferred_element_type=jnp.float32)
    rank_here = lax.dynamic_index_in_dim(tile_ranks, owner_index, 2, keepdims=False)
    rank_mask = (rank_index[None, None, :] < rank_here[:, :, None]).reshape(fronts_here, -1)
    projected = jnp.where(rank_mask[..., None], projected, 0.0).astype(jnp.bfloat16)
    by_row = lax.all_to_all(projected, "owner", split_axis=1, concat_axis=1, tiled=True)
    product = jnp.einsum("ftq,fqc->ftc", left_factor, by_row, preferred_element_type=jnp.float32)
    reduced = contrib_rhs.astype(jnp.float32) - product
    owner_maps = lax.dynamic_slice_in_dim(parent_map, owner_index * tile_rows, tile_rows, 1)
    reduced_cols = lax.all_to_all(reduced, "blk", split_axis=2, concat_axis=0, tiled=True)
    parent_buffer = jnp.zeros((tile_rows * owner_count, local_cols), jnp.float32)
    parent_buffer = parent_buffer.at[owner_maps.reshape(-1)].add(
        reduced_cols.reshape(-1, local_cols)
    )
    parent_update = lax.psum_scatter(parent_buffer, "owner", scatter_dimension=0, tiled=True)
    return (solved, parent_update)


def solution(mesh):
    return jax.shard_map(
        per_device,
        mesh=mesh,
        in_specs=(
            P(None, "owner", "blk"),
            P(None, "owner", "blk"),
            P("blk", "owner", None),
            P("blk", "owner", None),
            P("blk", "owner", None),
            P("blk", None, None),
            P("blk", "owner", None),
            P(),
        ),
        out_specs=(P("blk", "owner", None), P("owner", "blk")),
        check_vma=False,
    )
```

profile of v0, /device:TPU:16, one launch (start us, length us, event | category | flops | bytes accessed | tf_op | source)
XLA Modules:
  0.0 459.2 jit_solution(12548970720188136085)
XLA Ops:
  7.2 0.0 copy-start
  7.2 0.0 copy-start.8
  7.2 2.9 copy.23
  10.1 0.0 copy-done.8
  10.2 0.0 copy-start.6
  10.2 1.5 broadcast_multiply_fusion
  11.7 7.3 %all-to-all-start = ((bf16[16,512,128]{1,2,0:T(8,128)(2,1)}), bf16[16,512,128]{1,2,0:T(8,128)(2,1)S(1)}, u32[]{:S(2)}, u32[]{:S(2)}) async-start(bf16[16,512,128]{1,2,0:T(8,128)(2,1)} %broadcast_multiply_fusion), calls=%async_computation | async-start | bytes 4194304 | tf_op jit(solution)/shard_map/all_to_all | solution.py:27
  19.0 0.0 copy-done.6
  19.0 0.2 dynamic-slice_reduce_fusion
  19.2 0.1 broadcast_reduce_fusion
  19.3 0.1 lt.50
  19.4 0.1 lt.47
  19.4 27.0 %all-to-all-done = bf16[16,512,128]{1,2,0:T(8,128)(2,1)S(1)} async-done(((bf16[16,512,128]{1,2,0:T(8,128)(2,1)}), bf16[16,512,128]{1,2,0:T(8,128)(2,1)S(1)}, u32[]{:S(2)}, u32[]{:S(2)}) %all-to-all-start) | async-done | bytes 2097184 | tf_op jit(solution)/shard_map/all_to_all | solution.py:27
  46.4 2.3 convolution_convert_fusion
  48.8 0.0 copy-start.3
  48.8 1.3 copy-done.3
  50.1 0.0 copy-done
  50.1 4.3 fusion
  54.4 20.6 %copy.25 = bf16[1,1024,2048]{2,0,1:T(2,128)(2,1)} copy(bf16[1,1024,2048]{1,2,0:T(8,128)(2,1)} %fusion) | data formatting | bytes 8388608 | tf_op jit(solution)/shard_map/convert_element_type | solution.py:36
  75.0 0.5 broadcast.45
  75.5 26.7 %reduce.6 = bf16[1024,2048]{1,0:T(8,128)(2,1)} reduce(bf16[1024,1,2048]{2,1,0:T(2,128)(2,1)} %bitcast.46, bf16[]{:T(256)} %broadcast.45), dimensions={1}, to_apply=%bitcast.42.reduce_sub_computation | reduce | bytes 8388610
  102.2 11.4 %reshape.127 = bf16[16,2,65536]{2,1,0:T(2,128)(2,1)} reshape(bf16[1024,2048]{1,0:T(8,128)(2,1)} %reduce.6) | data formatting | bytes 8388608
  113.5 0.0 copy-start.2
  113.5 9.5 %all-to-all-start.1 = ((bf16[16,2,65536]{2,1,0:T(2,128)(2,1)}), bf16[16,2,65536]{2,1,0:T(2,128)(2,1)}, u32[]{:S(2)}, u32[]{:S(2)}) async-start(bf16[16,2,65536]{2,1,0:T(2,128)(2,1)} %reshape.127), calls=%async_computation.1 | async-start | bytes 8388608 | tf_op jit(solution)/shard_map/all_to_all | solution.py:37
  123.0 0.0 copy-done.2
  123.0 2.5 copy.24
  125.6 0.0 copy-start.5
  125.6 0.0 copy-start.7
  125.6 92.4 %all-to-all-done.1 = bf16[16,2,65536]{2,1,0:T(2,128)(2,1)} async-done(((bf16[16,2,65536]{2,1,0:T(2,128)(2,1)}), bf16[16,2,65536]{2,1,0:T(2,128)(2,1)}, u32[]{:S(2)}, u32[]{:S(2)}) %all-to-all-start.1) | async-done | bytes 4194336 | tf_op jit(solution)/shard_map/all_to_all | solution.py:37
  218.0 12.3 %reshape.128 = bf16[1024,1,2048]{2,1,0:T(2,128)(2,1)} reshape(bf16[16,2,65536]{2,1,0:T(2,128)(2,1)} %all-to-all-done.1) | data formatting | bytes 8388608
  230.3 0.0 copy-done.5
  230.3 0.0 copy-done.7
  230.3 8.8 %bitcast_subtract_fusion = f32[1,512,2048]{1,2,0:T(8,128)S(1)} fusion(bf16[1,512,2048]{1,2,0:T(8,128)(2,1)S(1)} %copy-done.5, bf16[1,1024,2048]{2,0,1:T(2,128)(2,1)} %bitcast.47, bf16[1,512,1024]{2,1,0:T(8,128)(2,1)S(1)} %copy-done.7), kind=kOutput, calls=%fused_computation.6 | convolution fusion | flops 2149580800 | bytes 11534336 | tf_op jit(solution)/shard_map/ftq,fqc->ftc/dot_general | solution.py:38
  239.1 11.7 %copy.26 = f32[1,512,2048]{1,0,2:T(1,128)} copy(f32[1,512,2048]{1,2,0:T(8,128)S(1)} %bitcast_subtract_fusion) | data formatting | bytes 8388608 | tf_op jit(solution)/shard_map/sub | solution.py:39
  250.8 7.0 %all-to-all-start.2 = ((f32[1,512,2048]{1,0,2:T(1,128)}), f32[1,512,2048]{1,0,2:T(1,128)}, u32[]{:S(2)}, u32[]{:S(2)}) async-start(f32[1,512,2048]{1,0,2:T(1,128)} %copy.26), calls=%async_computation.2 | async-start | bytes 8388608 | tf_op jit(solution)/shard_map/all_to_all | solution.py:41
  257.8 0.0 reduce-scatter.2.cloned.1.call-start
  257.9 0.8 dynamic-slice_bitcast_fusion
  258.7 54.9 %all-to-all-done.2 = f32[1,512,2048]{1,0,2:T(1,128)} async-done(((f32[1,512,2048]{1,0,2:T(1,128)}), f32[1,512,2048]{1,0,2:T(1,128)}, u32[]{:S(2)}, u32[]{:S(2)}) %all-to-all-start.2) | async-done | bytes 4194336 | tf_op jit(solution)/shard_map/all_to_all | solution.py:41
  313.6 10.9 %copy.27 = f32[16,1,512,128]{3,2,0,1:T(8,128)} copy(f32[16,1,512,128]{2,1,3,0:T(1,128)} %bitcast.15) | data formatting | bytes 8388608 | tf_op jit(solution)/shard_map/all_to_all | solution.py:41
  324.5 0.0 copy-start.4
  324.5 46.6 %scatter_custom_fusion = f32[8192,128]{1,0:T(8,128)} fusion(s32[8192]{0:T(1024)S(1)} %bitcast.52, f32[8192,128]{1,0:T(8,128)} %bitcast.48, f32[]{:T(128)} %constant.7.clone.1), kind=kCustom, calls=%fused_computation.8 | custom fusion | flops 1048576 | bytes 4194816 | tf_op jit(solution)/shard_map/scatter-add | solution.py:43
  371.1 0.0 copy-start.1
  371.1 0.0 reduce-scatter.2.cloned.1.call-update
  371.1 0.0 copy-done.4
  371.1 2.4 copy.28
  373.5 78.8 %reduce-scatter.2.cloned.1.call-done = f32[512,128]{1,0:T(8,128)} async-done(((f32[8192,128]{1,0:T(8,128)}), f32[512,128]{1,0:T(8,128)}) %reduce-scatter.2.cloned.1.call-update) | async-done | bytes 262160 | tf_op jit(solution)/shard_map/reduce_scatter | solution.py:46
  452.3 0.0 copy-done.1
  (5 shorter events, 0.1 us)
Async XLA Ops:
  7.2 42.9 %copy-start = (bf16[1,512,1024]{2,1,0:T(8,128)(2,1)S(1)}, bf16[1,512,1024]{2,1,0:T(8,128)(2,1)}, u32[]{:S(2)}) copy-start(bf16[1,512,1024]{2,1,0:T(8,128)(2,1)} %param.11) | copy-start | bytes 3145732
  7.2 3.0 copy-start.8
  10.2 8.8 %copy-start.6 = (s32[1,16,16]{2,1,0:T(8,128)S(1)}, s32[1,16,16]{2,1,0:T(8,128)}, u32[]{:S(2)}) copy-start(s32[1,16,16]{2,1,0:T(8,128)} %param.13) | copy-start | bytes 3076
  11.7 34.7 %all-to-all-start = ((bf16[16,512,128]{1,2,0:T(8,128)(2,1)}), bf16[16,512,128]{1,2,0:T(8,128)(2,1)S(1)}, u32[]{:S(2)}, u32[]{:S(2)}) async-start(bf16[16,512,128]{1,2,0:T(8,128)(2,1)} %broadcast_multiply_fusion), calls=%async_computation | async-start | bytes 4194304 | tf_op jit(solution)/shard_map/all_to_all | solution.py:27
  48.8 1.3 copy-start.3
  113.5 9.5 %copy-start.2 = (bf16[1,512,2048]{2,1,0:T(8,128)(2,1)S(1)}, bf16[1,512,2048]{2,1,0:T(8,128)(2,1)}, u32[]{:S(2)}) copy-start(bf16[1,512,2048]{2,1,0:T(8,128)(2,1)} %param.14) | copy-start | bytes 6291460
  113.5 104.5 %all-to-all-start.1 = ((bf16[16,2,65536]{2,1,0:T(2,128)(2,1)}), bf16[16,2,65536]{2,1,0:T(2,128)(2,1)}, u32[]{:S(2)}, u32[]{:S(2)}) async-start(bf16[16,2,65536]{2,1,0:T(2,128)(2,1)} %reshape.127), calls=%async_computation.1 | async-start | bytes 8388608 | tf_op jit(solution)/shard_map/all_to_all | solution.py:37
  125.6 104.8 %copy-start.5 = (bf16[1,512,2048]{1,2,0:T(8,128)(2,1)S(1)}, bf16[1,512,2048]{1,2,0:T(8,128)(2,1)}, u32[]{:S(2)}) copy-start(bf16[1,512,2048]{1,2,0:T(8,128)(2,1)} %copy.24) | copy-start | bytes 6291460
  125.6 104.8 %copy-start.7 = (bf16[1,512,1024]{2,1,0:T(8,128)(2,1)S(1)}, bf16[1,512,1024]{2,1,0:T(8,128)(2,1)}, u32[]{:S(2)}) copy-start(bf16[1,512,1024]{2,1,0:T(8,128)(2,1)} %param.12) | copy-start | bytes 3145732
  250.8 62.7 %all-to-all-start.2 = ((f32[1,512,2048]{1,0,2:T(1,128)}), f32[1,512,2048]{1,0,2:T(1,128)}, u32[]{:S(2)}, u32[]{:S(2)}) async-start(f32[1,512,2048]{1,0,2:T(1,128)} %copy.26), calls=%async_computation.2 | async-start | bytes 8388608 | tf_op jit(solution)/shard_map/all_to_all | solution.py:41
  257.8 194.5 %reduce-scatter.2.cloned.1.call-start = ((), (), s32[]{:S(2)}) async-start(), calls=%async_computation.4 | async-start | bytes 4456448 | tf_op jit(solution)/shard_map/reduce_scatter | solution.py:46
  324.5 46.6 %copy-start.4 = (bf16[2048,512]{1,0:T(8,128)(2,1)S(1)}, bf16[2048,512]{1,0:T(8,128)(2,1)}, u32[]{:S(2)}) copy-start(bf16[2048,512]{1,0:T(8,128)(2,1)} %copy-done.3) | copy-start | bytes 6291460
  371.1 81.2 %copy-start.1 = (bf16[1,512,1024]{2,1,0:T(8,128)(2,1)S(1)}, bf16[1,512,1024]{2,1,0:T(8,128)(2,1)}, u32[]{:S(2)}) copy-start(bf16[1,512,1024]{2,1,0:T(8,128)(2,1)} %param.11) | copy-start | bytes 3145732
Sparse Core Ops, SparseCore 0:
  371.3 81.0 reduce-scatter.1
where the time goes:
time: 461 us; the launch traced here: 459 us
  waiting for transfers between devices  253 us (55%)
  local copies, waits for them, and re-layouts  77.9 us (17%)
  other arithmetic  74.9 us (16%)
  starting transfers between devices  23.8 us (5%)
  matrix products  15.4 us (3%)
  between operations  14.2 us (3%)
    all_to_all x1, waiting for transfers between devices, per_device(): lax.all_to_all(projected, 'owner', split_axis=1, concat_axis=1, tiled=True)  92.4 us
    reduce_scatter x1, waiting for transfers between devices, per_device(): lax.psum_scatter(parent_buffer, 'owner', scatter_dimension=0, tiled=True)  78.8 us
    all_to_all x1, waiting for transfers between devices, per_device(): lax.all_to_all(reduced, 'blk', split_axis=2, concat_axis=0, tiled=True)  54.9 us
    scatter-add x1, other arithmetic, per_device(): parent_buffer.at[owner_maps.reshape(-1)]  46.6 us
    unnamed x26, local copies, waits for them, and re-layouts  34.2 us
    all_to_all x1, waiting for transfers between devices, per_device(): lax.all_to_all(masked, 'blk', split_axis=0, concat_axis=2, tiled=True)  27 us
    unnamed x1, other arithmetic  26.7 us
    convert_element_type x1, local copies, waits for them, and re-layouts, per_device(): jnp.where(rank_mask[..., None], projected, 0.0).astype(jnp.bfloat16)  20.6 us
  transfers between devices with their start and end apart: 4, of which 4 were waited for; matrix products, arithmetic and copies ran while one was open for 1% of the time, Pallas kernels for 0%

commit v1 on v0

v1 whole, which is shorter than its diff:
```python
import functools

import jax
import jax.numpy as jnp
from jax import lax
from jax.experimental import pallas as pl
from jax.experimental.pallas import tpu as pltpu
from jax.sharding import PartitionSpec as P

RK = 64
CW = 128
WIN = 80
EXP_ROWS = 16
CODE_BITS = 14
VMEM_LIMIT = 48 * 1024 * 1024


def vmem():
    return pl.BlockSpec(memory_space=pltpu.VMEM)


def smem():
    return pl.BlockSpec(memory_space=pltpu.SMEM)


def params():
    return pltpu.CompilerParams(vmem_limit_bytes=VMEM_LIMIT)


def cost(flops, bytes_accessed):
    return pl.CostEstimate(flops=int(flops), bytes_accessed=int(bytes_accessed), transcendentals=0)


def groups_of(count):
    if count == 16:
        return [[0, 1, 2, 3], [4, 5, 8, 9, 12, 13, 10, 11], [14, 15, 6, 7]]
    order = list(range(count))
    return [order[: count // 4], order[count // 4 : 3 * count // 4], order[3 * count // 4 :]]


def mask_body(count, fronts_ref, pattern_ref, *refs):
    for step in range(count):
        keep = pattern_ref[fronts_ref[step]].astype(jnp.float32)
        source, target = refs[step], refs[count + step]
        target[...] = (source[0].astype(jnp.float32) * keep).astype(jnp.bfloat16)


def mask_fronts(rhs, pattern, fronts):
    count = fronts.shape[0]
    rows, cols = rhs.shape[1:]

    def pick(step):
        return lambda i, fronts_ref, pattern_ref: (fronts_ref[step], 0, 0)

    return pl.pallas_call(
        functools.partial(mask_body, count),
        out_shape=[jax.ShapeDtypeStruct((rows, cols), jnp.bfloat16)] * count,
        grid_spec=pltpu.PrefetchScalarGridSpec(
            num_scalar_prefetch=2,
            grid=(1,),
            in_specs=[pl.BlockSpec((1, rows, cols), pick(step)) for step in range(count)],
            out_specs=[pl.BlockSpec((rows, cols), lambda i, a, b: (0, 0))] * count,
        ),
        compiler_params=params(),
        cost_estimate=cost(count * rows * cols, 4 * count * rows * cols),
        name="mask_fronts",
    )(fronts, pattern, *([rhs] * count))


def right_body(right_ref, keep_ref, out_ref):
    kept = right_ref[...].astype(jnp.float32) * keep_ref[...]
    out_ref[...] = kept.T.astype(jnp.bfloat16)


def right_transposed(right, keep):
    rows, width = right.shape
    return pl.pallas_call(
        right_body,
        out_shape=jax.ShapeDtypeStruct((width, rows), jnp.bfloat16),
        in_specs=[vmem()] * 2,
        out_specs=vmem(),
        compiler_params=params(),
        cost_estimate=cost(rows * width, 4 * rows * width),
        name="right_transposed",
    )(right, keep)


def solve_body(count, inverse_ref, right_ref, *refs):
    sources = refs[:count]
    solved_ref, projected_ref = refs[count:]
    tiles = projected_ref.shape[0]
    for start in range(0, count, 2):
        width = min(2, count - start) * CW
        block = jnp.concatenate([ref[...] for ref in sources[start : start + 2]], axis=1)
        solved = jnp.dot(inverse_ref[...], block, preferred_element_type=jnp.float32)
        solved = solved.astype(jnp.bfloat16)
        for step in range(width // CW):
            solved_ref[start + step] = solved[:, step * CW : (step + 1) * CW]
        projected = jnp.dot(right_ref[...], solved, preferred_element_type=jnp.float32)
        projected_ref[:, :, start * CW : start * CW + width] = projected.astype(
            jnp.bfloat16
        ).reshape(tiles, RK, width)


def solve_group(inverse, right, blocks):
    count = len(blocks)
    rows = inverse.shape[0]
    width = right.shape[0]
    return pl.pallas_call(
        functools.partial(solve_body, count),
        out_shape=[
            jax.ShapeDtypeStruct((count, rows, CW), jnp.bfloat16),
            jax.ShapeDtypeStruct((width // RK, RK, count * CW), jnp.bfloat16),
        ],
        in_specs=[vmem()] * (2 + count),
        out_specs=[vmem()] * 2,
        compiler_params=params(),
        cost_estimate=cost(2 * rows * (rows + width) * count * CW, 2 * count * CW * (2 * rows + width)),
        name="solve_group",
    )(inverse, right, *blocks)


def place_body(starts, columns_ref, *refs):
    out_ref = refs[-1]
    step = pl.program_id(0)
    for begin, end, ref in zip(starts[:-1], starts[1:], refs[:-1]):

        @pl.when((step >= begin) & (step < end))
        def _(ref=ref):
            out_ref[0] = ref[0]


def place_blocks(columns, parts):
    starts = [0]
    for part in parts:
        starts.append(starts[-1] + part.shape[0])
    rows = parts[0].shape[1]

    def pick(begin, end):
        return lambda i, columns_ref: (jnp.clip(i - begin, 0, end - begin - 1), 0, 0)

    return pl.pallas_call(
        functools.partial(place_body, starts),
        out_shape=jax.ShapeDtypeStruct((1, rows, starts[-1] * CW), jnp.bfloat16),
        grid_spec=pltpu.PrefetchScalarGridSpec(
            num_scalar_prefetch=1,
            grid=(starts[-1],),
            in_specs=[
                pl.BlockSpec((1, rows, CW), pick(begin, end))
                for begin, end in zip(starts[:-1], starts[1:])
            ],
            out_specs=pl.BlockSpec((1, rows, CW), lambda i, columns_ref: (0, 0, columns_ref[i])),
        ),
        compiler_params=params(),
        cost_estimate=cost(0, 4 * rows * starts[-1] * CW),
        name="place_blocks",
    )(columns, *parts)


def order_row(row_keys, column_keys):
    smaller = (column_keys < row_keys).astype(jnp.float32)
    return jnp.sum(smaller, axis=0, keepdims=True)


def sort_body(columns_ref, row_ref, column_ref, left_ref, contrib_ref, left_out, contrib_out, one_hot):
    rows = row_ref.shape[1]

    @pl.when(pl.program_id(0) == 0)
    def _():
        rank = order_row(row_ref[...], column_ref[...])
        place = lax.broadcasted_iota(jnp.int32, (rows, rows), 0).astype(jnp.float32)
        one_hot[...] = (place == rank).astype(jnp.float32).astype(jnp.bfloat16)
        left = jnp.dot(one_hot[...], left_ref[...], preferred_element_type=jnp.float32)
        left_out[...] = left.astype(jnp.bfloat16)

    sorted_rows = jnp.dot(one_hot[...], contrib_ref[...], preferred_element_type=jnp.float32)
    contrib_out[0] = sorted_rows.astype(jnp.bfloat16)


def sort_rows(columns, keys, left, contrib):
    rows, width = left.shape
    count = columns.shape[0]
    return pl.pallas_call(
        sort_body,
        out_shape=[
            jax.ShapeDtypeStruct((rows, width), jnp.bfloat16),
            jax.ShapeDtypeStruct((count, rows, CW), jnp.bfloat16),
        ],
        grid_spec=pltpu.PrefetchScalarGridSpec(
            num_scalar_prefetch=1,
            grid=(count,),
            in_specs=[
                pl.BlockSpec((1, rows), lambda i, c: (0, 0)),
                pl.BlockSpec((rows, 1), lambda i, c: (0, 0)),
                pl.BlockSpec((rows, width), lambda i, c: (0, 0)),
                pl.BlockSpec((rows, CW), lambda i, c: (0, c[i])),
            ],
            out_specs=[
                pl.BlockSpec((rows, width), lambda i, c: (0, 0)),
                pl.BlockSpec((1, rows, CW), lambda i, c: (i, 0, 0)),
            ],
            scratch_shapes=[pltpu.VMEM((rows, rows), jnp.bfloat16)],
        ),
        compiler_params=params(),
        cost_estimate=cost(2 * rows * rows * (width + count * CW), 4 * rows * (width + count * CW)),
        name="sort_rows",
    )(columns, keys.reshape(1, rows), keys.reshape(rows, 1), left, contrib)


def target_body(row_ref, column_ref, out_ref):
    rows = row_ref.shape[2]
    keys = row_ref[0]
    rank = order_row(keys, column_ref[0])
    place = lax.broadcasted_iota(jnp.int32, (rows, rows), 0).astype(jnp.float32)
    ordered = jnp.sum(jnp.where(place == rank, keys, 0.0), axis=1, keepdims=True)
    out_ref[0] = jnp.broadcast_to(ordered, (rows, CW)).astype(jnp.int32)


def sorted_targets(maps):
    count, rows = maps.shape
    keys = maps.astype(jnp.float32)
    return pl.pallas_call(
        target_body,
        out_shape=jax.ShapeDtypeStruct((count, rows, CW), jnp.int32),
        grid=(count,),
        in_specs=[
            pl.BlockSpec((1, 1, rows), lambda i: (i, 0, 0)),
            pl.BlockSpec((1, rows, 1), lambda i: (i, 0, 0)),
        ],
        out_specs=pl.BlockSpec((1, rows, CW), lambda i: (i, 0, 0)),
        compiler_params=params(),
        cost_estimate=cost(5 * count * rows * rows, 4 * count * rows * CW),
        name="sorted_targets",
    )(keys.reshape(count, 1, rows), keys.reshape(count, rows, 1))


def update_body(count, first, left_ref, projected_ref, contrib_ref, *out_refs):
    rows, width = left_ref.shape
    for start in range(0, count, 2):
        span = min(2, count - start)
        part = projected_ref[:, :, start * CW : (start + span) * CW].reshape(width, span * CW)
        product = jnp.dot(left_ref[...], part, preferred_element_type=jnp.float32)
        for step in range(span):
            reduced = contrib_ref[first + start + step].astype(jnp.float32)
            reduced = reduced - product[:, step * CW : (step + 1) * CW]
            top = jnp.max(jnp.abs(reduced), axis=0, keepdims=True)
            exponent = jnp.floor(jnp.log2(jnp.maximum(top, 2.0**-108))) + 1.0
            scale = jnp.exp2(CODE_BITS - exponent)
            code = jnp.floor(reduced * scale + 0.5).astype(jnp.int32)
            out = out_refs[start + step]
            out[:rows, :] = code.astype(jnp.int16)
            out[rows:, :] = jnp.broadcast_to(exponent.astype(jnp.int32), (EXP_ROWS, CW)).astype(jnp.int16)


def update_group(left, projected, contrib, first):
    rows, width = left.shape
    count = projected.shape[2] // CW
    return pl.pallas_call(
        functools.partial(update_body, count, first),
        out_shape=[jax.ShapeDtypeStruct((rows + EXP_ROWS, CW), jnp.int16)] * count,
        in_specs=[vmem()] * 3,
        out_specs=[vmem()] * count,
        compiler_params=params(),
        cost_estimate=cost(2 * rows * width * count * CW, 2 * count * CW * (width + 2 * rows)),
        name="update_group",
    )(left, projected, contrib)


def scatter_body(count, first, has_partial, starts_ref, targets_ref, *refs):
    sources = refs[:count]
    partial_ref = refs[count] if has_partial else None
    out_ref, values, one_hot = refs[-3:]
    rows = targets_ref.shape[1]
    tile = pl.program_id(0)

    @pl.when(tile == 0)
    def _():
        for step in range(count):
            code = sources[step][:rows, :].astype(jnp.int32).astype(jnp.float32)
            exponent = sources[step][rows:, :].astype(jnp.int32).astype(jnp.float32)[:1]
            value = code * jnp.exp2(exponent - CODE_BITS)
            high = value.astype(jnp.bfloat16)
            low = (value - high.astype(jnp.float32)).astype(jnp.bfloat16)
            values[step * rows : (step + 1) * rows, :CW] = high
            values[step * rows : (step + 1) * rows, CW:] = low

    parts = []
    lane = lax.broadcasted_iota(jnp.int32, (WIN, rows), 1) + tile * rows
    for step in range(count):
        begin = jnp.minimum((starts_ref[first + step, tile] // 16) * 16, rows - WIN)
        begin = pl.multiple_of(begin, 16)
        target = targets_ref[first + step, pl.ds(begin, WIN), :]
        target = jnp.concatenate([target] * (rows // CW), axis=1)
        match = jnp.where(target == lane, 1.0, 0.0)
        one_hot[step * WIN : (step + 1) * WIN, :] = match.astype(jnp.bfloat16)
        parts.append(values[pl.ds(pl.multiple_of(step * rows + begin, 16), WIN), :])
    window = jnp.concatenate(parts, axis=0)
    total = lax.dot_general(
        window, one_hot[...], (((0,), (0,)), ((), ())), preferred_element_type=jnp.float32
    )
    total = total[:CW] + total[CW:]
    if has_partial:
        total = total + partial_ref[0]
    out_ref[0] = total.astype(out_ref.dtype)


def scatter_rows(starts, targets, first, coded, partial, out_dtype):
    count = len(coded)
    rows = targets.shape[1]
    tiles = starts.shape[1]
    has_partial = partial is not None
    tile_spec = pl.BlockSpec((1, CW, rows), lambda t: (t, 0, 0))
    whole = pl.BlockSpec((rows + EXP_ROWS, CW), lambda t: (0, 0))
    extra = [tile_spec] if has_partial else []
    operands = [partial] if has_partial else []
    return pl.pallas_call(
        functools.partial(scatter_body, count, first, has_partial),
        out_shape=jax.ShapeDtypeStruct((tiles, CW, rows), out_dtype),
        grid=(tiles,),
        in_specs=[smem(), pl.BlockSpec(targets.shape, lambda t: (0, 0, 0))] + [whole] * count + extra,
        out_specs=tile_spec,
        scratch_shapes=[
            pltpu.VMEM((count * rows, 2 * CW), jnp.bfloat16),
            pltpu.VMEM((count * WIN, rows), jnp.bfloat16),
        ],
        compiler_params=params(),
        cost_estimate=cost(4 * CW * count * WIN * rows * tiles, 8 * tiles * CW * rows),
        name="scatter_rows",
    )(starts, targets, *coded, *operands)


def total_body(parts_ref, out_ref):
    total = jnp.sum(parts_ref[...].astype(jnp.float32), axis=0)
    out_ref[...] = total.T


def total_rows(parts):
    tiles, cols, rows = parts.shape
    return pl.pallas_call(
        total_body,
        out_shape=jax.ShapeDtypeStruct((rows, cols), jnp.float32),
        grid=(rows // CW,),
        in_specs=[pl.BlockSpec((tiles, cols, CW), lambda i: (0, 0, i))],
        out_specs=pl.BlockSpec((CW, cols), lambda i: (i, 0)),
        compiler_params=params(),
        cost_estimate=cost(tiles * cols * rows, 2 * tiles * cols * rows),
        name="total_rows",
    )(parts)


def after(first, *later):
    held = lax.optimization_barrier((first,) + later)
    return held[1:]


def per_device(
    rhs_pivot,
    block_pattern,
    diag_inverse,
    right_factor,
    left_factor,
    tile_ranks,
    contrib_rhs,
    parent_map,
):
    owner = lax.axis_index("owner")
    blk = lax.axis_index("blk")
    partners = lax.axis_size("blk")
    inverse, right = diag_inverse[0], right_factor[0]
    left, contrib = left_factor[0], contrib_rhs[0]
    rows = inverse.shape[0]
    tiles = lax.axis_size("owner")
    groups = groups_of(partners)
    order = sum(groups, [])
    firsts = [order.index(group[0]) for group in groups]
    columns = jnp.bitwise_xor(blk, jnp.array(order, jnp.int32))
    pattern = block_pattern.reshape(-1)

    def exchange(value, k):
        if k == 0:
            return value
        return lax.ppermute(value, "blk", [(i, i ^ k) for i in range(partners)])

    ranks_here = lax.dynamic_index_in_dim(tile_ranks[0], owner, 1, keepdims=False)
    keep = jnp.arange(RK, dtype=jnp.int32)[None, :] < ranks_here[:, None]
    keep = keep.astype(jnp.float32).reshape(1, -1)

    received = []
    for first, group in zip(firsts, groups):
        masked = mask_fronts(rhs_pivot, pattern, columns[first : first + len(group)])
        received.append([exchange(value, k) for value, k in zip(masked, group)])

    right_t = right_transposed(right, keep)

    solved, projected = [], []
    for blocks in received:
        part, sent = solve_group(inverse, right_t, blocks)
        solved.append(part)
        projected.append(lax.all_to_all(sent, "owner", split_axis=0, concat_axis=0, tiled=True))

    maps = lax.dynamic_slice_in_dim(parent_map, owner * rows, rows, 1)
    maps = jnp.take(maps, columns, axis=0)
    own_keys = lax.dynamic_slice_in_dim(
        lax.dynamic_index_in_dim(parent_map, blk, 0, keepdims=False), owner * rows, rows, 0
    ).astype(jnp.float32)
    edges = jnp.arange(tiles, dtype=jnp.int32) * rows
    starts = jnp.sum((maps[:, :, None] < edges[None, None, :]).astype(jnp.int32), axis=1)
    own_keys, maps = after(solved[0], own_keys, maps)
    left_sorted, contrib_sorted = sort_rows(columns, own_keys, left, contrib)
    targets = sorted_targets(maps)

    arrived = []
    for first, group, part in zip(firsts, groups, projected):
        coded = update_group(left_sorted, part, contrib_sorted, first)
        arrived.append([exchange(value, k) for value, k in zip(coded, group)])

    partial = scatter_rows(starts, targets, 0, arrived[0] + arrived[1], None, jnp.float32)
    parts = scatter_rows(starts, targets, firsts[2], arrived[2], partial, jnp.bfloat16)
    parts = lax.all_to_all(parts, "owner", split_axis=0, concat_axis=0, tiled=True)
    parent_update = total_rows(parts)
    pivot_solution = place_blocks(columns, solved)
    return (pivot_solution, parent_update)


def solution(mesh):
    return jax.shard_map(
        per_device,
        mesh=mesh,
        in_specs=(
            P(None, "owner", "blk"),
            P(None, "owner", "blk"),
            P("blk", "owner", None),
            P("blk", "owner", None),
            P("blk", "owner", None),
            P("blk", None, None),
            P("blk", "owner", None),
            P(),
        ),
        out_specs=(P("blk", "owner", None), P("owner", "blk")),
        check_vma=False,
    )
```

time: 461 us -> 289 us (0.63)
  waiting for transfers between devices: 253 us -> 96.1 us
  other arithmetic: 74.9 us -> 2.07 us
  Pallas kernels: 0 us -> 71.2 us
  starting transfers between devices: 23.8 us -> 91.3 us
  local copies, waits for them, and re-layouts: 77.9 us -> 24.3 us
  matrix products: 15.4 us -> 0 us
  between operations: 14.2 us -> 1.12 us
    all_to_all x3 -> x4, waiting for transfers between devices: 174 us -> 66.5 us  [the longest x1 40.7 us: per_device(): lax.all_to_all(parts, 'owner', split_axis=0, concat_axis=0, tiled=True)]
    reduce_scatter x1 -> x0, waiting for transfers between devices: 78.8 us -> none  [per_device(): lax.psum_scatter(parent_buffer, 'owner', scatter_dimension=0, tiled=True)]
    pallas_call x0 -> x16, Pallas kernels: none -> 71.2 us  [the longest x2 24.4 us: scatter_rows(): pl.pallas_call(functools.partial(scatter_body, count, first, has_partial)...]
    ppermute x0 -> x30, starting transfers between devices: none -> 57.8 us  [exchange(): return lax.ppermute(value, 'blk', [(i, i ^ k) for i in range(partners)])]
    scatter-add x1 -> x0, other arithmetic: 46.6 us -> none  [per_device(): parent_buffer.at[owner_maps.reshape(-1)]]
    ppermute x0 -> x30, waiting for transfers between devices: none -> 29.6 us  [exchange(): return lax.ppermute(value, 'blk', [(i, i ^ k) for i in range(partners)])]
    unnamed x1 -> x0, other arithmetic: 26.7 us -> none
    convert_element_type x1, local copies, waits for them, and re-layouts: 20.6 us -> 0.08 us  [per_device(): keep = keep.astype(jnp.float32).reshape(1, -1)]
  transfers between devices with their start and end apart: 4 -> 34, of which waited for: 4 -> 8; matrix products, arithmetic and copies ran while one was open for 1% -> 2% of each run, Pallas kernels for 0% -> 19%
where the time goes in v1:
time: 289 us; the launch traced here: 286 us
  waiting for transfers between devices  96.1 us (33%)
  starting transfers between devices  91.3 us (32%)
  Pallas kernels  71.2 us (25%)
  local copies, waits for them, and re-layouts  24.3 us (8%)
    ppermute x30, starting transfers between devices, exchange(): return lax.ppermute(value, 'blk', [(i, i ^ k) for i in range(partners)])  57.8 us
    all_to_all x1, waiting for transfers between devices, per_device(): lax.all_to_all(parts, 'owner', split_axis=0, concat_axis=0, tiled=True)  40.7 us
    ppermute x30, waiting for transfers between devices, exchange(): return lax.ppermute(value, 'blk', [(i, i ^ k) for i in range(partners)])  29.6 us
    all_to_all x3, waiting for transfers between devices, per_device(): lax.all_to_all(sent, 'owner', split_axis=0, concat_axis=0, tiled=True)  25.7 us
    all_to_all x3, starting transfers between devices, per_device(): lax.all_to_all(sent, 'owner', split_axis=0, concat_axis=0, tiled=True)  25.2 us
    pallas_call x2, Pallas kernels, scatter_rows(): pl.pallas_call(functools.partial(scatter_body, count, first, has_partial)...  24.4 us
    unnamed x74, local copies, waits for them, and re-layouts  19.7 us
    pallas_call x1, Pallas kernels, sort_rows(): pl.pallas_call(sort_body, out_shape=[jax.ShapeDtypeStruct((rows, width),...  11.5 us
  transfers between devices with their start and end apart: 34, of which 8 were waited for; matrix products, arithmetic and copies ran while one was open for 2% of the time, Pallas kernels for 19%

profile of v1, /device:TPU:16, one launch (start us, length us, event | category | flops | bytes accessed | tf_op | source)
XLA Modules:
  0.0 286.1 jit_solution(4011324826023248804)
XLA Ops:
  0.6 0.7 broadcast_xor_fusion.columns_ref
  1.4 1.6 copy-done.1
  4.4 1.6 collective-permute-start.1
  7.0 3.8 %collective-permute-done.1.refs_2_ = bf16[512,128]{1,0:T(8,128)(2,1)S(1)} collective-permute-done((bf16[512,128]{1,0:T(8,128)(2,1)S(1)}, bf16[512,128]{1,0:T(8,128)(2,1)S(1)}, u32[]{:S(2)}, u32[]{:S(2)}) %collective-permute-start.1) | collective-permute-done | bytes 131104 | tf_op jit(solution)/shard_map/ppermute | solution.py:382
  10.8 1.9 collective-permute-done.2.refs_3_
  12.6 1.3 solve_group.3
  14.0 1.0 copy-done.12
  14.9 1.0 copy-done.15
  15.9 0.8 copy-done.16
  16.7 9.3 %all-to-all-start.1 = ((bf16[16,64,512]{2,1,0:T(8,128)(2,1)}), bf16[16,64,512]{2,1,0:T(8,128)(2,1)S(1)}, u32[]{:S(2)}, u32[]{:S(2)}) async-start(bf16[16,64,512]{2,1,0:T(8,128)(2,1)} %copy-done.15), calls=%async_computation.1 | async-start | bytes 2097152 | tf_op jit(solution)/shard_map/all_to_all | solution.py:399
  26.1 0.7 mask_fronts.4
  26.9 3.1 %collective-permute-start.3 = (bf16[512,128]{1,0:T(8,128)(2,1)S(1)}, bf16[512,128]{1,0:T(8,128)(2,1)S(1)}, u32[]{:S(2)}, u32[]{:S(2)}) collective-permute-start(bf16[512,128]{1,0:T(8,128)(2,1)S(1)} %get-tuple-element.49), channel_id=1, source_target_pairs={{0,4},{1,5},{2,6},{3,7},{4,0},{5,1},{6,2},{7,3},{8,12},{9,13},{10,... | collective-permute-start | bytes 393224 | tf_op jit(solution)/shard_map/ppermute | solution.py:382
  30.6 2.8 collective-permute-start.6
  33.4 3.1 %collective-permute-start.7 = (bf16[512,128]{1,0:T(8,128)(2,1)S(1)}, bf16[512,128]{1,0:T(8,128)(2,1)S(1)}, u32[]{:S(2)}, u32[]{:S(2)}) collective-permute-start(bf16[512,128]{1,0:T(8,128)(2,1)S(1)} %get-tuple-element.53), channel_id=1, source_target_pairs={{0,12},{1,13},{2,14},{3,15},{4,8},{5,9},{6,10},{7,11},{8,4},{9,5},... | collective-permute-start | bytes 393224 | tf_op jit(solution)/shard_map/ppermute | solution.py:382
  36.5 2.3 collective-permute-start.8
  38.9 1.4 collective-permute-start.9
  40.3 3.0 %collective-permute-start.10 = (bf16[512,128]{1,0:T(8,128)(2,1)S(1)}, bf16[512,128]{1,0:T(8,128)(2,1)S(1)}, u32[]{:S(2)}, u32[]{:S(2)}) collective-permute-start(bf16[512,128]{1,0:T(8,128)(2,1)S(1)} %get-tuple-element.56), channel_id=1, source_target_pairs={{0,11},{1,10},{2,9},{3,8},{4,15},{5,14},{6,13},{7,12},{8,3},{9,2},... | collective-permute-start | bytes 393224 | tf_op jit(solution)/shard_map/ppermute | solution.py:382
  43.3 13.7 %collective-permute-done.6.refs_3_ = bf16[512,128]{1,0:T(8,128)(2,1)S(1)} collective-permute-done((bf16[512,128]{1,0:T(8,128)(2,1)S(1)}, bf16[512,128]{1,0:T(8,128)(2,1)S(1)}, u32[]{:S(2)}, u32[]{:S(2)}) %collective-permute-start.6) | collective-permute-done | bytes 131104 | tf_op jit(solution)/shard_map/ppermute | solution.py:382
  57.0 2.2 solve_group.4
  59.1 1.3 copy-done.8
  60.5 1.0 copy-done.9
  61.4 10.5 %all-to-all-start.2 = ((bf16[16,64,1024]{2,1,0:T(8,128)(2,1)}), bf16[16,64,1024]{2,1,0:T(8,128)(2,1)}, u32[]{:S(2)}, u32[]{:S(2)}) async-start(bf16[16,64,1024]{2,1,0:T(8,128)(2,1)} %copy-done.8), calls=%async_computation.2 | async-start | bytes 4194304 | tf_op jit(solution)/shard_map/all_to_all | solution.py:399
  72.6 4.2 %collective-permute-start.11 = (bf16[512,128]{1,0:T(8,128)(2,1)S(1)}, bf16[512,128]{1,0:T(8,128)(2,1)S(1)}, u32[]{:S(2)}, u32[]{:S(2)}) collective-permute-start(bf16[512,128]{1,0:T(8,128)(2,1)S(1)} %get-tuple-element.58), channel_id=1, source_target_pairs={{0,14},{1,15},{2,12},{3,13},{4,10},{5,11},{6,8},{7,9},{8,6},{9,7},... | collective-permute-start | bytes 393224 | tf_op jit(solution)/shard_map/ppermute | solution.py:382
  76.8 4.2 %collective-permute-start.13 = (bf16[512,128]{1,0:T(8,128)(2,1)S(1)}, bf16[512,128]{1,0:T(8,128)(2,1)S(1)}, u32[]{:S(2)}, u32[]{:S(2)}) collective-permute-start(bf16[512,128]{1,0:T(8,128)(2,1)S(1)} %get-tuple-element.60), channel_id=1, source_target_pairs={{0,6},{1,7},{2,4},{3,5},{4,2},{5,3},{6,0},{7,1},{8,14},{9,15},{10,... | collective-permute-start | bytes 393224 | tf_op jit(solution)/shard_map/ppermute | solution.py:382
  81.6 2.2 collective-permute-done.11.refs_0_
  83.8 4.9 %collective-permute-done.12.refs_1_ = bf16[512,128]{1,0:T(8,128)(2,1)S(1)} collective-permute-done((bf16[512,128]{1,0:T(8,128)(2,1)S(1)}, bf16[512,128]{1,0:T(8,128)(2,1)S(1)}, u32[]{:S(2)}, u32[]{:S(2)}) %collective-permute-start.12) | collective-permute-done | bytes 131104 | tf_op jit(solution)/shard_map/ppermute | solution.py:382
  88.7 3.1 %collective-permute-done.14.refs_3_ = bf16[512,128]{1,0:T(8,128)(2,1)S(1)} collective-permute-done((bf16[512,128]{1,0:T(8,128)(2,1)S(1)}, bf16[512,128]{1,0:T(8,128)(2,1)S(1)}, u32[]{:S(2)}, u32[]{:S(2)}) %collective-permute-start.14) | collective-permute-done | bytes 131104 | tf_op jit(solution)/shard_map/ppermute | solution.py:382
  91.8 2.3 solve_group.5
  94.1 0.8 copy-done.18
  94.9 25.7 %all-to-all-done.2.projected_ref = bf16[16,64,1024]{2,1,0:T(8,128)(2,1)} async-done(((bf16[16,64,1024]{2,1,0:T(8,128)(2,1)}), bf16[16,64,1024]{2,1,0:T(8,128)(2,1)}, u32[]{:S(2)}, u32[]{:S(2)}) %all-to-all-start.2) | async-done | bytes 2097184 | tf_op jit(solution)/shard_map/all_to_all | solution.py:399
  120.6 5.5 %all-to-all-start = ((bf16[16,64,512]{2,1,0:T(8,128)(2,1)}), bf16[16,64,512]{2,1,0:T(8,128)(2,1)}, u32[]{:S(2)}, u32[]{:S(2)}) async-start(bf16[16,64,512]{2,1,0:T(8,128)(2,1)} %get-tuple-element.66), calls=%async_computation | async-start | bytes 2097152 | tf_op jit(solution)/shard_map/all_to_all | solution.py:399
  126.1 0.8 constant_dynamic-slice_fusion
  127.5 0.8 dynamic-slice_convert_fusion
  128.5 1.2 copy-done.22
  129.7 11.5 %sort_rows.1 = (bf16[512,1024]{1,0:T(8,128)(2,1)S(1)}, bf16[16,512,128]{2,1,0:T(8,128)(2,1)S(1)}) custom-call(s32[16]{0:T(128)S(1)} %broadcast_xor_fusion.columns_ref, f32[1,512]{1,0:T(1,128)S(1)} %dynamic-slice_convert_fusion, f32[512,1]{1,0:T(8,128)S(1)} %copy.15.column_ref, bf16[512,1024]{1,0:T(8,128)(2,1)S(1)} %bitcast.15, bf16[512,2048]{1,0:T(8,128)(2,1)} %bitcast.19), custom_call_target="tpu_custom_call" | custom-call | flops 1610612736 | bytes 6291456 | tf_op jit(solution)/shard_map/sort_rows/pallas_call | solution.py:183
  141.3 1.0 update_group.4
  142.6 4.4 %collective-permute-start.20 = (s16[528,128]{1,0:T(8,128)(2,1)S(1)}, s16[528,128]{1,0:T(8,128)(2,1)S(1)}, u32[]{:S(2)}, u32[]{:S(2)}) collective-permute-start(s16[528,128]{1,0:T(8,128)(2,1)S(1)} %get-tuple-element.75), channel_id=1, source_target_pairs={{0,2},{1,3},{2,0},{3,1},{4,6},{5,7},{6,4},{7,5},{8,10},{9,11},{10,... | collective-permute-start | bytes 405512 | tf_op jit(solution)/shard_map/ppermute | solution.py:382
  147.2 4.8 %update_group.5 = (s16[528,128]{1,0:T(8,128)(2,1)S(1)}, s16[528,128]{1,0:T(8,128)(2,1)S(1)}, s16[528,128]{1,0:T(8,128)(2,1)S(1)}, s16[528,128]{1,0:T(8,128)(2,1)...) custom-call(bf16[512,1024]{1,0:T(8,128)(2,1)S(1)} %get-tuple-element.65, ...), custom_call_target="tpu_custom_call" | custom-call | flops 1073741824 | bytes 4194304 | tf_op jit(solution)/shard_map/update_group/pallas_call | solution.py:258
  152.0 3.8 %collective-permute-start.22 = (s16[528,128]{1,0:T(8,128)(2,1)S(1)}, s16[528,128]{1,0:T(8,128)(2,1)S(1)}, u32[]{:S(2)}, u32[]{:S(2)}) collective-permute-start(s16[528,128]{1,0:T(8,128)(2,1)S(1)} %get-tuple-element.78), channel_id=1, source_target_pairs={{0,4},{1,5},{2,6},{3,7},{4,0},{5,1},{6,2},{7,3},{8,12},{9,13},{10,... | collective-permute-start | bytes 405512 | tf_op jit(solution)/shard_map/ppermute | solution.py:382
  155.8 1.2 collective-permute-start.24
  157.4 1.9 collective-permute-start.25
  159.3 0.7 copy-done.28
  160.0 4.1 %collective-permute-start.26 = (s16[528,128]{1,0:T(8,128)(2,1)}, s16[528,128]{1,0:T(8,128)(2,1)}, u32[]{:S(2)}, u32[]{:S(2)}) collective-permute-start(s16[528,128]{1,0:T(8,128)(2,1)} %get-tuple-element.82), channel_id=1, source_target_pairs={{0,12},{1,13},{2,14},{3,15},{4,8},{5,9},{6,10},{7,11},{8,4},{9,5},... | collective-permute-start | bytes 405512 | tf_op jit(solution)/shard_map/ppermute | solution.py:382
  164.8 1.8 collective-permute-start.27
  167.2 1.7 collective-permute-start.28
  168.9 0.7 copy-done.34
  169.6 2.2 collective-permute-start.29
  171.8 2.7 copy.14.column_ref
  174.5 11.2 %sorted_targets.1.targets_ref = s32[16,512,128]{2,1,0:T(8,128)S(1)} custom-call(f32[16,1,512]{2,1,0:T(1,128)S(1)} %reshape.78.row_ref, f32[16,512,1]{2,1,0:T(8,128)} %copy.14.column_ref), custom_call_target="tpu_custom_call" | custom-call | flops 20971520 | bytes 4194304 | tf_op jit(solution)/shard_map/sorted_targets/pallas_call | solution.py:222
  185.7 2.0 copy-done.5
  187.7 2.3 update_group.3
  190.0 4.4 %collective-permute-start.15 = (s16[528,128]{1,0:T(8,128)(2,1)S(1)}, s16[528,128]{1,0:T(8,128)(2,1)S(1)}, u32[]{:S(2)}, u32[]{:S(2)}) collective-permute-start(s16[528,128]{1,0:T(8,128)(2,1)S(1)} %get-tuple-element.68), channel_id=1, source_target_pairs={{0,14},{1,15},{2,12},{3,13},{4,10},{5,11},{6,8},{7,9},{8,6},{9,7},... | collective-permute-start | bytes 405512 | tf_op jit(solution)/shard_map/ppermute | solution.py:382
  194.5 1.2 collective-permute-start.16
  195.7 3.4 %collective-permute-start.17 = (s16[528,128]{1,0:T(8,128)(2,1)S(1)}, s16[528,128]{1,0:T(8,128)(2,1)S(1)}, u32[]{:S(2)}, u32[]{:S(2)}) collective-permute-start(s16[528,128]{1,0:T(8,128)(2,1)S(1)} %get-tuple-element.70), channel_id=1, source_target_pairs={{0,6},{1,7},{2,4},{3,5},{4,2},{5,3},{6,0},{7,1},{8,14},{9,15},{10,... | collective-permute-start | bytes 405512 | tf_op jit(solution)/shard_map/ppermute | solution.py:382
  199.4 11.7 %scatter_rows.2.refs_4_ = f32[16,128,512]{2,1,0:T(8,128)S(1)} custom-call(s32[16,16]{1,0:T(8,128)S(1)} %convert_reduce_fusion.starts_ref, s32[16,512,128]{2,1,0:T(8,128)} %copy-done.5, s16[528,128]{1,0:T(8,128)(2,1)S(1)} %get-tuple-element.73.refs_0_, s16[528,128]{1,0:T(8,128)(2,1)S(1)} %collective-permute-done.19.refs_1_, s16[528,128]{1,0:T(8,128)(2,1)S(1)} %copy-done.27, ...), custom_call_target="tpu_custom_call" | custom-call | flops 4026531840 | bytes 8388608 | tf_op jit(solution)/shard_map/scatter_rows/pallas_call | solution.py:316
  211.1 2.0 copy-done.7
  213.1 12.6 %scatter_rows.3 = bf16[16,128,512]{2,1,0:T(8,128)(2,1)S(1)} custom-call(s32[16,16]{1,0:T(8,128)S(1)} %convert_reduce_fusion.starts_ref, s32[16,512,128]{2,1,0:T(8,128)} %copy-done.5, s16[528,128]{1,0:T(8,128)(2,1)S(1)} %collective-permute-done.15.refs_0_, s16[528,128]{1,0:T(8,128)(2,1)S(1)} %collective-permute-done.16.refs_1_, ...), custom_call_target="tpu_custom_call" | custom-call | flops 1342177280 | bytes 8388608 | tf_op jit(solution)/shard_map/scatter_rows/pallas_call | solution.py:316
  225.8 1.3 copy-done.6
  227.1 8.2 %all-to-all-start.3 = ((bf16[16,128,512]{2,1,0:T(8,128)(2,1)}), bf16[16,128,512]{2,1,0:T(8,128)(2,1)S(1)}, u32[]{:S(2)}, u32[]{:S(2)}) async-start(bf16[16,128,512]{2,1,0:T(8,128)(2,1)} %copy-done.6), calls=%async_computation.3 | async-start | bytes 4194304 | tf_op jit(solution)/shard_map/all_to_all | solution.py:419
  235.3 1.0 copy-done.17
  236.4 1.0 copy-done.19
  237.4 5.9 %place_blocks.1 = bf16[1,512,2048]{2,1,0:T(8,128)(2,1)} custom-call(s32[16]{0:T(128)S(1)} %broadcast_xor_fusion.columns_ref, bf16[4,512,128]{2,1,0:T(8,128)(2,1)S(1)} %copy-done.17, bf16[8,512,128]{2,1,0:T(8,128)(2,1)S(1)} %copy-done.10, bf16[4,512,128]{2,1,0:T(8,128)(2,1)S(1)} %copy-done.19), custom_call_target="tpu_custom_call" | custom-call | bytes 4194304 | tf_op jit(solution)/shard_map/place_blocks/pallas_call | solution.py:142
  243.3 40.7 %all-to-all-done.3.parts_ref = bf16[16,128,512]{2,1,0:T(8,128)(2,1)S(1)} async-done(((bf16[16,128,512]{2,1,0:T(8,128)(2,1)}), bf16[16,128,512]{2,1,0:T(8,128)(2,1)S(1)}, u32[]{:S(2)}, u32[]{:S(2)}) %all-to-all-start.3) | async-done | bytes 2097184 | tf_op jit(solution)/shard_map/all_to_all | solution.py:419
  284.1 2.0 total_rows.1
  (112 shorter events, 7.8 us)
Async XLA Ops:
  0.6 5.6 %copy-start = (s32[1,16,16]{2,1,0:T(8,128)S(1)}, s32[1,16,16]{2,1,0:T(8,128)}, u32[]{:S(2)}) copy-start(s32[1,16,16]{2,1,0:T(8,128)} %param.14) | copy-start | bytes 3076
  1.4 1.6 copy-start.1
  3.6 3.0 %copy-start.11 = (bf16[1,512,1024]{2,1,0:T(8,128)(2,1)S(1)}, bf16[1,512,1024]{2,1,0:T(8,128)(2,1)}, u32[]{:S(2)}) copy-start(bf16[1,512,1024]{2,1,0:T(8,128)(2,1)} %param.12) | copy-start | bytes 3145732
  4.3 8.4 %copy-start.23 = (bf16[1,512,512]{2,1,0:T(8,128)(2,1)S(1)}, bf16[1,512,512]{2,1,0:T(8,128)(2,1)}, u32[]{:S(2)}) copy-start(bf16[1,512,512]{2,1,0:T(8,128)(2,1)} %param.11) | copy-start | bytes 1572868
  4.3 2.7 collective-permute-start
  4.4 6.4 %collective-permute-start.1 = (bf16[512,128]{1,0:T(8,128)(2,1)S(1)}, bf16[512,128]{1,0:T(8,128)(2,1)S(1)}, u32[]{:S(2)}, u32[]{:S(2)}) collective-permute-start(bf16[512,128]{1,0:T(8,128)(2,1)S(1)} %get-tuple-element.46), channel_id=1, source_target_pairs={{0,2},{1,3},{2,0},{3,1},{4,6},{5,7},{6,4},{7,5},{8,10},{9,11},{10,... | collective-permute-start | bytes 393224 | tf_op jit(solution)/shard_map/ppermute | solution.py:382
  6.0 6.7 %collective-permute-start.2 = (bf16[512,128]{1,0:T(8,128)(2,1)S(1)}, bf16[512,128]{1,0:T(8,128)(2,1)S(1)}, u32[]{:S(2)}, u32[]{:S(2)}) collective-permute-start(bf16[512,128]{1,0:T(8,128)(2,1)S(1)} %get-tuple-element.47), channel_id=1, source_target_pairs={{0,3},{1,2},{2,1},{3,0},{4,7},{5,6},{6,5},{7,4},{8,11},{9,10},{10,... | collective-permute-start | bytes 393224 | tf_op jit(solution)/shard_map/ppermute | solution.py:382
  12.6 13.5 %copy-start.2 = (bf16[16,512,128]{2,1,0:T(8,128)(2,1)S(1)}, bf16[16,512,128]{2,1,0:T(8,128)(2,1)}, u32[]{:S(2)}) copy-start(bf16[16,512,128]{2,1,0:T(8,128)(2,1)} %refs_3_.5) | copy-start | bytes 6291460
  12.6 13.5 %copy-start.21 = (s32[16,1,1]{0,2,1:T(1,128)S(1)}, s32[16,1,1]{0,2,1:T(1,128)}, u32[]{:S(2)}) copy-start(s32[16,1,1]{0,2,1:T(1,128)} %param.10) | copy-start | bytes 196
  13.9 1.0 copy-start.12
  14.9 1.0 copy-start.15
  16.7 44.7 %all-to-all-start.1 = ((bf16[16,64,512]{2,1,0:T(8,128)(2,1)}), bf16[16,64,512]{2,1,0:T(8,128)(2,1)S(1)}, u32[]{:S(2)}, u32[]{:S(2)}) async-start(bf16[16,64,512]{2,1,0:T(8,128)(2,1)} %copy-done.15), calls=%async_computation.1 | async-start | bytes 2097152 | tf_op jit(solution)/shard_map/all_to_all | solution.py:399
  26.1 30.8 %copy-start.13 = (bf16[1024,512]{1,0:T(8,128)(2,1)S(1)}, bf16[1024,512]{1,0:T(8,128)(2,1)}, u32[]{:S(2)}) copy-start(bf16[1024,512]{1,0:T(8,128)(2,1)} %copy-done.12) | copy-start | bytes 3145732
  26.1 30.8 %copy-start.24 = (bf16[1,512,512]{2,1,0:T(8,128)(2,1)S(1)}, bf16[1,512,512]{2,1,0:T(8,128)(2,1)}, u32[]{:S(2)}) copy-start(bf16[1,512,512]{2,1,0:T(8,128)(2,1)} %param.11) | copy-start | bytes 1572868
  26.9 9.7 %collective-permute-start.3 = (bf16[512,128]{1,0:T(8,128)(2,1)S(1)}, bf16[512,128]{1,0:T(8,128)(2,1)S(1)}, u32[]{:S(2)}, u32[]{:S(2)}) collective-permute-start(bf16[512,128]{1,0:T(8,128)(2,1)S(1)} %get-tuple-element.49), channel_id=1, source_target_pairs={{0,4},{1,5},{2,6},{3,7},{4,0},{5,1},{6,2},{7,3},{8,12},{9,13},{10,... | collective-permute-start | bytes 393224 | tf_op jit(solution)/shard_map/ppermute | solution.py:382
  30.0 8.9 %collective-permute-start.4 = (bf16[512,128]{1,0:T(8,128)(2,1)S(1)}, bf16[512,128]{1,0:T(8,128)(2,1)S(1)}, u32[]{:S(2)}, u32[]{:S(2)}) collective-permute-start(bf16[512,128]{1,0:T(8,128)(2,1)S(1)} %get-tuple-element.50), channel_id=1, source_target_pairs={{0,5},{1,4},{2,7},{3,6},{4,1},{5,0},{6,3},{7,2},{8,13},{9,12},{10,... | collective-permute-start | bytes 393224 | tf_op jit(solution)/shard_map/ppermute | solution.py:382
  30.0 10.3 %collective-permute-start.5 = (bf16[512,128]{1,0:T(8,128)(2,1)S(1)}, bf16[512,128]{1,0:T(8,128)(2,1)S(1)}, u32[]{:S(2)}, u32[]{:S(2)}) collective-permute-start(bf16[512,128]{1,0:T(8,128)(2,1)S(1)} %get-tuple-element.51), channel_id=1, source_target_pairs={{0,8},{1,9},{2,10},{3,11},{4,12},{5,13},{6,14},{7,15},{8,0},{9,1},... | collective-permute-start | bytes 393224 | tf_op jit(solution)/shard_map/ppermute | solution.py:382
  30.6 26.3 %collective-permute-start.6 = (bf16[512,128]{1,0:T(8,128)(2,1)S(1)}, bf16[512,128]{1,0:T(8,128)(2,1)S(1)}, u32[]{:S(2)}, u32[]{:S(2)}) collective-permute-start(bf16[512,128]{1,0:T(8,128)(2,1)S(1)} %get-tuple-element.52), channel_id=1, source_target_pairs={{0,9},{1,8},{2,11},{3,10},{4,13},{5,12},{6,15},{7,14},{8,1},{9,0},... | collective-permute-start | bytes 393224 | tf_op jit(solution)/shard_map/ppermute | solution.py:382
  33.4 23.5 %collective-permute-start.7 = (bf16[512,128]{1,0:T(8,128)(2,1)S(1)}, bf16[512,128]{1,0:T(8,128)(2,1)S(1)}, u32[]{:S(2)}, u32[]{:S(2)}) collective-permute-start(bf16[512,128]{1,0:T(8,128)(2,1)S(1)} %get-tuple-element.53), channel_id=1, source_target_pairs={{0,12},{1,13},{2,14},{3,15},{4,8},{5,9},{6,10},{7,11},{8,4},{9,5},... | collective-permute-start | bytes 393224 | tf_op jit(solution)/shard_map/ppermute | solution.py:382
  36.5 20.4 %collective-permute-start.8 = (bf16[512,128]{1,0:T(8,128)(2,1)S(1)}, bf16[512,128]{1,0:T(8,128)(2,1)S(1)}, u32[]{:S(2)}, u32[]{:S(2)}) collective-permute-start(bf16[512,128]{1,0:T(8,128)(2,1)S(1)} %get-tuple-element.54), channel_id=1, source_target_pairs={{0,13},{1,12},{2,15},{3,14},{4,9},{5,8},{6,11},{7,10},{8,5},{9,4},... | collective-permute-start | bytes 393224 | tf_op jit(solution)/shard_map/ppermute | solution.py:382
  38.9 18.0 %collective-permute-start.9 = (bf16[512,128]{1,0:T(8,128)(2,1)S(1)}, bf16[512,128]{1,0:T(8,128)(2,1)S(1)}, u32[]{:S(2)}, u32[]{:S(2)}) collective-permute-start(bf16[512,128]{1,0:T(8,128)(2,1)S(1)} %get-tuple-element.55), channel_id=1, source_target_pairs={{0,10},{1,11},{2,8},{3,9},{4,14},{5,15},{6,12},{7,13},{8,2},{9,3},... | collective-permute-start | bytes 393224 | tf_op jit(solution)/shard_map/ppermute | solution.py:382
  40.3 16.6 %collective-permute-start.10 = (bf16[512,128]{1,0:T(8,128)(2,1)S(1)}, bf16[512,128]{1,0:T(8,128)(2,1)S(1)}, u32[]{:S(2)}, u32[]{:S(2)}) collective-permute-start(bf16[512,128]{1,0:T(8,128)(2,1)S(1)} %get-tuple-element.56), channel_id=1, source_target_pairs={{0,11},{1,10},{2,9},{3,8},{4,15},{5,14},{6,13},{7,12},{8,3},{9,2},... | collective-permute-start | bytes 393224 | tf_op jit(solution)/shard_map/ppermute | solution.py:382
  59.1 1.3 copy-start.8
  60.5 1.0 copy-start.9
  61.4 59.2 %all-to-all-start.2 = ((bf16[16,64,1024]{2,1,0:T(8,128)(2,1)}), bf16[16,64,1024]{2,1,0:T(8,128)(2,1)}, u32[]{:S(2)}, u32[]{:S(2)}) async-start(bf16[16,64,1024]{2,1,0:T(8,128)(2,1)} %copy-done.8), calls=%async_computation.2 | async-start | bytes 4194304 | tf_op jit(solution)/shard_map/all_to_all | solution.py:399
  71.9 19.8 %copy-start.14 = (bf16[1024,512]{1,0:T(8,128)(2,1)S(1)}, bf16[1024,512]{1,0:T(8,128)(2,1)}, u32[]{:S(2)}) copy-start(bf16[1024,512]{1,0:T(8,128)(2,1)} %copy-done.12) | copy-start | bytes 3145732
  71.9 19.8 %copy-start.25 = (bf16[1,512,512]{2,1,0:T(8,128)(2,1)S(1)}, bf16[1,512,512]{2,1,0:T(8,128)(2,1)}, u32[]{:S(2)}) copy-start(bf16[1,512,512]{2,1,0:T(8,128)(2,1)} %param.11) | copy-start | bytes 1572868
  72.6 11.2 %collective-permute-start.11 = (bf16[512,128]{1,0:T(8,128)(2,1)S(1)}, bf16[512,128]{1,0:T(8,128)(2,1)S(1)}, u32[]{:S(2)}, u32[]{:S(2)}) collective-permute-start(bf16[512,128]{1,0:T(8,128)(2,1)S(1)} %get-tuple-element.58), channel_id=1, source_target_pairs={{0,14},{1,15},{2,12},{3,13},{4,10},{5,11},{6,8},{7,9},{8,6},{9,7},... | collective-permute-start | bytes 393224 | tf_op jit(solution)/shard_map/ppermute | solution.py:382
  76.8 11.9 %collective-permute-start.12 = (bf16[512,128]{1,0:T(8,128)(2,1)S(1)}, bf16[512,128]{1,0:T(8,128)(2,1)S(1)}, u32[]{:S(2)}, u32[]{:S(2)}) collective-permute-start(bf16[512,128]{1,0:T(8,128)(2,1)S(1)} %get-tuple-element.59), channel_id=1, source_target_pairs={{0,15},{1,14},{2,13},{3,12},{4,11},{5,10},{6,9},{7,8},{8,7},{9,6},... | collective-permute-start | bytes 393224 | tf_op jit(solution)/shard_map/ppermute | solution.py:382
  76.8 11.9 %collective-permute-start.13 = (bf16[512,128]{1,0:T(8,128)(2,1)S(1)}, bf16[512,128]{1,0:T(8,128)(2,1)S(1)}, u32[]{:S(2)}, u32[]{:S(2)}) collective-permute-start(bf16[512,128]{1,0:T(8,128)(2,1)S(1)} %get-tuple-element.60), channel_id=1, source_target_pairs={{0,6},{1,7},{2,4},{3,5},{4,2},{5,3},{6,0},{7,1},{8,14},{9,15},{10,... | collective-permute-start | bytes 393224 | tf_op jit(solution)/shard_map/ppermute | solution.py:382
  81.0 45.1 %copy-start.36 = (s32[16]{0:T(128)S(1)}, s32[16]{0:T(128)}, u32[]{:S(2)}) copy-start(s32[16]{0:T(128)} %constant.52.clone) | copy-start | bytes 196
  81.0 10.8 %collective-permute-start.14 = (bf16[512,128]{1,0:T(8,128)(2,1)S(1)}, bf16[512,128]{1,0:T(8,128)(2,1)S(1)}, u32[]{:S(2)}, u32[]{:S(2)}) collective-permute-start(bf16[512,128]{1,0:T(8,128)(2,1)S(1)} %get-tuple-element.61), channel_id=1, source_target_pairs={{0,7},{1,6},{2,5},{3,4},{4,3},{5,2},{6,1},{7,0},{8,15},{9,14},{10,... | collective-permute-start | bytes 393224 | tf_op jit(solution)/shard_map/ppermute | solution.py:382
  120.6 67.1 %all-to-all-start = ((bf16[16,64,512]{2,1,0:T(8,128)(2,1)}), bf16[16,64,512]{2,1,0:T(8,128)(2,1)}, u32[]{:S(2)}, u32[]{:S(2)}) async-start(bf16[16,64,512]{2,1,0:T(8,128)(2,1)} %get-tuple-element.66), calls=%async_computation | async-start | bytes 2097152 | tf_op jit(solution)/shard_map/all_to_all | solution.py:399
  128.5 1.2 copy-start.22
  141.3 1.3 copy-start.3
  142.6 13.2 %collective-permute-start.19 = (s16[528,128]{1,0:T(8,128)(2,1)S(1)}, s16[528,128]{1,0:T(8,128)(2,1)S(1)}, u32[]{:S(2)}, u32[]{:S(2)}) collective-permute-start(s16[528,128]{1,0:T(8,128)(2,1)S(1)} %get-tuple-element.74), channel_id=1, source_target_pairs={{0,1},{1,0},{2,3},{3,2},{4,5},{5,4},{6,7},{7,6},{8,9},{9,8},{10,11... | collective-permute-start | bytes 405512 | tf_op jit(solution)/shard_map/ppermute | solution.py:382
  142.6 14.8 %collective-permute-start.20 = (s16[528,128]{1,0:T(8,128)(2,1)S(1)}, s16[528,128]{1,0:T(8,128)(2,1)S(1)}, u32[]{:S(2)}, u32[]{:S(2)}) collective-permute-start(s16[528,128]{1,0:T(8,128)(2,1)S(1)} %get-tuple-element.75), channel_id=1, source_target_pairs={{0,2},{1,3},{2,0},{3,1},{4,6},{5,7},{6,4},{7,5},{8,10},{9,11},{10,... | collective-permute-start | bytes 405512 | tf_op jit(solution)/shard_map/ppermute | solution.py:382
  147.0 12.3 %collective-permute-start.21 = (s16[528,128]{1,0:T(8,128)(2,1)S(1)}, s16[528,128]{1,0:T(8,128)(2,1)S(1)}, u32[]{:S(2)}, u32[]{:S(2)}) collective-permute-start(s16[528,128]{1,0:T(8,128)(2,1)S(1)} %get-tuple-element.76), channel_id=1, source_target_pairs={{0,3},{1,2},{2,1},{3,0},{4,7},{5,6},{6,5},{7,4},{8,11},{9,10},{10,... | collective-permute-start | bytes 405512 | tf_op jit(solution)/shard_map/ppermute | solution.py:382
  152.0 12.1 %collective-permute-start.22 = (s16[528,128]{1,0:T(8,128)(2,1)S(1)}, s16[528,128]{1,0:T(8,128)(2,1)S(1)}, u32[]{:S(2)}, u32[]{:S(2)}) collective-permute-start(s16[528,128]{1,0:T(8,128)(2,1)S(1)} %get-tuple-element.78), channel_id=1, source_target_pairs={{0,4},{1,5},{2,6},{3,7},{4,0},{5,1},{6,2},{7,3},{8,12},{9,13},{10,... | collective-permute-start | bytes 405512 | tf_op jit(solution)/shard_map/ppermute | solution.py:382
  155.8 10.8 %collective-permute-start.23 = (s16[528,128]{1,0:T(8,128)(2,1)S(1)}, s16[528,128]{1,0:T(8,128)(2,1)S(1)}, u32[]{:S(2)}, u32[]{:S(2)}) collective-permute-start(s16[528,128]{1,0:T(8,128)(2,1)S(1)} %get-tuple-element.79), channel_id=1, source_target_pairs={{0,5},{1,4},{2,7},{3,6},{4,1},{5,0},{6,3},{7,2},{8,13},{9,12},{10,... | collective-permute-start | bytes 405512 | tf_op jit(solution)/shard_map/ppermute | solution.py:382
  155.8 13.2 %collective-permute-start.24 = (s16[528,128]{1,0:T(8,128)(2,1)S(1)}, s16[528,128]{1,0:T(8,128)(2,1)S(1)}, u32[]{:S(2)}, u32[]{:S(2)}) collective-permute-start(s16[528,128]{1,0:T(8,128)(2,1)S(1)} %get-tuple-element.80), channel_id=1, source_target_pairs={{0,8},{1,9},{2,10},{3,11},{4,12},{5,13},{6,14},{7,15},{8,0},{9,1},... | collective-permute-start | bytes 405512 | tf_op jit(solution)/shard_map/ppermute | solution.py:382
  157.4 14.4 %copy-start.26 = (s16[528,128]{1,0:T(8,128)(2,1)}, s16[528,128]{1,0:T(8,128)(2,1)S(1)}, u32[]{:S(2)}) copy-start(s16[528,128]{1,0:T(8,128)(2,1)S(1)} %collective-permute-done.20.refs_2_) | copy-start | bytes 405508
  157.4 32.6 %collective-permute-start.25 = (s16[528,128]{1,0:T(8,128)(2,1)}, s16[528,128]{1,0:T(8,128)(2,1)}, u32[]{:S(2)}, u32[]{:S(2)}) collective-permute-start(s16[528,128]{1,0:T(8,128)(2,1)} %get-tuple-element.81), channel_id=1, source_target_pairs={{0,9},{1,8},{2,11},{3,10},{4,13},{5,12},{6,15},{7,14},{8,1},{9,0},... | collective-permute-start | bytes 405512 | tf_op jit(solution)/shard_map/ppermute | solution.py:382
  160.0 34.5 %collective-permute-start.26 = (s16[528,128]{1,0:T(8,128)(2,1)}, s16[528,128]{1,0:T(8,128)(2,1)}, u32[]{:S(2)}, u32[]{:S(2)}) collective-permute-start(s16[528,128]{1,0:T(8,128)(2,1)} %get-tuple-element.82), channel_id=1, source_target_pairs={{0,12},{1,13},{2,14},{3,15},{4,8},{5,9},{6,10},{7,11},{8,4},{9,5},... | collective-permute-start | bytes 405512 | tf_op jit(solution)/shard_map/ppermute | solution.py:382
  164.8 31.0 %collective-permute-start.27 = (s16[528,128]{1,0:T(8,128)(2,1)}, s16[528,128]{1,0:T(8,128)(2,1)}, u32[]{:S(2)}, u32[]{:S(2)}) collective-permute-start(s16[528,128]{1,0:T(8,128)(2,1)} %get-tuple-element.83), channel_id=1, source_target_pairs={{0,13},{1,12},{2,15},{3,14},{4,9},{5,8},{6,11},{7,10},{8,5},{9,4},... | collective-permute-start | bytes 405512 | tf_op jit(solution)/shard_map/ppermute | solution.py:382
  167.2 31.9 %collective-permute-start.28 = (s16[528,128]{1,0:T(8,128)(2,1)}, s16[528,128]{1,0:T(8,128)(2,1)}, u32[]{:S(2)}, u32[]{:S(2)}) collective-permute-start(s16[528,128]{1,0:T(8,128)(2,1)} %get-tuple-element.84), channel_id=1, source_target_pairs={{0,10},{1,11},{2,8},{3,9},{4,14},{5,15},{6,12},{7,13},{8,2},{9,3},... | collective-permute-start | bytes 405512 | tf_op jit(solution)/shard_map/ppermute | solution.py:382
  169.6 29.8 %collective-permute-start.29 = (s16[528,128]{1,0:T(8,128)(2,1)}, s16[528,128]{1,0:T(8,128)(2,1)}, u32[]{:S(2)}, u32[]{:S(2)}) collective-permute-start(s16[528,128]{1,0:T(8,128)(2,1)} %get-tuple-element.85), channel_id=1, source_target_pairs={{0,11},{1,10},{2,9},{3,8},{4,15},{5,14},{6,13},{7,12},{8,3},{9,2},... | collective-permute-start | bytes 405512 | tf_op jit(solution)/shard_map/ppermute | solution.py:382
  174.5 13.2 %copy-start.4 = (bf16[16,512,128]{2,1,0:T(8,128)(2,1)S(1)}, bf16[16,512,128]{2,1,0:T(8,128)(2,1)}, u32[]{:S(2)}) copy-start(bf16[16,512,128]{2,1,0:T(8,128)(2,1)} %copy-done.3) | copy-start | bytes 6291460
  185.7 2.0 copy-start.5
  187.7 11.6 %copy-start.27 = (s16[528,128]{1,0:T(8,128)(2,1)S(1)}, s16[528,128]{1,0:T(8,128)(2,1)}, u32[]{:S(2)}) copy-start(s16[528,128]{1,0:T(8,128)(2,1)} %copy-done.26) | copy-start | bytes 405508
  187.7 11.6 %copy-start.29 = (s16[528,128]{1,0:T(8,128)(2,1)S(1)}, s16[528,128]{1,0:T(8,128)(2,1)}, u32[]{:S(2)}) copy-start(s16[528,128]{1,0:T(8,128)(2,1)} %copy-done.28) | copy-start | bytes 405508
  187.7 11.6 %copy-start.31 = (s16[528,128]{1,0:T(8,128)(2,1)S(1)}, s16[528,128]{1,0:T(8,128)(2,1)}, u32[]{:S(2)}) copy-start(s16[528,128]{1,0:T(8,128)(2,1)} %copy-done.30) | copy-start | bytes 405508
  187.7 11.6 %copy-start.33 = (s16[528,128]{1,0:T(8,128)(2,1)S(1)}, s16[528,128]{1,0:T(8,128)(2,1)}, u32[]{:S(2)}) copy-start(s16[528,128]{1,0:T(8,128)(2,1)} %copy-done.32) | copy-start | bytes 405508
  187.7 11.6 %copy-start.35 = (s16[528,128]{1,0:T(8,128)(2,1)S(1)}, s16[528,128]{1,0:T(8,128)(2,1)}, u32[]{:S(2)}) copy-start(s16[528,128]{1,0:T(8,128)(2,1)} %copy-done.34) | copy-start | bytes 405508
  190.0 23.1 %collective-permute-start.15 = (s16[528,128]{1,0:T(8,128)(2,1)S(1)}, s16[528,128]{1,0:T(8,128)(2,1)S(1)}, u32[]{:S(2)}, u32[]{:S(2)}) collective-permute-start(s16[528,128]{1,0:T(8,128)(2,1)S(1)} %get-tuple-element.68), channel_id=1, source_target_pairs={{0,14},{1,15},{2,12},{3,13},{4,10},{5,11},{6,8},{7,9},{8,6},{9,7},... | collective-permute-start | bytes 405512 | tf_op jit(solution)/shard_map/ppermute | solution.py:382
  194.5 18.6 %collective-permute-start.16 = (s16[528,128]{1,0:T(8,128)(2,1)S(1)}, s16[528,128]{1,0:T(8,128)(2,1)S(1)}, u32[]{:S(2)}, u32[]{:S(2)}) collective-permute-start(s16[528,128]{1,0:T(8,128)(2,1)S(1)} %get-tuple-element.69), channel_id=1, source_target_pairs={{0,15},{1,14},{2,13},{3,12},{4,11},{5,10},{6,9},{7,8},{8,7},{9,6},... | collective-permute-start | bytes 405512 | tf_op jit(solution)/shard_map/ppermute | solution.py:382
  195.7 17.4 %collective-permute-start.17 = (s16[528,128]{1,0:T(8,128)(2,1)S(1)}, s16[528,128]{1,0:T(8,128)(2,1)S(1)}, u32[]{:S(2)}, u32[]{:S(2)}) collective-permute-start(s16[528,128]{1,0:T(8,128)(2,1)S(1)} %get-tuple-element.70), channel_id=1, source_target_pairs={{0,6},{1,7},{2,4},{3,5},{4,2},{5,3},{6,0},{7,1},{8,14},{9,15},{10,... | collective-permute-start | bytes 405512 | tf_op jit(solution)/shard_map/ppermute | solution.py:382
  199.1 14.0 %collective-permute-start.18 = (s16[528,128]{1,0:T(8,128)(2,1)S(1)}, s16[528,128]{1,0:T(8,128)(2,1)S(1)}, u32[]{:S(2)}, u32[]{:S(2)}) collective-permute-start(s16[528,128]{1,0:T(8,128)(2,1)S(1)} %get-tuple-element.71), channel_id=1, source_target_pairs={{0,7},{1,6},{2,5},{3,4},{4,3},{5,2},{6,1},{7,0},{8,15},{9,14},{10,... | collective-permute-start | bytes 405512 | tf_op jit(solution)/shard_map/ppermute | solution.py:382
  211.1 2.0 copy-start.7
  225.8 1.3 copy-start.6
  227.1 8.2 %copy-start.10 = (bf16[8,512,128]{2,1,0:T(8,128)(2,1)S(1)}, bf16[8,512,128]{2,1,0:T(8,128)(2,1)}, u32[]{:S(2)}) copy-start(bf16[8,512,128]{2,1,0:T(8,128)(2,1)} %copy-done.9) | copy-start | bytes 3145732
  227.1 57.0 %all-to-all-start.3 = ((bf16[16,128,512]{2,1,0:T(8,128)(2,1)}), bf16[16,128,512]{2,1,0:T(8,128)(2,1)S(1)}, u32[]{:S(2)}, u32[]{:S(2)}) async-start(bf16[16,128,512]{2,1,0:T(8,128)(2,1)} %copy-done.6), calls=%async_computation.3 | async-start | bytes 4194304 | tf_op jit(solution)/shard_map/all_to_all | solution.py:419
  235.3 1.0 copy-start.17
  236.4 1.0 copy-start.19
  (7 other events, 4.9 us)

commit v2 on v0

v2 whole, which is shorter than its diff:
```python
import functools

import jax
import jax.numpy as jnp
from jax import lax
from jax.experimental import pallas as pl
from jax.experimental.pallas import tpu as pltpu
from jax.sharding import PartitionSpec as P

RK = 64
CW = 128
WIN = 144
HALF = CW // 2
EXP_ROWS = 16
RING = 8
TILE_BATCH = 4
CODE_BITS = 14
MIB = 1024 * 1024


def vmem():
    return pl.BlockSpec(memory_space=pltpu.VMEM)


def smem():
    return pl.BlockSpec(memory_space=pltpu.SMEM)


def token_shape():
    return jax.ShapeDtypeStruct((8, CW), jnp.float32)


def token_spec():
    return pl.BlockSpec((8, CW), lambda *grid: (0, 0))


def set_token(token_ref):
    token_ref[...] = jnp.zeros_like(token_ref)


def untouched(count):
    return [pl.BlockSpec(memory_space=pltpu.HBM)] * count


def params(mib):
    return pltpu.CompilerParams(vmem_limit_bytes=mib * MIB)


def cost(flops, bytes_accessed):
    return pl.CostEstimate(flops=int(flops), bytes_accessed=int(bytes_accessed), transcendentals=0)


def groups_of(count):
    if count == 8:
        return [[4, 5, 6, 2], [7, 3, 1, 0]]
    return [list(range(count // 2, count)), list(range(count // 2))]


def halves(first, second):
    left = jnp.concatenate([first[:, :HALF], second[:, :HALF]], axis=1)
    right = jnp.concatenate([first[:, HALF:], second[:, HALF:]], axis=1)
    return left, right


def swapped(flag, first, second):
    return jnp.where(flag, second, first), jnp.where(flag, first, second)


def mask_body(pattern_ref, rhs_ref, out_ref, token_ref):
    for step in range(rhs_ref.shape[0]):
        front = pl.program_id(0) * rhs_ref.shape[0] + step
        keep = pattern_ref[front].astype(jnp.float32)
        out_ref[step] = (rhs_ref[step].astype(jnp.float32) * keep).astype(jnp.bfloat16)
    set_token(token_ref)


def mask_all(rhs, pattern):
    count, rows, cols = rhs.shape
    spec = pl.BlockSpec((4, rows, cols), lambda i: (i, 0, 0))
    return pl.pallas_call(
        mask_body,
        out_shape=[pltpu.HBM(rhs.shape, jnp.bfloat16), token_shape()],
        grid=(count // 4,),
        in_specs=[smem(), spec],
        out_specs=[spec, token_spec()],
        compiler_params=params(60),
        cost_estimate=cost(count * rows * cols, 4 * count * rows * cols),
        name="mask_all",
    )(pattern, rhs)


def right_body(ring, odd_ref, right_ref, keep_ref, out_ref):
    kept = (right_ref[...].astype(jnp.float32) * keep_ref[...]).T
    span = ring * RK
    pieces = []
    for begin in range(0, kept.shape[0], span):
        pieces += [kept[begin + RK : begin + span], kept[begin : begin + RK]]
    turned = jnp.concatenate(pieces, axis=0)
    out_ref[...] = jnp.where(odd_ref[0] > 0, turned, kept).astype(jnp.bfloat16)


def right_transposed(odd, right, keep, ring):
    rows, width = right.shape
    return pl.pallas_call(
        functools.partial(right_body, ring),
        out_shape=pltpu.HBM((width, rows), jnp.bfloat16),
        in_specs=[smem()] + [vmem()] * 2,
        out_specs=vmem(),
        compiler_params=params(16),
        cost_estimate=cost(rows * width, 4 * rows * width),
        name="right_transposed",
    )(odd, right, keep)


def solve_body(count, ring, pairs_ref, odd_ref, inverse_ref, right_ref, *refs):
    sources = refs[:count]
    solved_ref, projected_ref, token_ref = refs[-3:]
    set_token(token_ref)
    depth = projected_ref.shape[0]
    odd = odd_ref[0]
    for step in range(count):
        block = jnp.concatenate(halves(sources[step][0], sources[step][1]), axis=1)
        solved = jnp.dot(inverse_ref[...], block, preferred_element_type=jnp.float32)
        solved = solved.astype(jnp.bfloat16)
        solved_ref[step, 0], solved_ref[step, 1] = halves(solved[:, :CW], solved[:, CW:])
        projected = jnp.dot(right_ref[...], solved, preferred_element_type=jnp.float32)
        projected = projected.astype(jnp.bfloat16)
        span = slice(step * CW, (step + 1) * CW)
        for begin in range(0, depth, ring):
            for tile in range(0, ring, 2):
                row = (begin + tile) * RK
                pair = projected[row : row + 2 * RK]
                projected_ref[begin + tile + 1, :, span] = pair[:, CW:]
                projected_ref[begin + lax.rem(tile + 2 * odd, ring), :, span] = pair[:, :CW]


def solve_group(pairs, odd, inverse, right, blocks, ring, earlier):
    count = pairs.shape[0]
    rows = inverse.shape[0]
    width = right.shape[0]
    depth = width // RK

    def whole(shape):
        return pl.BlockSpec(shape, lambda i, pairs_ref, odd_ref: (0,) * len(shape))

    def pick(step):
        return lambda i, pairs_ref, odd_ref: (pairs_ref[step], 0, 0)

    return pl.pallas_call(
        functools.partial(solve_body, count, ring),
        out_shape=[
            pltpu.HBM((count, 2, rows, CW), jnp.bfloat16),
            pltpu.HBM((depth, 2 * RK, count * CW), jnp.bfloat16),
            token_shape(),
        ],
        grid_spec=pltpu.PrefetchScalarGridSpec(
            num_scalar_prefetch=2,
            grid=(1,),
            in_specs=[whole((rows, rows)), whole((width, rows))]
            + [pl.BlockSpec((2, rows, CW), pick(step)) for step in range(count)]
            + untouched(len(earlier)),
            out_specs=[
                whole((count, 2, rows, CW)),
                whole((depth, 2 * RK, count * CW)),
                token_spec(),
            ],
        ),
        compiler_params=params(20),
        cost_estimate=cost(4 * rows * (rows + width) * count * CW, 4 * count * CW * (2 * rows + width)),
        name="solve_group",
    )(pairs, odd, inverse, right, *([blocks] * count), *earlier)


def place_body(starts, pairs_ref, *refs):
    out_ref = refs[-1]
    step = pl.program_id(0)
    for begin, end, ref in zip(starts[:-1], starts[1:], refs[:-1]):

        @pl.when((step >= begin) & (step < end))
        def _(ref=ref):
            out_ref[0, :, :CW] = ref[0, 0]
            out_ref[0, :, CW:] = ref[0, 1]


def place_blocks(pairs, parts):
    starts = [0]
    for part in parts:
        starts.append(starts[-1] + part.shape[0])
    rows = parts[0].shape[2]

    def pick(begin, end):
        return lambda i, pairs_ref: (jnp.clip(i - begin, 0, end - begin - 1), 0, 0, 0)

    return pl.pallas_call(
        functools.partial(place_body, starts),
        out_shape=jax.ShapeDtypeStruct((1, rows, starts[-1] * 2 * CW), jnp.bfloat16),
        grid_spec=pltpu.PrefetchScalarGridSpec(
            num_scalar_prefetch=1,
            grid=(starts[-1],),
            in_specs=[
                pl.BlockSpec((1, 2, rows, CW), pick(begin, end))
                for begin, end in zip(starts[:-1], starts[1:])
            ],
            out_specs=pl.BlockSpec((1, rows, 2 * CW), lambda i, pairs_ref: (0, 0, pairs_ref[i])),
        ),
        compiler_params=params(6),
        cost_estimate=cost(0, 8 * rows * starts[-1] * CW),
        name="place_blocks",
    )(pairs, *parts)


def pack_body(high_ref, contrib_ref, after_ref, keep_ref, send_ref):
    high = high_ref[0] > 0
    for step in range(keep_ref.shape[1] // CW):
        even = contrib_ref[:, 2 * step * CW : (2 * step + 1) * CW]
        other = contrib_ref[:, (2 * step + 1) * CW : (2 * step + 2) * CW]
        span = slice(step * CW, (step + 1) * CW)
        keep_ref[:, span], send_ref[:, span] = swapped(high, *halves(even, other))


def pack_contrib(high, contrib, earlier):
    rows, cols = contrib.shape
    spec = pl.BlockSpec((rows, cols // 4), lambda i: (0, i))
    return pl.pallas_call(
        pack_body,
        out_shape=[pltpu.HBM((rows, cols // 2), jnp.bfloat16)] * 2,
        grid=(2,),
        in_specs=[smem(), pl.BlockSpec((rows, cols // 2), lambda i: (0, i))] + untouched(1),
        out_specs=[spec] * 2,
        compiler_params=params(60),
        cost_estimate=cost(rows * cols, 4 * rows * cols),
        name="pack_contrib",
    )(high, contrib, earlier)


def ordering(keys):
    rows = keys.shape[1]
    column = jnp.broadcast_to(keys, (CW, rows)).T
    smaller = (jnp.concatenate([column] * (rows // CW), axis=1) < keys).astype(jnp.float32)
    rank = jnp.sum(smaller, axis=0, keepdims=True)
    place = lax.broadcasted_iota(jnp.int32, (rows, rows), 0).astype(jnp.float32)
    return jnp.where(place == rank, 1.0, 0.0).astype(jnp.bfloat16)


def sort_body(
    high_ref, keys_ref, own_ref, other_ref, kept_ref, got_ref, left_out, contrib_out, token_ref, one_hot
):
    rows = own_ref.shape[0]

    @pl.when(pl.program_id(0) == 0)
    def _():
        one_hot[...] = ordering(keys_ref[...])
        set_token(token_ref)

    def sort(value, begin):
        order = one_hot[:, begin : begin + rows]
        return jnp.dot(order, value, preferred_element_type=jnp.float32)

    own, other = sort(own_ref[...], 0), sort(other_ref[...], rows)
    low, top = swapped(high_ref[0] > 0, own, other)
    for step in range(low.shape[1] // CW):
        span = slice(step * CW, (step + 1) * CW)
        pair = halves(low[:, span], top[:, span])
        left_out[:, 2 * step * CW : (2 * step + 1) * CW] = pair[0].astype(jnp.bfloat16)
        left_out[:, (2 * step + 1) * CW : (2 * step + 2) * CW] = pair[1].astype(jnp.bfloat16)

    contrib = sort(kept_ref[...], 0) + sort(got_ref[...], rows)
    for step in range(contrib_out.shape[0]):
        contrib_out[step] = contrib[:, step * CW : (step + 1) * CW].astype(jnp.bfloat16)


def sort_rows(high, keys, own, other, kept, got):
    rows, width = own.shape
    cols = kept.shape[1]
    joint = 2 * rows
    steps = min(4, cols // CW)
    spread = min(steps, width // CW)
    return pl.pallas_call(
        sort_body,
        out_shape=[
            pltpu.HBM((joint, 2 * width), jnp.bfloat16),
            pltpu.HBM((cols // CW, joint, CW), jnp.bfloat16),
            token_shape(),
        ],
        grid=(steps,),
        in_specs=[
            smem(),
            pl.BlockSpec((1, joint), lambda i: (0, 0)),
            pl.BlockSpec((rows, width // spread), lambda i: (0, i % spread)),
            pl.BlockSpec((rows, width // spread), lambda i: (0, i % spread)),
            pl.BlockSpec((rows, cols // steps), lambda i: (0, i)),
            pl.BlockSpec((rows, cols // steps), lambda i: (0, i)),
        ],
        out_specs=[
            pl.BlockSpec((joint, 2 * width // spread), lambda i: (0, i % spread)),
            pl.BlockSpec((cols // CW // steps, joint, CW), lambda i: (i, 0, 0)),
            token_spec(),
        ],
        scratch_shapes=[pltpu.VMEM((joint, joint), jnp.bfloat16)],
        compiler_params=params(28),
        cost_estimate=cost(2 * joint * rows * (2 * width + 2 * cols), 8 * rows * (width + cols)),
        name="sort_rows",
    )(high, keys.reshape(1, joint), own, other, kept, got)


def target_body(keys_ref, after_ref, out_ref, token_ref):
    for step in range(keys_ref.shape[0]):
        keys = keys_ref[step]
        out_ref[step] = jnp.broadcast_to(keys, (CW, keys.shape[1])).T
    set_token(token_ref)


def sorted_targets(maps, earlier):
    count, rows = maps.shape
    batch = 2 if count % 2 == 0 else 1
    return pl.pallas_call(
        target_body,
        out_shape=[pltpu.HBM((count, rows, CW), jnp.float32), token_shape()],
        grid=(count // batch,),
        in_specs=[pl.BlockSpec((batch, 1, rows), lambda i: (i, 0, 0))] + untouched(1),
        out_specs=[pl.BlockSpec((batch, rows, CW), lambda i: (i, 0, 0)), token_spec()],
        compiler_params=params(16),
        cost_estimate=cost(count * rows * CW, 4 * count * rows * CW),
        name="sorted_targets",
    )(maps.reshape(count, 1, rows), earlier)


def coded_rows(value, out_ref):
    rows = value.shape[0]
    top = jnp.max(jnp.abs(value), axis=0, keepdims=True)
    exponent = jnp.floor(jnp.log2(jnp.maximum(top, 2.0**-108))) + 1.0
    code = jnp.floor(value * jnp.exp2(CODE_BITS - exponent) + 0.5).astype(jnp.int32)
    out_ref[:rows, :] = code.astype(jnp.int16)
    out_ref[rows:, :] = jnp.broadcast_to(exponent.astype(jnp.int32), (EXP_ROWS, CW)).astype(jnp.int16)


def update_body(count, odd_ref, pairs_ref, left_ref, projected_ref, contrib_ref, *refs):
    out_refs = refs[-2 * count :]
    joint, width = left_ref.shape
    rows = joint // 2
    odd = odd_ref[0] > 0
    for start in range(0, count, 2):
        span = min(2, count - start)
        part = projected_ref[:, :, start * CW : (start + span) * CW].reshape(width, span * CW)
        product = jnp.dot(left_ref[...], part, preferred_element_type=jnp.float32)
        for step in range(start, start + span):
            reduced = contrib_ref[pairs_ref[step]].astype(jnp.float32)
            reduced = reduced - product[:, (step - start) * CW : (step - start + 1) * CW]
            first, second = swapped(odd, *halves(reduced[:rows], reduced[rows:]))
            coded_rows(first, out_refs[2 * step])
            coded_rows(second, out_refs[2 * step + 1])


def update_group(odd, pairs, left, projected, contrib, earlier):
    joint, width = left.shape
    count = projected.shape[2] // CW
    return pl.pallas_call(
        functools.partial(update_body, count),
        out_shape=[pltpu.HBM((joint // 2 + EXP_ROWS, CW), jnp.int16)] * (2 * count),
        in_specs=[smem()] * 2 + [vmem()] * 3 + untouched(len(earlier)),
        out_specs=[vmem()] * (2 * count),
        compiler_params=params(28),
        cost_estimate=cost(2 * joint * width * count * CW, 2 * count * CW * (width + 2 * joint)),
        name="update_group",
    )(odd, pairs, left, projected, contrib, *earlier)


def scatter_body(count, has_partial, starts_ref, targets_ref, *refs):
    sources = refs[:count]
    partial_ref = refs[count] if has_partial else None
    out_ref, token_ref, values, one_hot = refs[-4:]
    joint = targets_ref.shape[1]
    rows = joint // 2

    @pl.when(pl.program_id(0) == 0)
    def _():
        for step in range(count):
            code = sources[step][:rows, :].astype(jnp.int32).astype(jnp.float32)
            exponent = sources[step][rows:, :].astype(jnp.int32).astype(jnp.float32)[:1]
            value = code * jnp.exp2(exponent - CODE_BITS)
            high = value.astype(jnp.bfloat16).astype(jnp.float32)
            low = value - high
            top, bottom = halves(high, low)
            values[step * joint : step * joint + rows, :] = top.astype(jnp.bfloat16)
            values[step * joint + rows : (step + 1) * joint, :] = bottom.astype(jnp.bfloat16)

    set_token(token_ref)
    lanes = lax.broadcasted_iota(jnp.int32, (WIN, rows), 1)
    batch = out_ref.shape[0]
    for place in range(batch):
        tile = pl.program_id(0) * batch + place
        lane = (lanes + tile * rows).astype(jnp.float32)
        parts = []
        for step in range(count):
            begin = jnp.minimum((starts_ref[step, tile] // 16) * 16, joint - WIN)
            begin = pl.multiple_of(begin, 16)
            target = targets_ref[step, pl.ds(begin, WIN), :]
            target = jnp.concatenate([target] * (rows // CW), axis=1)
            match = jnp.where(target == lane, 1.0, 0.0)
            one_hot[place, step * WIN : (step + 1) * WIN, :] = match.astype(jnp.bfloat16)
            parts.append(values[pl.ds(pl.multiple_of(step * joint + begin, 16), WIN), :])
        window = jnp.concatenate(parts, axis=0)
        total = lax.dot_general(
            window, one_hot[place], (((0,), (0,)), ((), ())), preferred_element_type=jnp.float32
        )
        total = total[:HALF] + total[HALF:]
        if has_partial:
            total = total + partial_ref[place]
        out_ref[place] = total.astype(out_ref.dtype)


def scatter_rows(starts, targets, coded, partial, out_dtype):
    count = len(coded)
    joint = targets.shape[1]
    rows = joint // 2
    tiles = starts.shape[1]
    batch = min(TILE_BATCH, tiles)
    has_partial = partial is not None
    tile_spec = pl.BlockSpec((batch, HALF, rows), lambda t: (t, 0, 0))
    whole = pl.BlockSpec((rows + EXP_ROWS, CW), lambda t: (0, 0))
    extra = [tile_spec] if has_partial else []
    operands = [partial] if has_partial else []
    return pl.pallas_call(
        functools.partial(scatter_body, count, has_partial),
        out_shape=[pltpu.HBM((tiles, HALF, rows), out_dtype), token_shape()],
        grid=(tiles // batch,),
        in_specs=[smem(), pl.BlockSpec(targets.shape, lambda t: (0, 0, 0))] + [whole] * count + extra,
        out_specs=[tile_spec, token_spec()],
        scratch_shapes=[
            pltpu.VMEM((count * joint, CW), jnp.bfloat16),
            pltpu.VMEM((batch, count * WIN, rows), jnp.bfloat16),
        ],
        compiler_params=params(36),
        cost_estimate=cost(2 * CW * count * WIN * rows * tiles, 8 * tiles * HALF * rows),
        name="scatter_rows",
    )(starts, targets, *coded, *operands)


def total_body(parts_ref, out_ref):
    sources, cols, rows = parts_ref.shape
    parts = parts_ref[...].astype(jnp.float32).reshape(sources // 2, 2, cols, rows)
    out_ref[...] = jnp.sum(parts, axis=0).reshape(2 * cols, rows).T


def total_rows(parts):
    sources, cols, rows = parts.shape
    return pl.pallas_call(
        total_body,
        out_shape=jax.ShapeDtypeStruct((rows, 2 * cols), jnp.float32),
        grid=(rows // CW,),
        in_specs=[pl.BlockSpec((sources, cols, CW), lambda i: (0, 0, i))],
        out_specs=pl.BlockSpec((CW, 2 * cols), lambda i: (i, 0)),
        compiler_params=params(6),
        cost_estimate=cost(sources * cols * rows, 2 * sources * cols * rows),
        name="total_rows",
    )(parts)


def per_device(
    rhs_pivot,
    block_pattern,
    diag_inverse,
    right_factor,
    left_factor,
    tile_ranks,
    contrib_rhs,
    parent_map,
):
    owner = lax.axis_index("owner")
    blk = lax.axis_index("blk")
    partners = lax.axis_size("blk")
    tiles = lax.axis_size("owner")
    ring = RING if tiles % RING == 0 else tiles
    inverse, right = diag_inverse[0], right_factor[0]
    rows = inverse.shape[0]
    groups = groups_of(partners // 2)
    all_pairs = jnp.bitwise_xor(blk // 2, jnp.array(sum(groups, []), jnp.int32))
    pairs = [jnp.bitwise_xor(blk // 2, jnp.array(group, jnp.int32)) for group in groups]
    offsets = [[2 * q + side for q in group for side in range(2)] for group in groups]
    fronts = [jnp.bitwise_xor(blk, jnp.array(ks, jnp.int32)) for ks in offsets]
    odd = (blk % 2).reshape(1)
    half = (owner % 2).reshape(1)
    second = ((owner + blk) % 2).reshape(1)

    def mate(tile, front):
        shift = front % 2
        place = (tile % ring + shift) ^ 1
        return tile // ring * ring + (place - shift) % ring

    across = [
        (tile * partners + front, mate(tile, front) * partners + front)
        for tile in range(tiles)
        for front in range(partners)
    ]

    def exchange(values, ks):
        steps = [[(i, i ^ k) for i in range(partners)] for k in ks]
        return [v if k == 0 else lax.ppermute(v, "blk", p) for v, k, p in zip(values, ks, steps)]

    def over_owner(value):
        return lax.all_to_all(value, "owner", split_axis=0, concat_axis=0, tiled=True)

    pattern = block_pattern.reshape(-1)
    masked, token = mask_all(rhs_pivot, pattern)
    front_rhs = lax.all_to_all(masked, "blk", split_axis=0, concat_axis=0, tiled=True)
    other_left = lax.ppermute(left_factor[0], ("owner", "blk"), across)
    kept, away = pack_contrib(half, contrib_rhs[0], token)
    got = lax.ppermute(away, ("owner", "blk"), across)

    ranks_here = lax.dynamic_index_in_dim(tile_ranks[0], owner, 1, keepdims=False)
    keep = jnp.arange(RK, dtype=jnp.int32)[None, :] < ranks_here[:, None]
    right_t = right_transposed(odd, right, keep.astype(jnp.float32).reshape(1, -1), ring)

    def tile_maps(tile):
        return lax.dynamic_slice_in_dim(parent_map, tile * rows, rows, 1)

    is_odd = (jnp.arange(partners) % 2 == 1)[:, None]
    other_maps = jnp.where(is_odd, tile_maps(mate(owner, 1)), tile_maps(mate(owner, 0)))
    maps = jnp.concatenate([tile_maps(owner), other_maps], axis=1)
    own_keys = lax.dynamic_index_in_dim(maps, blk, 0, keepdims=False).astype(jnp.float32)
    edges = (jnp.arange(tiles) * rows).astype(jnp.float32)
    ordered = jnp.sort(maps.astype(jnp.float32), axis=1)
    group_maps, starts = [], []
    for chosen in fronts:
        group_maps.append(jnp.take(ordered, chosen, axis=0))
        below = group_maps[-1][:, :, None] < edges[None, None, :]
        starts.append(jnp.sum(below.astype(jnp.int32), axis=1))

    solved, projected = [], []
    spread = [sorted_targets(keys, token) for keys in group_maps]
    ready = [later for _, later in spread] + [other_left, got]
    part, sent, _ = solve_group(pairs[0], odd, inverse, right_t, front_rhs, ring, ready)
    solved.append(part)
    projected.append(over_owner(sent))
    left, contrib, ready = sort_rows(second, own_keys, left_factor[0], other_left, kept, got)

    partial, token = None, None
    count = len(groups)
    for index in range(count):
        if index + 1 < count:
            part, sent, _ = solve_group(
                pairs[index + 1], odd, inverse, right_t, front_rhs, ring, [ready]
            )
            solved.append(part)
            projected.append(over_owner(sent))
        earlier = [] if partial is None else [token]
        coded = update_group(odd, pairs[index], left, projected[index], contrib, earlier)
        arrived = exchange(coded, offsets[index])
        dtype = jnp.float32 if index + 1 < count else jnp.bfloat16
        partial, token = scatter_rows(starts[index], spread[index][0], arrived, partial, dtype)
    parent_update = total_rows(over_owner(partial))
    pivot_solution = place_blocks(all_pairs, solved)
    return (pivot_solution, parent_update)


def solution(mesh):
    return jax.shard_map(
        per_device,
        mesh=mesh,
        in_specs=(
            P(None, "owner", "blk"),
            P(None, "owner", "blk"),
            P("blk", "owner", None),
            P("blk", "owner", None),
            P("blk", "owner", None),
            P("blk", None, None),
            P("blk", "owner", None),
            P(),
        ),
        out_specs=(P("blk", "owner", None), P("owner", "blk")),
        check_vma=False,
    )
```

time: 461 us -> 244 us (0.53)
  waiting for transfers between devices: 253 us -> 101 us
  other arithmetic: 74.9 us -> 7.42 us
  local copies, waits for them, and re-layouts: 77.9 us -> 11.7 us
  Pallas kernels: 0 us -> 61 us
  starting transfers between devices: 23.8 us -> 60.8 us
  matrix products: 15.4 us -> 0 us
  between operations: 14.2 us -> 0.96 us
    all_to_all x3 -> x4, waiting for transfers between devices: 174 us -> 57 us  [the longest x3 57 us: over_owner(): lax.all_to_all(value, 'owner', split_axis=0, concat_axis=0, tiled=True)]
    reduce_scatter x1 -> x0, waiting for transfers between devices: 78.8 us -> none  [per_device(): lax.psum_scatter(parent_buffer, 'owner', scatter_dimension=0, tiled=True)]
    pallas_call x0 -> x14, Pallas kernels: none -> 61 us  [the longest x2 11.8 us: scatter_rows(): pl.pallas_call(functools.partial(scatter_body, count, has_partial), out_s...]
    scatter-add x1 -> x0, other arithmetic: 46.6 us -> none  [per_device(): parent_buffer.at[owner_maps.reshape(-1)]]
    ppermute x0 -> x17, waiting for transfers between devices: none -> 44.2 us  [the longest x15 37.1 us: exchange(): lax.ppermute(v, 'blk', p)]
    unnamed x1 -> x0, other arithmetic: 26.7 us -> none
    ppermute x0 -> x17, starting transfers between devices: none -> 24.3 us  [the longest x15 22.2 us: exchange(): lax.ppermute(v, 'blk', p)]
    unnamed x26 -> x44, local copies, waits for them, and re-layouts: 34.2 us -> 10.2 us
  transfers between devices with their start and end apart: 4 -> 21, of which waited for: 4 -> 12; matrix products, arithmetic and copies ran while one was open for 1% -> 4% of each run, Pallas kernels for 0% -> 16%
where the time goes in v2:
time: 244 us; the launch traced here: 243 us
  waiting for transfers between devices  101 us (41%)
  Pallas kernels  61 us (25%)
  starting transfers between devices  60.8 us (25%)
  local copies, waits for them, and re-layouts  11.7 us (5%)
  other arithmetic  7.42 us (3%)
    all_to_all x3, waiting for transfers between devices, over_owner(): lax.all_to_all(value, 'owner', split_axis=0, concat_axis=0, tiled=True)  57 us
    ppermute x15, waiting for transfers between devices, exchange(): lax.ppermute(v, 'blk', p)  37.1 us
    all_to_all x3, starting transfers between devices, over_owner(): lax.all_to_all(value, 'owner', split_axis=0, concat_axis=0, tiled=True)  29.2 us
    ppermute x15, starting transfers between devices, exchange(): lax.ppermute(v, 'blk', p)  22.2 us
    pallas_call x2, Pallas kernels, scatter_rows(): pl.pallas_call(functools.partial(scatter_body, count, has_partial), out_s...  11.8 us
    pallas_call x2, Pallas kernels, update_group(): pl.pallas_call(functools.partial(update_body, count), out_shape=[pltpu.HB...  11.5 us
    unnamed x44, local copies, waits for them, and re-layouts  10.2 us
    pallas_call x1, Pallas kernels, sort_rows(): pl.pallas_call(sort_body, out_shape=[pltpu.HBM((joint, 2 * width), jnp.bf...  9.2 us
  transfers between devices with their start and end apart: 21, of which 12 were waited for; matrix products, arithmetic and copies ran while one was open for 4% of the time, Pallas kernels for 16%

profile of v2, /device:TPU:16, one launch (start us, length us, event | category | flops | bytes accessed | tf_op | source)
XLA Modules:
  0.0 243.1 jit_solution(17205348479019783974)
XLA Ops:
  0.6 0.0 copy-start
  0.6 3.9 %mask_all.1 = (bf16[16,512,128]{2,1,0:T(8,128)(2,1)}, f32[8,128]{1,0:T(8,128)}) custom-call(s32[16]{0:T(128)} %bitcast.14, bf16[16,512,128]{2,1,0:T(8,128)(2,1)} %rhs_ref.1), custom_call_target="tpu_custom_call" | custom-call | flops 1048576 | bytes 4194304 | tf_op jit(solution)/shard_map/mask_all/pallas_call | solution.py:80
  4.6 7.3 %all-to-all-start = ((bf16[16,512,128]{2,1,0:T(8,128)(2,1)}), bf16[16,512,128]{2,1,0:T(8,128)(2,1)S(1)}, u32[]{:S(2)}, u32[]{:S(2)}) async-start(bf16[16,512,128]{2,1,0:T(8,128)(2,1)} %get-tuple-element.39), calls=%async_computation | async-start | bytes 4194304 | tf_op jit(solution)/shard_map/all_to_all | solution.py:505
  11.8 0.0 copy-start.18
  11.9 3.1 %pack_contrib.1 = (bf16[512,1024]{1,0:T(8,128)(2,1)}, bf16[512,1024]{1,0:T(8,128)(2,1)}) custom-call(s32[1]{0:T(128)} %bitcast.5.high_ref, bf16[512,2048]{1,0:T(8,128)(2,1)} %bitcast.13, f32[8,128]{1,0:T(8,128)} %get-tuple-element.41.after_ref), custom_call_target="tpu_custom_call" | custom-call | flops 1048576 | bytes 4194304 | tf_op jit(solution)/shard_map/pack_contrib/pallas_call | solution.py:224
  14.9 2.0 collective-permute-start.1
  16.9 0.1 collective-permute-start
  17.1 0.9 constant_dynamic-slice_fusion
  18.0 5.8 %sort.15 = (f32[16,1024]{1,0:T(8,128)S(1)}, s32[16,1024]{1,0:T(8,128)}) sort(f32[16,1024]{1,0:T(8,128)S(1)} %fusion, s32[16,1024]{1,0:T(8,128)S(1)} %iota.20), dimensions={1}, to_apply=%region_0.1 | sort | flops 229376 | bytes 262144 | tf_op jit(solution)/shard_map/jit(sort)/sort | solution.py:522
  23.8 0.6 gather_fusion.1
  24.4 0.1 broadcast_select_fusion
  24.5 0.6 gather_fusion
  25.1 0.1 broadcast_select_fusion.1
  25.2 0.2 dynamic-slice_reduce_fusion
  25.4 0.1 fusion.1
  25.5 0.1 reshape.81.keep_ref
  25.6 1.2 copy-done.9
  26.8 1.4 right_transposed.1.right_ref
  28.2 3.0 %sorted_targets.3 = (f32[8,1024,128]{2,1,0:T(8,128)}, f32[8,128]{1,0:T(8,128)S(1)}) custom-call(f32[8,1,1024]{2,1,0:T(1,128)S(1)} %reshape.78.keys_ref, f32[8,128]{1,0:T(8,128)S(1)} %copy-done.10), custom_call_target="tpu_custom_call" | custom-call | flops 1048576 | bytes 4194304 | tf_op jit(solution)/shard_map/sorted_targets/pallas_call | solution.py:316
  31.2 3.1 %sorted_targets.2 = (f32[8,1024,128]{2,1,0:T(8,128)}, f32[8,128]{1,0:T(8,128)S(1)}) custom-call(f32[8,1,1024]{2,1,0:T(1,128)S(1)} %reshape.77.keys_ref, f32[8,128]{1,0:T(8,128)S(1)} %copy-done.10), custom_call_target="tpu_custom_call" | custom-call | flops 1048576 | bytes 4194304 | tf_op jit(solution)/shard_map/sorted_targets/pallas_call | solution.py:316
  34.3 7.1 %collective-permute-done.refs_6_.other_ref = bf16[512,1024]{1,0:T(8,128)(2,1)} collective-permute-done((bf16[512,1024]{1,0:T(8,128)(2,1)}, bf16[512,1024]{1,0:T(8,128)(2,1)}, u32[]{:S(2)}, u32[]{:S(2)}) %collective-permute-start) | collective-permute-done | bytes 1048608 | tf_op jit(solution)/shard_map/ppermute | solution.py:506
  41.4 1.2 copy-done.3
  42.6 4.3 %solve_group.2 = (bf16[4,2,512,128]{3,2,1,0:T(8,128)(2,1)}, bf16[16,128,512]{2,1,0:T(8,128)(2,1)}, f32[8,128]{1,0:T(8,128)}) custom-call(s32[4]{0:T(128)S(1)} %broadcast_xor_fusion.1.pairs_ref, s32[1]{0:T(128)} %bitcast.odd_ref, bf16[512,512]{1,0:T(8,128)(2,1)S(1)} %bitcast.8, bf16[1024,512]{1,0:T(8,128)(2,1)S(1)} %copy-done.3, ...), custom_call_target="tpu_custom_call" | custom-call | flops 1610612736 | bytes 4194304 | tf_op jit(solution)/shard_map/solve_group/pallas_call | solution.py:149
  46.9 9.5 %all-to-all-start.2 = ((bf16[16,128,512]{2,1,0:T(8,128)(2,1)}), bf16[16,128,512]{2,1,0:T(8,128)(2,1)}, u32[]{:S(2)}, u32[]{:S(2)}) async-start(bf16[16,128,512]{2,1,0:T(8,128)(2,1)} %get-tuple-element.54), calls=%async_computation.2 | async-start | bytes 4194304 | tf_op jit(solution)/shard_map/all_to_all | solution.py:501
  56.5 1.2 copy-done.13
  57.7 1.2 copy-done.14
  58.9 9.2 %sort_rows.1 = (bf16[1024,2048]{1,0:T(8,128)(2,1)}, bf16[8,1024,128]{2,1,0:T(8,128)(2,1)}, f32[8,128]{1,0:T(8,128)S(1)}) custom-call(s32[1]{0:T(128)} %bitcast.7.high_ref, f32[1,1024]{1,0:T(1,128)S(1)} %fusion.3.keys_ref, bf16[512,1024]{1,0:T(8,128)(2,1)S(1)} %bitcast.12, bf16[512,1024]{1,0:T(8,128)(2,1)} %collective-permute-done.refs_6_.other_ref, ...), custom_call_target="tpu_custom_call" | custom-call | flops 4294967296 | bytes 8388608 | tf_op jit(solution)/shard_map/sort_rows/pallas_call | solution.py:278
  68.1 4.3 %solve_group.3 = (bf16[4,2,512,128]{3,2,1,0:T(8,128)(2,1)}, bf16[16,128,512]{2,1,0:T(8,128)(2,1)}, f32[8,128]{1,0:T(8,128)}) custom-call(s32[4]{0:T(128)S(1)} %broadcast_xor_fusion.pairs_ref, s32[1]{0:T(128)} %bitcast.odd_ref, bf16[512,512]{1,0:T(8,128)(2,1)S(1)} %bitcast.9, bf16[1024,512]{1,0:T(8,128)(2,1)S(1)} %copy-done.4, ...), custom_call_target="tpu_custom_call" | custom-call | flops 1610612736 | bytes 4194304 | tf_op jit(solution)/shard_map/solve_group/pallas_call | solution.py:149
  72.4 33.3 %all-to-all-done.2.projected_ref = bf16[16,128,512]{2,1,0:T(8,128)(2,1)} async-done(((bf16[16,128,512]{2,1,0:T(8,128)(2,1)}), bf16[16,128,512]{2,1,0:T(8,128)(2,1)}, u32[]{:S(2)}, u32[]{:S(2)}) %all-to-all-start.2) | async-done | bytes 2097184 | tf_op jit(solution)/shard_map/all_to_all | solution.py:501
  105.8 6.1 %all-to-all-start.1 = ((bf16[16,128,512]{2,1,0:T(8,128)(2,1)}), bf16[16,128,512]{2,1,0:T(8,128)(2,1)}, u32[]{:S(2)}, u32[]{:S(2)}) async-start(bf16[16,128,512]{2,1,0:T(8,128)(2,1)} %get-tuple-element.51), calls=%async_computation.1 | async-start | bytes 4194304 | tf_op jit(solution)/shard_map/all_to_all | solution.py:501
  111.9 2.2 copy-done.1
  114.1 5.7 %update_group.2 = (s16[528,128]{1,0:T(8,128)(2,1)}, s16[528,128]{1,0:T(8,128)(2,1)}, s16[528,128]{1,0:T(8,128)(2,1)}, s16[528,128]{1,0:T(8,128)(2,1)}, s16[528,1...) custom-call(s32[1]{0:T(128)} %bitcast.odd_ref, ...), custom_call_target="tpu_custom_call" | custom-call | flops 2147483648 | bytes 4194304 | tf_op jit(solution)/shard_map/update_group/pallas_call | solution.py:357
  119.8 0.8 collective-permute-start.2
  120.6 1.8 collective-permute-start.3
  122.4 1.8 collective-permute-start.4
  124.3 3.0 %collective-permute-start.5 = (s16[528,128]{1,0:T(8,128)(2,1)}, s16[528,128]{1,0:T(8,128)(2,1)S(1)}, u32[]{:S(2)}, u32[]{:S(2)}) collective-permute-start(s16[528,128]{1,0:T(8,128)(2,1)} %get-tuple-element.58), channel_id=1, source_target_pairs={{0,11},{1,10},{2,9},{3,8},{4,15},{5,14},{6,13},{7,12},{8,3},{9,2},... | collective-permute-start | bytes 405512 | tf_op jit(solution)/shard_map/ppermute | solution.py:498
  127.2 2.5 %collective-permute-start.6 = (s16[528,128]{1,0:T(8,128)(2,1)}, s16[528,128]{1,0:T(8,128)(2,1)S(1)}, u32[]{:S(2)}, u32[]{:S(2)}) collective-permute-start(s16[528,128]{1,0:T(8,128)(2,1)} %get-tuple-element.59), channel_id=1, source_target_pairs={{0,12},{1,13},{2,14},{3,15},{4,8},{5,9},{6,10},{7,11},{8,4},{9,5},... | collective-permute-start | bytes 405512 | tf_op jit(solution)/shard_map/ppermute | solution.py:498
  129.7 17.1 %collective-permute-done.2.refs_0_ = s16[528,128]{1,0:T(8,128)(2,1)S(1)} collective-permute-done((s16[528,128]{1,0:T(8,128)(2,1)}, s16[528,128]{1,0:T(8,128)(2,1)S(1)}, u32[]{:S(2)}, u32[]{:S(2)}) %collective-permute-start.2) | collective-permute-done | bytes 135200 | tf_op jit(solution)/shard_map/ppermute | solution.py:498
  146.8 3.8 %collective-permute-done.3.refs_1_ = s16[528,128]{1,0:T(8,128)(2,1)S(1)} collective-permute-done((s16[528,128]{1,0:T(8,128)(2,1)}, s16[528,128]{1,0:T(8,128)(2,1)S(1)}, u32[]{:S(2)}, u32[]{:S(2)}) %collective-permute-start.3) | collective-permute-done | bytes 135200 | tf_op jit(solution)/shard_map/ppermute | solution.py:498
  150.6 3.5 %collective-permute-start.8 = (s16[528,128]{1,0:T(8,128)(2,1)}, s16[528,128]{1,0:T(8,128)(2,1)S(1)}, u32[]{:S(2)}, u32[]{:S(2)}) collective-permute-start(s16[528,128]{1,0:T(8,128)(2,1)} %get-tuple-element.61), channel_id=1, source_target_pairs={{0,4},{1,5},{2,6},{3,7},{4,0},{5,1},{6,2},{7,3},{8,12},{9,13},{10,... | collective-permute-start | bytes 405512 | tf_op jit(solution)/shard_map/ppermute | solution.py:498
  154.1 0.1 collective-permute-start.9
  154.2 0.4 convert_reduce_fusion
  154.7 1.1 collective-permute-done.7.refs_5_
  155.8 2.8 %collective-permute-done.8.refs_6_ = s16[528,128]{1,0:T(8,128)(2,1)S(1)} collective-permute-done((s16[528,128]{1,0:T(8,128)(2,1)}, s16[528,128]{1,0:T(8,128)(2,1)S(1)}, u32[]{:S(2)}, u32[]{:S(2)}) %collective-permute-start.8) | collective-permute-done | bytes 135200 | tf_op jit(solution)/shard_map/ppermute | solution.py:498
  158.6 3.1 %collective-permute-done.9.refs_7_ = s16[528,128]{1,0:T(8,128)(2,1)S(1)} collective-permute-done((s16[528,128]{1,0:T(8,128)(2,1)}, s16[528,128]{1,0:T(8,128)(2,1)S(1)}, u32[]{:S(2)}, u32[]{:S(2)}) %collective-permute-start.9) | collective-permute-done | bytes 135200 | tf_op jit(solution)/shard_map/ppermute | solution.py:498
  161.7 5.9 %scatter_rows.2 = (f32[16,64,512]{2,1,0:T(8,128)}, f32[8,128]{1,0:T(8,128)S(1)}) custom-call(s32[8,16]{1,0:T(8,128)S(1)} %get-tuple-element.74.starts_ref, f32[8,1024,128]{2,1,0:T(8,128)S(1)} %copy-done.12, s16[528,128]{1,0:T(8,128)(2,1)S(1)} %collective-permute-done.2.refs_0_, s16[528,128]{1,0:T(8,128)(2,1)S(1)} %collective-permute-done.3.refs_1_, ...), custom_call_target="tpu_custom_call" | custom-call | flops 2415919104 | bytes 4194304 | tf_op jit(solution)/shard_map/scatter_rows/pallas_call | solution.py:423
  167.6 2.2 copy-done.2
  169.8 5.7 %update_group.3 = (s16[528,128]{1,0:T(8,128)(2,1)}, s16[528,128]{1,0:T(8,128)(2,1)}, s16[528,128]{1,0:T(8,128)(2,1)}, s16[528,128]{1,0:T(8,128)(2,1)}, s16[528,1...) custom-call(s32[1]{0:T(128)} %bitcast.odd_ref, ...), custom_call_target="tpu_custom_call" | custom-call | flops 2147483648 | bytes 4194304 | tf_op jit(solution)/shard_map/update_group/pallas_call | solution.py:357
  175.6 4.3 %collective-permute-start.10 = (s16[528,128]{1,0:T(8,128)(2,1)}, s16[528,128]{1,0:T(8,128)(2,1)S(1)}, u32[]{:S(2)}, u32[]{:S(2)}) collective-permute-start(s16[528,128]{1,0:T(8,128)(2,1)} %get-tuple-element.64), channel_id=1, source_target_pairs={{0,14},{1,15},{2,12},{3,13},{4,10},{5,11},{6,8},{7,9},{8,6},{9,7},... | collective-permute-start | bytes 405512 | tf_op jit(solution)/shard_map/ppermute | solution.py:498
  179.8 0.9 collective-permute-start.11
  180.7 1.5 collective-permute-start.12
  182.3 1.6 collective-permute-start.13
  183.9 1.2 collective-permute-done.10.refs_0_
  185.1 0.4 collective-permute-start.15
  185.4 4.1 %collective-permute-done.11.refs_1_ = s16[528,128]{1,0:T(8,128)(2,1)S(1)} collective-permute-done((s16[528,128]{1,0:T(8,128)(2,1)}, s16[528,128]{1,0:T(8,128)(2,1)S(1)}, u32[]{:S(2)}, u32[]{:S(2)}) %collective-permute-start.11) | collective-permute-done | bytes 135200 | tf_op jit(solution)/shard_map/ppermute | solution.py:498
  189.5 0.1 collective-permute-start.16
  189.7 2.6 %collective-permute-done.12.refs_2_ = s16[528,128]{1,0:T(8,128)(2,1)S(1)} collective-permute-done((s16[528,128]{1,0:T(8,128)(2,1)}, s16[528,128]{1,0:T(8,128)(2,1)S(1)}, u32[]{:S(2)}, u32[]{:S(2)}) %collective-permute-start.12) | collective-permute-done | bytes 135200 | tf_op jit(solution)/shard_map/ppermute | solution.py:498
  192.3 1.2 collective-permute-done.13.refs_3_
  193.5 0.9 copy-done.15
  194.4 5.9 %scatter_rows.3 = (bf16[16,64,512]{2,1,0:T(8,128)(2,1)}, f32[8,128]{1,0:T(8,128)}) custom-call(s32[8,16]{1,0:T(8,128)S(1)} %get-tuple-element.75.starts_ref, f32[8,1024,128]{2,1,0:T(8,128)S(1)} %copy-done.11, s16[528,128]{1,0:T(8,128)(2,1)S(1)} %collective-permute-done.10.refs_0_, s16[528,128]{1,0:T(8,128)(2,1)S(1)} %collective-permute-done.11.refs_1_, ...), custom_call_target="tpu_custom_call" | custom-call | flops 2415919104 | bytes 4194304 | tf_op jit(solution)/shard_map/scatter_rows/pallas_call | solution.py:423
  200.3 13.6 %all-to-all-start.3 = ((bf16[16,64,512]{2,1,0:T(8,128)(2,1)}), bf16[16,64,512]{2,1,0:T(8,128)(2,1)S(1)}, u32[]{:S(2)}, u32[]{:S(2)}) async-start(bf16[16,64,512]{2,1,0:T(8,128)(2,1)} %get-tuple-element.73), calls=%async_computation.3 | async-start | bytes 2097152 | tf_op jit(solution)/shard_map/all_to_all | solution.py:501
  214.0 3.7 %place_blocks.1 = bf16[1,512,2048]{2,1,0:T(8,128)(2,1)} custom-call(s32[8]{0:T(128)S(1)} %broadcast_xor_fusion.2.pairs_ref, bf16[4,2,512,128]{3,2,1,0:T(8,128)(2,1)S(1)} %copy-done.7, bf16[4,2,512,128]{3,2,1,0:T(8,128)(2,1)S(1)} %copy-done.8), custom_call_target="tpu_custom_call" | custom-call | bytes 4194304 | tf_op jit(solution)/shard_map/place_blocks/pallas_call | solution.py:194
  217.7 23.7 %all-to-all-done.3.parts_ref = bf16[16,64,512]{2,1,0:T(8,128)(2,1)S(1)} async-done(((bf16[16,64,512]{2,1,0:T(8,128)(2,1)}), bf16[16,64,512]{2,1,0:T(8,128)(2,1)S(1)}, u32[]{:S(2)}, u32[]{:S(2)}) %all-to-all-start.3) | async-done | bytes 1048608 | tf_op jit(solution)/shard_map/all_to_all | solution.py:501
  241.3 1.7 total_rows.1
  (59 shorter events, 0.2 us)
Async XLA Ops:
  0.6 24.6 %copy-start = (s32[1,16,16]{2,1,0:T(8,128)S(1)}, s32[1,16,16]{2,1,0:T(8,128)}, u32[]{:S(2)}) copy-start(s32[1,16,16]{2,1,0:T(8,128)} %param.20) | copy-start | bytes 3076
  4.6 36.8 %all-to-all-start = ((bf16[16,512,128]{2,1,0:T(8,128)(2,1)}), bf16[16,512,128]{2,1,0:T(8,128)(2,1)S(1)}, u32[]{:S(2)}, u32[]{:S(2)}) async-start(bf16[16,512,128]{2,1,0:T(8,128)(2,1)} %get-tuple-element.39), calls=%async_computation | async-start | bytes 4194304 | tf_op jit(solution)/shard_map/all_to_all | solution.py:505
  11.8 6.1 %copy-start.17 = (s32[8]{0:T(128)S(1)}, s32[8]{0:T(128)}, u32[]{:S(2)}) copy-start(s32[8]{0:T(128)} %constant.138.clone) | copy-start | bytes 100
  11.8 6.1 %copy-start.18 = (s32[8]{0:T(128)S(1)}, s32[8]{0:T(128)}, u32[]{:S(2)}) copy-start(s32[8]{0:T(128)} %constant.139.clone) | copy-start | bytes 100
  14.9 13.3 %copy-start.10 = (f32[8,128]{1,0:T(8,128)S(1)}, f32[8,128]{1,0:T(8,128)}, u32[]{:S(2)}) copy-start(f32[8,128]{1,0:T(8,128)} %get-tuple-element.41.after_ref) | copy-start | bytes 12292
  14.9 19.4 %copy-start.21 = (s32[4]{0:T(128)S(1)}, s32[4]{0:T(128)}, u32[]{:S(2)}) copy-start(s32[4]{0:T(128)} %constant.136.clone) | copy-start | bytes 52
  14.9 26.4 %copy-start.6 = (bf16[1,512,512]{2,1,0:T(8,128)(2,1)S(1)}, bf16[1,512,512]{2,1,0:T(8,128)(2,1)}, u32[]{:S(2)}) copy-start(bf16[1,512,512]{2,1,0:T(8,128)(2,1)} %param.17) | copy-start | bytes 1572868
  14.9 19.4 %collective-permute-start.1 = (bf16[512,1024]{1,0:T(8,128)(2,1)}, bf16[512,1024]{1,0:T(8,128)(2,1)}, u32[]{:S(2)}, u32[]{:S(2)}) collective-permute-start(bf16[512,1024]{1,0:T(8,128)(2,1)} %get-tuple-element.44), channel_id=1, source_target_pairs={{0,16},{1,113},{2,18},{3,115},{4,20},{5,117},{6,22},{7,119},{8,24}... | collective-permute-start | bytes 3145736 | tf_op jit(solution)/shard_map/ppermute | solution.py:508
  16.9 24.4 %collective-permute-start = (bf16[512,1024]{1,0:T(8,128)(2,1)}, bf16[512,1024]{1,0:T(8,128)(2,1)}, u32[]{:S(2)}, u32[]{:S(2)}) collective-permute-start(bf16[512,1024]{1,0:T(8,128)(2,1)} %bitcast.11), channel_id=1, source_target_pairs={{0,16},{1,113},{2,18},{3,115},{4,20},{5,117},{6,22},{7,119},{8,24}... | collective-permute-start | bytes 3145736 | tf_op jit(solution)/shard_map/ppermute | solution.py:506
  25.6 1.2 copy-start.9
  41.4 1.2 copy-start.3
  46.9 9.5 %copy-start.20 = (s32[4]{0:T(128)S(1)}, s32[4]{0:T(128)}, u32[]{:S(2)}) copy-start(s32[4]{0:T(128)} %constant.137.clone) | copy-start | bytes 52
  46.9 58.8 %all-to-all-start.2 = ((bf16[16,128,512]{2,1,0:T(8,128)(2,1)}), bf16[16,128,512]{2,1,0:T(8,128)(2,1)}, u32[]{:S(2)}, u32[]{:S(2)}) async-start(bf16[16,128,512]{2,1,0:T(8,128)(2,1)} %get-tuple-element.54), calls=%async_computation.2 | async-start | bytes 4194304 | tf_op jit(solution)/shard_map/all_to_all | solution.py:501
  56.5 1.2 copy-start.13
  57.7 1.2 copy-start.14
  58.9 9.2 %copy-start.4 = (bf16[1024,512]{1,0:T(8,128)(2,1)S(1)}, bf16[1024,512]{1,0:T(8,128)(2,1)}, u32[]{:S(2)}) copy-start(bf16[1024,512]{1,0:T(8,128)(2,1)} %right_transposed.1.right_ref) | copy-start | bytes 3145732
  105.8 6.1 %copy-start.5 = (bf16[8,1024,128]{2,1,0:T(8,128)(2,1)S(1)}, bf16[8,1024,128]{2,1,0:T(8,128)(2,1)}, u32[]{:S(2)}) copy-start(bf16[8,1024,128]{2,1,0:T(8,128)(2,1)} %get-tuple-element.52.contrib_ref) | copy-start | bytes 6291460
  105.8 61.8 %all-to-all-start.1 = ((bf16[16,128,512]{2,1,0:T(8,128)(2,1)}), bf16[16,128,512]{2,1,0:T(8,128)(2,1)}, u32[]{:S(2)}, u32[]{:S(2)}) async-start(bf16[16,128,512]{2,1,0:T(8,128)(2,1)} %get-tuple-element.51), calls=%async_computation.1 | async-start | bytes 4194304 | tf_op jit(solution)/shard_map/all_to_all | solution.py:501
  111.9 2.2 copy-start.1
  114.1 47.6 %copy-start.12 = (f32[8,1024,128]{2,1,0:T(8,128)S(1)}, f32[8,1024,128]{2,1,0:T(8,128)}, u32[]{:S(2)}) copy-start(f32[8,1024,128]{2,1,0:T(8,128)} %get-tuple-element.53.targets_ref) | copy-start | bytes 12582916
  119.8 27.0 %collective-permute-start.2 = (s16[528,128]{1,0:T(8,128)(2,1)}, s16[528,128]{1,0:T(8,128)(2,1)S(1)}, u32[]{:S(2)}, u32[]{:S(2)}) collective-permute-start(s16[528,128]{1,0:T(8,128)(2,1)} %get-tuple-element.55), channel_id=1, source_target_pairs={{0,8},{1,9},{2,10},{3,11},{4,12},{5,13},{6,14},{7,15},{8,0},{9,1},... | collective-permute-start | bytes 405512 | tf_op jit(solution)/shard_map/ppermute | solution.py:498
  120.6 30.0 %collective-permute-start.3 = (s16[528,128]{1,0:T(8,128)(2,1)}, s16[528,128]{1,0:T(8,128)(2,1)S(1)}, u32[]{:S(2)}, u32[]{:S(2)}) collective-permute-start(s16[528,128]{1,0:T(8,128)(2,1)} %get-tuple-element.56), channel_id=1, source_target_pairs={{0,9},{1,8},{2,11},{3,10},{4,13},{5,12},{6,15},{7,14},{8,1},{9,0},... | collective-permute-start | bytes 405512 | tf_op jit(solution)/shard_map/ppermute | solution.py:498
  122.4 31.7 %collective-permute-start.4 = (s16[528,128]{1,0:T(8,128)(2,1)}, s16[528,128]{1,0:T(8,128)(2,1)S(1)}, u32[]{:S(2)}, u32[]{:S(2)}) collective-permute-start(s16[528,128]{1,0:T(8,128)(2,1)} %get-tuple-element.57), channel_id=1, source_target_pairs={{0,10},{1,11},{2,8},{3,9},{4,14},{5,15},{6,12},{7,13},{8,2},{9,3},... | collective-permute-start | bytes 405512 | tf_op jit(solution)/shard_map/ppermute | solution.py:498
  124.3 30.4 %collective-permute-start.5 = (s16[528,128]{1,0:T(8,128)(2,1)}, s16[528,128]{1,0:T(8,128)(2,1)S(1)}, u32[]{:S(2)}, u32[]{:S(2)}) collective-permute-start(s16[528,128]{1,0:T(8,128)(2,1)} %get-tuple-element.58), channel_id=1, source_target_pairs={{0,11},{1,10},{2,9},{3,8},{4,15},{5,14},{6,13},{7,12},{8,3},{9,2},... | collective-permute-start | bytes 405512 | tf_op jit(solution)/shard_map/ppermute | solution.py:498
  127.2 27.4 %collective-permute-start.6 = (s16[528,128]{1,0:T(8,128)(2,1)}, s16[528,128]{1,0:T(8,128)(2,1)S(1)}, u32[]{:S(2)}, u32[]{:S(2)}) collective-permute-start(s16[528,128]{1,0:T(8,128)(2,1)} %get-tuple-element.59), channel_id=1, source_target_pairs={{0,12},{1,13},{2,14},{3,15},{4,8},{5,9},{6,10},{7,11},{8,4},{9,5},... | collective-permute-start | bytes 405512 | tf_op jit(solution)/shard_map/ppermute | solution.py:498
  146.8 8.9 %collective-permute-start.7 = (s16[528,128]{1,0:T(8,128)(2,1)}, s16[528,128]{1,0:T(8,128)(2,1)S(1)}, u32[]{:S(2)}, u32[]{:S(2)}) collective-permute-start(s16[528,128]{1,0:T(8,128)(2,1)} %get-tuple-element.60), channel_id=1, source_target_pairs={{0,13},{1,12},{2,15},{3,14},{4,9},{5,8},{6,11},{7,10},{8,5},{9,4},... | collective-permute-start | bytes 405512 | tf_op jit(solution)/shard_map/ppermute | solution.py:498
  150.6 7.9 %collective-permute-start.8 = (s16[528,128]{1,0:T(8,128)(2,1)}, s16[528,128]{1,0:T(8,128)(2,1)S(1)}, u32[]{:S(2)}, u32[]{:S(2)}) collective-permute-start(s16[528,128]{1,0:T(8,128)(2,1)} %get-tuple-element.61), channel_id=1, source_target_pairs={{0,4},{1,5},{2,6},{3,7},{4,0},{5,1},{6,2},{7,3},{8,12},{9,13},{10,... | collective-permute-start | bytes 405512 | tf_op jit(solution)/shard_map/ppermute | solution.py:498
  154.1 7.6 %collective-permute-start.9 = (s16[528,128]{1,0:T(8,128)(2,1)}, s16[528,128]{1,0:T(8,128)(2,1)S(1)}, u32[]{:S(2)}, u32[]{:S(2)}) collective-permute-start(s16[528,128]{1,0:T(8,128)(2,1)} %get-tuple-element.62), channel_id=1, source_target_pairs={{0,5},{1,4},{2,7},{3,6},{4,1},{5,0},{6,3},{7,2},{8,13},{9,12},{10,... | collective-permute-start | bytes 405512 | tf_op jit(solution)/shard_map/ppermute | solution.py:498
  167.6 2.2 copy-start.2
  169.8 23.7 %copy-start.11 = (f32[8,1024,128]{2,1,0:T(8,128)S(1)}, f32[8,1024,128]{2,1,0:T(8,128)}, u32[]{:S(2)}) copy-start(f32[8,1024,128]{2,1,0:T(8,128)} %get-tuple-element.49.targets_ref) | copy-start | bytes 12582916
  169.8 23.7 %copy-start.16 = (f32[16,64,512]{2,1,0:T(8,128)S(1)}, f32[16,64,512]{2,1,0:T(8,128)}, u32[]{:S(2)}) copy-start(f32[16,64,512]{2,1,0:T(8,128)} %get-tuple-element.72.refs_8_) | copy-start | bytes 6291460
  175.6 9.5 %collective-permute-start.10 = (s16[528,128]{1,0:T(8,128)(2,1)}, s16[528,128]{1,0:T(8,128)(2,1)S(1)}, u32[]{:S(2)}, u32[]{:S(2)}) collective-permute-start(s16[528,128]{1,0:T(8,128)(2,1)} %get-tuple-element.64), channel_id=1, source_target_pairs={{0,14},{1,15},{2,12},{3,13},{4,10},{5,11},{6,8},{7,9},{8,6},{9,7},... | collective-permute-start | bytes 405512 | tf_op jit(solution)/shard_map/ppermute | solution.py:498
  179.8 9.7 %collective-permute-start.11 = (s16[528,128]{1,0:T(8,128)(2,1)}, s16[528,128]{1,0:T(8,128)(2,1)S(1)}, u32[]{:S(2)}, u32[]{:S(2)}) collective-permute-start(s16[528,128]{1,0:T(8,128)(2,1)} %get-tuple-element.65), channel_id=1, source_target_pairs={{0,15},{1,14},{2,13},{3,12},{4,11},{5,10},{6,9},{7,8},{8,7},{9,6},... | collective-permute-start | bytes 405512 | tf_op jit(solution)/shard_map/ppermute | solution.py:498
  180.7 11.5 %collective-permute-start.12 = (s16[528,128]{1,0:T(8,128)(2,1)}, s16[528,128]{1,0:T(8,128)(2,1)S(1)}, u32[]{:S(2)}, u32[]{:S(2)}) collective-permute-start(s16[528,128]{1,0:T(8,128)(2,1)} %get-tuple-element.66), channel_id=1, source_target_pairs={{0,6},{1,7},{2,4},{3,5},{4,2},{5,3},{6,0},{7,1},{8,14},{9,15},{10,... | collective-permute-start | bytes 405512 | tf_op jit(solution)/shard_map/ppermute | solution.py:498
  182.3 11.2 %collective-permute-start.13 = (s16[528,128]{1,0:T(8,128)(2,1)}, s16[528,128]{1,0:T(8,128)(2,1)S(1)}, u32[]{:S(2)}, u32[]{:S(2)}) collective-permute-start(s16[528,128]{1,0:T(8,128)(2,1)} %get-tuple-element.67), channel_id=1, source_target_pairs={{0,7},{1,6},{2,5},{3,4},{4,3},{5,2},{6,1},{7,0},{8,15},{9,14},{10,... | collective-permute-start | bytes 405512 | tf_op jit(solution)/shard_map/ppermute | solution.py:498
  183.9 9.6 %collective-permute-start.14 = (s16[528,128]{1,0:T(8,128)(2,1)}, s16[528,128]{1,0:T(8,128)(2,1)S(1)}, u32[]{:S(2)}, u32[]{:S(2)}) collective-permute-start(s16[528,128]{1,0:T(8,128)(2,1)} %get-tuple-element.68), channel_id=1, source_target_pairs={{0,2},{1,3},{2,0},{3,1},{4,6},{5,7},{6,4},{7,5},{8,10},{9,11},{10,... | collective-permute-start | bytes 405512 | tf_op jit(solution)/shard_map/ppermute | solution.py:498
  185.1 8.4 %collective-permute-start.15 = (s16[528,128]{1,0:T(8,128)(2,1)}, s16[528,128]{1,0:T(8,128)(2,1)S(1)}, u32[]{:S(2)}, u32[]{:S(2)}) collective-permute-start(s16[528,128]{1,0:T(8,128)(2,1)} %get-tuple-element.69), channel_id=1, source_target_pairs={{0,3},{1,2},{2,1},{3,0},{4,7},{5,6},{6,5},{7,4},{8,11},{9,10},{10,... | collective-permute-start | bytes 405512 | tf_op jit(solution)/shard_map/ppermute | solution.py:498
  189.5 4.0 %collective-permute-start.16 = (s16[528,128]{1,0:T(8,128)(2,1)}, s16[528,128]{1,0:T(8,128)(2,1)S(1)}, u32[]{:S(2)}, u32[]{:S(2)}) collective-permute-start(s16[528,128]{1,0:T(8,128)(2,1)} %get-tuple-element.71), channel_id=1, source_target_pairs={{0,1},{1,0},{2,3},{3,2},{4,5},{5,4},{6,7},{7,6},{8,9},{9,8},{10,11... | collective-permute-start | bytes 405512 | tf_op jit(solution)/shard_map/ppermute | solution.py:498
  193.5 0.9 copy-start.15
  200.3 13.6 %copy-start.19 = (s32[8]{0:T(128)S(1)}, s32[8]{0:T(128)}, u32[]{:S(2)}) copy-start(s32[8]{0:T(128)} %constant.135.clone) | copy-start | bytes 100
  200.3 13.6 %copy-start.7 = (bf16[4,2,512,128]{3,2,1,0:T(8,128)(2,1)S(1)}, bf16[4,2,512,128]{3,2,1,0:T(8,128)(2,1)}, u32[]{:S(2)}) copy-start(bf16[4,2,512,128]{3,2,1,0:T(8,128)(2,1)} %get-tuple-element.45.refs_0_) | copy-start | bytes 3145732
  200.3 13.7 %copy-start.8 = (bf16[4,2,512,128]{3,2,1,0:T(8,128)(2,1)S(1)}, bf16[4,2,512,128]{3,2,1,0:T(8,128)(2,1)}, u32[]{:S(2)}) copy-start(bf16[4,2,512,128]{3,2,1,0:T(8,128)(2,1)} %get-tuple-element.48.refs_1_) | copy-start | bytes 3145732
  200.3 41.0 %all-to-all-start.3 = ((bf16[16,64,512]{2,1,0:T(8,128)(2,1)}), bf16[16,64,512]{2,1,0:T(8,128)(2,1)S(1)}, u32[]{:S(2)}, u32[]{:S(2)}) async-start(bf16[16,64,512]{2,1,0:T(8,128)(2,1)} %get-tuple-element.73), calls=%async_computation.3 | async-start | bytes 2097152 | tf_op jit(solution)/shard_map/all_to_all | solution.py:501

commit v3 on v2

--- a/solution.py
+++ b/solution.py
@@ -13,6 +13,7 @@
 HALF = CW // 2
 EXP_ROWS = 16
 RING = 8
+BATCH = 4
 TILE_BATCH = 4
 CODE_BITS = 14
 MIB = 1024 * 1024
@@ -52,7 +53,7 @@
 
 def groups_of(count):
     if count == 8:
-        return [[4, 5, 6, 2], [7, 3, 1, 0]]
+        return [[4, 5, 2, 3], [6, 7, 1, 0]]
     return [list(range(count // 2, count)), list(range(count // 2))]
 
 
@@ -228,7 +229,7 @@
         in_specs=[smem(), pl.BlockSpec((rows, cols // 2), lambda i: (0, i))] + untouched(1),
         out_specs=[spec] * 2,
         compiler_params=params(60),
-        cost_estimate=cost(rows * cols, 4 * rows * cols),
+        cost_estimate=cost(0, MIB),
         name="pack_contrib",
     )(high, contrib, earlier)
 
@@ -320,7 +321,7 @@
         in_specs=[pl.BlockSpec((batch, 1, rows), lambda i: (i, 0, 0))] + untouched(1),
         out_specs=[pl.BlockSpec((batch, rows, CW), lambda i: (i, 0, 0)), token_spec()],
         compiler_params=params(16),
-        cost_estimate=cost(count * rows * CW, 4 * count * rows * CW),
+        cost_estimate=cost(0, MIB),
         name="sorted_targets",
     )(maps.reshape(count, 1, rows), earlier)
 
@@ -334,35 +335,47 @@
     out_ref[rows:, :] = jnp.broadcast_to(exponent.astype(jnp.int32), (EXP_ROWS, CW)).astype(jnp.int16)
 
 
-def update_body(count, odd_ref, pairs_ref, left_ref, projected_ref, contrib_ref, *refs):
+def update_body(count, pairs_ref, odd_ref, left_ref, projected_ref, *refs):
+    contribs = refs[:count]
     out_refs = refs[-2 * count :]
     joint, width = left_ref.shape
     rows = joint // 2
-    odd = odd_ref[0] > 0
-    for start in range(0, count, 2):
-        span = min(2, count - start)
-        part = projected_ref[:, :, start * CW : (start + span) * CW].reshape(width, span * CW)
-        product = jnp.dot(left_ref[...], part, preferred_element_type=jnp.float32)
-        for step in range(start, start + span):
-            reduced = contrib_ref[pairs_ref[step]].astype(jnp.float32)
-            reduced = reduced - product[:, (step - start) * CW : (step - start + 1) * CW]
-            first, second = swapped(odd, *halves(reduced[:rows], reduced[rows:]))
-            coded_rows(first, out_refs[2 * step])
-            coded_rows(second, out_refs[2 * step + 1])
-
-
-def update_group(odd, pairs, left, projected, contrib, earlier):
+    part = projected_ref[...].reshape(width, count * CW)
+    product = jnp.dot(left_ref[...], part, preferred_element_type=jnp.float32)
+    for step in range(count):
+        reduced = contribs[step][0].astype(jnp.float32) - product[:, step * CW : (step + 1) * CW]
+        sides = swapped(odd_ref[0] > 0, *halves(reduced[:rows], reduced[rows:]))
+        coded_rows(sides[0], out_refs[2 * step])
+        coded_rows(sides[1], out_refs[2 * step + 1])
+
+
+def update_group(odd, pairs, left, projected, place, contrib, earlier):
     joint, width = left.shape
-    count = projected.shape[2] // CW
+    depth = projected.shape[0]
+    count = pairs.shape[0]
+    coded = (joint // 2 + EXP_ROWS, CW)
+
+    def pick(step):
+        return lambda i, pairs_ref, odd_ref: (pairs_ref[step], 0, 0)
+
     return pl.pallas_call(
         functools.partial(update_body, count),
-        out_shape=[pltpu.HBM((joint // 2 + EXP_ROWS, CW), jnp.int16)] * (2 * count),
-        in_specs=[smem()] * 2 + [vmem()] * 3 + untouched(len(earlier)),
-        out_specs=[vmem()] * (2 * count),
+        out_shape=[pltpu.HBM(coded, jnp.int16)] * (2 * count),
+        grid_spec=pltpu.PrefetchScalarGridSpec(
+            num_scalar_prefetch=2,
+            grid=(1,),
+            in_specs=[
+                pl.BlockSpec((joint, width), lambda i, a, b: (0, 0)),
+                pl.BlockSpec((depth, 2 * RK, count * CW), lambda i, a, b: (0, 0, place)),
+            ]
+            + [pl.BlockSpec((1, joint, CW), pick(step)) for step in range(count)]
+            + untouched(len(earlier)),
+            out_specs=[pl.BlockSpec(coded, lambda i, a, b: (0, 0))] * (2 * count),
+        ),
         compiler_params=params(28),
         cost_estimate=cost(2 * joint * width * count * CW, 2 * count * CW * (width + 2 * joint)),
         name="update_group",
-    )(odd, pairs, left, projected, contrib, *earlier)
+    )(pairs, odd, left, projected, *([contrib] * count), *earlier)
 
 
 def scatter_body(count, has_partial, starts_ref, targets_ref, *refs):
@@ -476,8 +489,18 @@
     groups = groups_of(partners // 2)
     all_pairs = jnp.bitwise_xor(blk // 2, jnp.array(sum(groups, []), jnp.int32))
     pairs = [jnp.bitwise_xor(blk // 2, jnp.array(group, jnp.int32)) for group in groups]
-    offsets = [[2 * q + side for q in group for side in range(2)] for group in groups]
-    fronts = [jnp.bitwise_xor(blk, jnp.array(ks, jnp.int32)) for ks in offsets]
+    batches = [
+        [group[begin : begin + BATCH] for begin in range(0, len(group), BATCH)] for group in groups
+    ]
+    offsets = {
+        tuple(batch): [2 * q + side for q in batch for side in range(2)]
+        for group in batches
+        for batch in group
+    }
+    fronts = [
+        jnp.bitwise_xor(blk, jnp.array(sum((offsets[tuple(b)] for b in group), []), jnp.int32))
+        for group in batches
+    ]
     odd = (blk % 2).reshape(1)
     half = (owner % 2).reshape(1)
     second = ((owner + blk) % 2).reshape(1)
@@ -544,8 +567,11 @@
             solved.append(part)
             projected.append(over_owner(sent))
         earlier = [] if partial is None else [token]
-        coded = update_group(odd, pairs[index], left, projected[index], contrib, earlier)
-        arrived = exchange(coded, offsets[index])
+        arrived = []
+        for place, batch in enumerate(batches[index]):
+            chosen = jnp.bitwise_xor(blk // 2, jnp.array(batch, jnp.int32))
+            coded = update_group(odd, chosen, left, projected[index], place, contrib, earlier)
+            arrived += exchange(coded, offsets[tuple(batch)])
         dtype = jnp.float32 if index + 1 < count else jnp.bfloat16
         partial, token = scatter_rows(starts[index], spread[index][0], arrived, partial, dtype)
     parent_update = total_rows(over_owner(partial))

time: 244 us -> 233 us (0.955)
  waiting for transfers between devices: 101 us -> 87 us
    ppermute x15, waiting for transfers between devices: 37.1 us -> 20.6 us  [exchange(): lax.ppermute(v, 'blk', p)]
    ppermute x15, starting transfers between devices: 22.2 us -> 28.7 us  [exchange(): lax.ppermute(v, 'blk', p)]
    all_to_all x3, starting transfers between devices: 29.2 us -> 24.1 us  [over_owner(): lax.all_to_all(value, 'owner', split_axis=0, concat_axis=0, tiled=True)]
  transfers between devices with their start and end apart: 21 -> 21, of which waited for: 12 -> 11; matrix products, arithmetic and copies ran while one was open for 4% -> 4% of each run, Pallas kernels for 16% -> 17%
where the time goes in v3:
time: 233 us; the launch traced here: 232 us
  waiting for transfers between devices  87 us (37%)
  Pallas kernels  62.3 us (27%)
  starting transfers between devices  62.2 us (27%)
  local copies, waits for them, and re-layouts  11.7 us (5%)
  other arithmetic  7.42 us (3%)
    all_to_all x3, waiting for transfers between devices, over_owner(): lax.all_to_all(value, 'owner', split_axis=0, concat_axis=0, tiled=True)  59.3 us
    ppermute x15, starting transfers between devices, exchange(): lax.ppermute(v, 'blk', p)  28.7 us
    all_to_all x3, starting transfers between devices, over_owner(): lax.all_to_all(value, 'owner', split_axis=0, concat_axis=0, tiled=True)  24.1 us
    ppermute x15, waiting for transfers between devices, exchange(): lax.ppermute(v, 'blk', p)  20.6 us
    pallas_call x2, Pallas kernels, update_group(): pl.pallas_call(functools.partial(update_body, count), out_shape=[pltpu.HB...  12.8 us
    pallas_call x2, Pallas kernels, scatter_rows(): pl.pallas_call(functools.partial(scatter_body, count, has_partial), out_s...  11.8 us
    unnamed x44, local copies, waits for them, and re-layouts  10.2 us
    pallas_call x1, Pallas kernels, sort_rows(): pl.pallas_call(sort_body, out_shape=[pltpu.HBM((joint, 2 * width), jnp.bf...  9.2 us
  transfers between devices with their start and end apart: 21, of which 11 were waited for; matrix products, arithmetic and copies ran while one was open for 4% of the time, Pallas kernels for 17%

profile of v3, /device:TPU:16, one launch (start us, length us, event | category | flops | bytes accessed | tf_op | source)
XLA Modules:
  0.0 231.5 jit_solution(6861557950549813918)
XLA Ops:
  0.6 0.0 copy-start
  0.6 3.9 %mask_all.1 = (bf16[16,512,128]{2,1,0:T(8,128)(2,1)}, f32[8,128]{1,0:T(8,128)}) custom-call(s32[16]{0:T(128)} %bitcast.14, bf16[16,512,128]{2,1,0:T(8,128)(2,1)} %rhs_ref.1), custom_call_target="tpu_custom_call" | custom-call | flops 1048576 | bytes 4194304 | tf_op jit(solution)/shard_map/mask_all/pallas_call | solution.py:81
  4.6 7.3 %all-to-all-start = ((bf16[16,512,128]{2,1,0:T(8,128)(2,1)}), bf16[16,512,128]{2,1,0:T(8,128)(2,1)S(1)}, u32[]{:S(2)}, u32[]{:S(2)}) async-start(bf16[16,512,128]{2,1,0:T(8,128)(2,1)} %get-tuple-element.39), calls=%async_computation | async-start | bytes 4194304 | tf_op jit(solution)/shard_map/all_to_all | solution.py:528
  11.8 0.0 copy-start.18
  11.9 3.0 %pack_contrib.1 = (bf16[512,1024]{1,0:T(8,128)(2,1)}, bf16[512,1024]{1,0:T(8,128)(2,1)}) custom-call(s32[1]{0:T(128)} %bitcast.5.high_ref, bf16[512,2048]{1,0:T(8,128)(2,1)} %bitcast.13, f32[8,128]{1,0:T(8,128)} %get-tuple-element.41.after_ref), custom_call_target="tpu_custom_call" | custom-call | bytes 1048576 | tf_op jit(solution)/shard_map/pack_contrib/pallas_call | solution.py:225
  14.9 1.9 collective-permute-start.1
  16.8 0.1 collective-permute-start
  16.9 0.9 constant_dynamic-slice_fusion
  17.9 5.8 %sort.15 = (f32[16,1024]{1,0:T(8,128)S(1)}, s32[16,1024]{1,0:T(8,128)}) sort(f32[16,1024]{1,0:T(8,128)S(1)} %fusion, s32[16,1024]{1,0:T(8,128)S(1)} %iota.20), dimensions={1}, to_apply=%region_0.1 | sort | flops 229376 | bytes 262144 | tf_op jit(solution)/shard_map/jit(sort)/sort | solution.py:545
  23.7 0.6 gather_fusion.1
  24.3 0.1 broadcast_select_fusion
  24.4 3.0 %sorted_targets.3 = (f32[8,1024,128]{2,1,0:T(8,128)}, f32[8,128]{1,0:T(8,128)S(1)}) custom-call(f32[8,1,1024]{2,1,0:T(1,128)S(1)} %reshape.78.keys_ref, f32[8,128]{1,0:T(8,128)S(1)} %copy-done.10), custom_call_target="tpu_custom_call" | custom-call | bytes 1048576 | tf_op jit(solution)/shard_map/sorted_targets/pallas_call | solution.py:317
  27.4 0.6 gather_fusion
  28.0 0.1 broadcast_select_fusion.1
  28.1 3.1 %sorted_targets.2 = (f32[8,1024,128]{2,1,0:T(8,128)}, f32[8,128]{1,0:T(8,128)S(1)}) custom-call(f32[8,1,1024]{2,1,0:T(1,128)S(1)} %reshape.77.keys_ref, f32[8,128]{1,0:T(8,128)S(1)} %copy-done.10), custom_call_target="tpu_custom_call" | custom-call | bytes 1048576 | tf_op jit(solution)/shard_map/sorted_targets/pallas_call | solution.py:317
  31.2 0.2 dynamic-slice_reduce_fusion
  31.4 0.1 fusion.1
  31.5 0.1 reshape.81.keep_ref
  31.6 1.2 copy-done.9
  32.8 1.4 right_transposed.1.right_ref
  34.2 7.0 %collective-permute-done.refs_6_.other_ref = bf16[512,1024]{1,0:T(8,128)(2,1)} collective-permute-done((bf16[512,1024]{1,0:T(8,128)(2,1)}, bf16[512,1024]{1,0:T(8,128)(2,1)}, u32[]{:S(2)}, u32[]{:S(2)}) %collective-permute-start) | collective-permute-done | bytes 1048608 | tf_op jit(solution)/shard_map/ppermute | solution.py:529
  41.3 1.2 copy-done.4
  42.5 4.3 %solve_group.2 = (bf16[4,2,512,128]{3,2,1,0:T(8,128)(2,1)}, bf16[16,128,512]{2,1,0:T(8,128)(2,1)}, f32[8,128]{1,0:T(8,128)}) custom-call(s32[4]{0:T(128)S(1)} %broadcast_xor_fusion.1.pairs_ref, s32[1]{0:T(128)} %bitcast.odd_ref, bf16[512,512]{1,0:T(8,128)(2,1)S(1)} %bitcast.8, bf16[1024,512]{1,0:T(8,128)(2,1)S(1)} %copy-done.4, ...), custom_call_target="tpu_custom_call" | custom-call | flops 1610612736 | bytes 4194304 | tf_op jit(solution)/shard_map/solve_group/pallas_call | solution.py:150
  46.8 9.5 %all-to-all-start.2 = ((bf16[16,128,512]{2,1,0:T(8,128)(2,1)}), bf16[16,128,512]{2,1,0:T(8,128)(2,1)}, u32[]{:S(2)}, u32[]{:S(2)}) async-start(bf16[16,128,512]{2,1,0:T(8,128)(2,1)} %get-tuple-element.54), calls=%async_computation.2 | async-start | bytes 4194304 | tf_op jit(solution)/shard_map/all_to_all | solution.py:524
  56.4 1.2 copy-done.13
  57.6 1.2 copy-done.14
  58.8 9.2 %sort_rows.1 = (bf16[1024,2048]{1,0:T(8,128)(2,1)}, bf16[8,1024,128]{2,1,0:T(8,128)(2,1)}, f32[8,128]{1,0:T(8,128)S(1)}) custom-call(s32[1]{0:T(128)} %bitcast.7.high_ref, f32[1,1024]{1,0:T(1,128)S(1)} %fusion.3.keys_ref, bf16[512,1024]{1,0:T(8,128)(2,1)S(1)} %bitcast.12, bf16[512,1024]{1,0:T(8,128)(2,1)} %collective-permute-done.refs_6_.other_ref, ...), custom_call_target="tpu_custom_call" | custom-call | flops 4294967296 | bytes 8388608 | tf_op jit(solution)/shard_map/sort_rows/pallas_call | solution.py:279
  68.0 4.3 %solve_group.3 = (bf16[4,2,512,128]{3,2,1,0:T(8,128)(2,1)}, bf16[16,128,512]{2,1,0:T(8,128)(2,1)}, f32[8,128]{1,0:T(8,128)}) custom-call(s32[4]{0:T(128)S(1)} %broadcast_xor_fusion.pairs_ref, s32[1]{0:T(128)} %bitcast.odd_ref, bf16[512,512]{1,0:T(8,128)(2,1)S(1)} %bitcast.9, bf16[1024,512]{1,0:T(8,128)(2,1)S(1)} %copy-done.5, ...), custom_call_target="tpu_custom_call" | custom-call | flops 1610612736 | bytes 4194304 | tf_op jit(solution)/shard_map/solve_group/pallas_call | solution.py:150
  72.3 33.3 %all-to-all-done.2.projected_ref = bf16[16,128,512]{2,1,0:T(8,128)(2,1)} async-done(((bf16[16,128,512]{2,1,0:T(8,128)(2,1)}), bf16[16,128,512]{2,1,0:T(8,128)(2,1)}, u32[]{:S(2)}, u32[]{:S(2)}) %all-to-all-start.2) | async-done | bytes 2097184 | tf_op jit(solution)/shard_map/all_to_all | solution.py:524
  105.7 6.1 %all-to-all-start.1 = ((bf16[16,128,512]{2,1,0:T(8,128)(2,1)}), bf16[16,128,512]{2,1,0:T(8,128)(2,1)}, u32[]{:S(2)}, u32[]{:S(2)}) async-start(bf16[16,128,512]{2,1,0:T(8,128)(2,1)} %get-tuple-element.51), calls=%async_computation.1 | async-start | bytes 4194304 | tf_op jit(solution)/shard_map/all_to_all | solution.py:524
  111.8 2.2 copy-done.2
  114.0 6.4 %update_group.2 = (s16[528,128]{1,0:T(8,128)(2,1)}, s16[528,128]{1,0:T(8,128)(2,1)}, s16[528,128]{1,0:T(8,128)(2,1)}, s16[528,128]{1,0:T(8,128)(2,1)}, s16[528,1...) custom-call(s32[4]{0:T(128)S(1)} %broadcast_xor_fusion.1.pairs_ref, ...), custom_call_target="tpu_custom_call" | custom-call | flops 2147483648 | bytes 4194304 | tf_op jit(solution)/shard_map/update_group/pallas_call | solution.py:361
  120.4 0.8 collective-permute-start.2
  121.2 1.8 collective-permute-start.3
  123.0 1.8 collective-permute-start.4
  124.8 3.0 %collective-permute-start.5 = (s16[528,128]{1,0:T(8,128)(2,1)}, s16[528,128]{1,0:T(8,128)(2,1)S(1)}, u32[]{:S(2)}, u32[]{:S(2)}) collective-permute-start(s16[528,128]{1,0:T(8,128)(2,1)} %get-tuple-element.58), channel_id=1, source_target_pairs={{0,11},{1,10},{2,9},{3,8},{4,15},{5,14},{6,13},{7,12},{8,3},{9,2},... | collective-permute-start | bytes 405512 | tf_op jit(solution)/shard_map/ppermute | solution.py:521
  127.8 3.0 %collective-permute-start.6 = (s16[528,128]{1,0:T(8,128)(2,1)}, s16[528,128]{1,0:T(8,128)(2,1)S(1)}, u32[]{:S(2)}, u32[]{:S(2)}) collective-permute-start(s16[528,128]{1,0:T(8,128)(2,1)} %get-tuple-element.59), channel_id=1, source_target_pairs={{0,4},{1,5},{2,6},{3,7},{4,0},{5,1},{6,2},{7,3},{8,12},{9,13},{10,... | collective-permute-start | bytes 405512 | tf_op jit(solution)/shard_map/ppermute | solution.py:521
  130.7 8.6 %collective-permute-done.2.refs_0_ = s16[528,128]{1,0:T(8,128)(2,1)S(1)} collective-permute-done((s16[528,128]{1,0:T(8,128)(2,1)}, s16[528,128]{1,0:T(8,128)(2,1)S(1)}, u32[]{:S(2)}, u32[]{:S(2)}) %collective-permute-start.2) | collective-permute-done | bytes 135200 | tf_op jit(solution)/shard_map/ppermute | solution.py:521
  139.3 2.5 %collective-permute-done.3.refs_1_ = s16[528,128]{1,0:T(8,128)(2,1)S(1)} collective-permute-done((s16[528,128]{1,0:T(8,128)(2,1)}, s16[528,128]{1,0:T(8,128)(2,1)S(1)}, u32[]{:S(2)}, u32[]{:S(2)}) %collective-permute-start.3) | collective-permute-done | bytes 135200 | tf_op jit(solution)/shard_map/ppermute | solution.py:521
  141.9 2.7 %collective-permute-start.8 = (s16[528,128]{1,0:T(8,128)(2,1)}, s16[528,128]{1,0:T(8,128)(2,1)S(1)}, u32[]{:S(2)}, u32[]{:S(2)}) collective-permute-start(s16[528,128]{1,0:T(8,128)(2,1)} %get-tuple-element.61), channel_id=1, source_target_pairs={{0,6},{1,7},{2,4},{3,5},{4,2},{5,3},{6,0},{7,1},{8,14},{9,15},{10,... | collective-permute-start | bytes 405512 | tf_op jit(solution)/shard_map/ppermute | solution.py:521
  144.6 3.1 %collective-permute-start.9 = (s16[528,128]{1,0:T(8,128)(2,1)}, s16[528,128]{1,0:T(8,128)(2,1)S(1)}, u32[]{:S(2)}, u32[]{:S(2)}) collective-permute-start(s16[528,128]{1,0:T(8,128)(2,1)} %get-tuple-element.62), channel_id=1, source_target_pairs={{0,7},{1,6},{2,5},{3,4},{4,3},{5,2},{6,1},{7,0},{8,15},{9,14},{10,... | collective-permute-start | bytes 405512 | tf_op jit(solution)/shard_map/ppermute | solution.py:521
  147.7 0.4 convert_reduce_fusion
  148.2 0.1 collective-permute-done.8.refs_6_
  148.3 4.0 %collective-permute-done.9.refs_7_ = s16[528,128]{1,0:T(8,128)(2,1)S(1)} collective-permute-done((s16[528,128]{1,0:T(8,128)(2,1)}, s16[528,128]{1,0:T(8,128)(2,1)S(1)}, u32[]{:S(2)}, u32[]{:S(2)}) %collective-permute-start.9) | collective-permute-done | bytes 135200 | tf_op jit(solution)/shard_map/ppermute | solution.py:521
  152.3 5.9 %scatter_rows.2 = (f32[16,64,512]{2,1,0:T(8,128)}, f32[8,128]{1,0:T(8,128)S(1)}) custom-call(s32[8,16]{1,0:T(8,128)S(1)} %get-tuple-element.74.starts_ref, f32[8,1024,128]{2,1,0:T(8,128)S(1)} %copy-done.12, s16[528,128]{1,0:T(8,128)(2,1)S(1)} %collective-permute-done.2.refs_0_, s16[528,128]{1,0:T(8,128)(2,1)S(1)} %collective-permute-done.3.refs_1_, ...), custom_call_target="tpu_custom_call" | custom-call | flops 2415919104 | bytes 4194304 | tf_op jit(solution)/shard_map/scatter_rows/pallas_call | solution.py:436
  158.3 2.3 all-to-all-done.1.projected_ref
  160.6 2.2 copy-done.3
  162.8 6.4 %update_group.3 = (s16[528,128]{1,0:T(8,128)(2,1)}, s16[528,128]{1,0:T(8,128)(2,1)}, s16[528,128]{1,0:T(8,128)(2,1)}, s16[528,128]{1,0:T(8,128)(2,1)}, s16[528,1...) custom-call(s32[4]{0:T(128)S(1)} %broadcast_xor_fusion.pairs_ref, ...), custom_call_target="tpu_custom_call" | custom-call | flops 2147483648 | bytes 4194304 | tf_op jit(solution)/shard_map/update_group/pallas_call | solution.py:361
  169.2 2.7 %collective-permute-start.10 = (s16[528,128]{1,0:T(8,128)(2,1)}, s16[528,128]{1,0:T(8,128)(2,1)S(1)}, u32[]{:S(2)}, u32[]{:S(2)}) collective-permute-start(s16[528,128]{1,0:T(8,128)(2,1)} %get-tuple-element.64), channel_id=1, source_target_pairs={{0,12},{1,13},{2,14},{3,15},{4,8},{5,9},{6,10},{7,11},{8,4},{9,5},... | collective-permute-start | bytes 405512 | tf_op jit(solution)/shard_map/ppermute | solution.py:521
  171.8 1.7 collective-permute-start.11
  173.5 2.2 collective-permute-start.12
  175.6 4.5 %collective-permute-start.13 = (s16[528,128]{1,0:T(8,128)(2,1)}, s16[528,128]{1,0:T(8,128)(2,1)S(1)}, u32[]{:S(2)}, u32[]{:S(2)}) collective-permute-start(s16[528,128]{1,0:T(8,128)(2,1)} %get-tuple-element.67), channel_id=1, source_target_pairs={{0,15},{1,14},{2,13},{3,12},{4,11},{5,10},{6,9},{7,8},{8,7},{9,6},... | collective-permute-start | bytes 405512 | tf_op jit(solution)/shard_map/ppermute | solution.py:521
  180.2 0.2 collective-permute-start.14
  180.4 0.2 collective-permute-start.15
  180.6 0.6 collective-permute-done.11.refs_1_
  181.2 1.1 collective-permute-start.16
  182.3 1.4 collective-permute-done.12.refs_2_
  183.7 3.3 %collective-permute-done.13.refs_3_ = s16[528,128]{1,0:T(8,128)(2,1)S(1)} collective-permute-done((s16[528,128]{1,0:T(8,128)(2,1)}, s16[528,128]{1,0:T(8,128)(2,1)S(1)}, u32[]{:S(2)}, u32[]{:S(2)}) %collective-permute-start.13) | collective-permute-done | bytes 135200 | tf_op jit(solution)/shard_map/ppermute | solution.py:521
  187.0 0.9 copy-done.15
  187.9 5.9 %scatter_rows.3 = (bf16[16,64,512]{2,1,0:T(8,128)(2,1)}, f32[8,128]{1,0:T(8,128)}) custom-call(s32[8,16]{1,0:T(8,128)S(1)} %get-tuple-element.75.starts_ref, f32[8,1024,128]{2,1,0:T(8,128)S(1)} %copy-done.11, s16[528,128]{1,0:T(8,128)(2,1)S(1)} %collective-permute-done.10.refs_0_, s16[528,128]{1,0:T(8,128)(2,1)S(1)} %collective-permute-done.11.refs_1_, ...), custom_call_target="tpu_custom_call" | custom-call | flops 2415919104 | bytes 4194304 | tf_op jit(solution)/shard_map/scatter_rows/pallas_call | solution.py:436
  193.8 8.6 %all-to-all-start.3 = ((bf16[16,64,512]{2,1,0:T(8,128)(2,1)}), bf16[16,64,512]{2,1,0:T(8,128)(2,1)S(1)}, u32[]{:S(2)}, u32[]{:S(2)}) async-start(bf16[16,64,512]{2,1,0:T(8,128)(2,1)} %get-tuple-element.73), calls=%async_computation.3 | async-start | bytes 2097152 | tf_op jit(solution)/shard_map/all_to_all | solution.py:524
  202.4 3.7 %place_blocks.1 = bf16[1,512,2048]{2,1,0:T(8,128)(2,1)} custom-call(s32[8]{0:T(128)S(1)} %broadcast_xor_fusion.2.pairs_ref, bf16[4,2,512,128]{3,2,1,0:T(8,128)(2,1)S(1)} %copy-done.7, bf16[4,2,512,128]{3,2,1,0:T(8,128)(2,1)S(1)} %copy-done.8), custom_call_target="tpu_custom_call" | custom-call | bytes 4194304 | tf_op jit(solution)/shard_map/place_blocks/pallas_call | solution.py:195
  206.1 23.7 %all-to-all-done.3.parts_ref = bf16[16,64,512]{2,1,0:T(8,128)(2,1)S(1)} async-done(((bf16[16,64,512]{2,1,0:T(8,128)(2,1)}), bf16[16,64,512]{2,1,0:T(8,128)(2,1)S(1)}, u32[]{:S(2)}, u32[]{:S(2)}) %all-to-all-start.3) | async-done | bytes 1048608 | tf_op jit(solution)/shard_map/all_to_all | solution.py:524
  229.8 1.7 total_rows.1
  (59 shorter events, 0.2 us)
Async XLA Ops:
  0.6 30.6 %copy-start = (s32[1,16,16]{2,1,0:T(8,128)S(1)}, s32[1,16,16]{2,1,0:T(8,128)}, u32[]{:S(2)}) copy-start(s32[1,16,16]{2,1,0:T(8,128)} %param.22) | copy-start | bytes 3076
  4.6 36.7 %all-to-all-start = ((bf16[16,512,128]{2,1,0:T(8,128)(2,1)}), bf16[16,512,128]{2,1,0:T(8,128)(2,1)S(1)}, u32[]{:S(2)}, u32[]{:S(2)}) async-start(bf16[16,512,128]{2,1,0:T(8,128)(2,1)} %get-tuple-element.39), calls=%async_computation | async-start | bytes 4194304 | tf_op jit(solution)/shard_map/all_to_all | solution.py:528
  11.8 6.0 %copy-start.17 = (s32[8]{0:T(128)S(1)}, s32[8]{0:T(128)}, u32[]{:S(2)}) copy-start(s32[8]{0:T(128)} %constant.142.clone) | copy-start | bytes 100
  11.8 6.0 %copy-start.18 = (s32[8]{0:T(128)S(1)}, s32[8]{0:T(128)}, u32[]{:S(2)}) copy-start(s32[8]{0:T(128)} %constant.143.clone) | copy-start | bytes 100
  11.9 12.5 %copy-start.10 = (f32[8,128]{1,0:T(8,128)S(1)}, f32[8,128]{1,0:T(8,128)}, u32[]{:S(2)}) copy-start(f32[8,128]{1,0:T(8,128)} %get-tuple-element.41.after_ref) | copy-start | bytes 12292
  14.9 19.3 %copy-start.21 = (s32[4]{0:T(128)S(1)}, s32[4]{0:T(128)}, u32[]{:S(2)}) copy-start(s32[4]{0:T(128)} %constant.140.clone) | copy-start | bytes 52
  14.9 26.4 %copy-start.6 = (bf16[1,512,512]{2,1,0:T(8,128)(2,1)S(1)}, bf16[1,512,512]{2,1,0:T(8,128)(2,1)}, u32[]{:S(2)}) copy-start(bf16[1,512,512]{2,1,0:T(8,128)(2,1)} %param.19) | copy-start | bytes 1572868
  14.9 19.3 %collective-permute-start.1 = (bf16[512,1024]{1,0:T(8,128)(2,1)}, bf16[512,1024]{1,0:T(8,128)(2,1)}, u32[]{:S(2)}, u32[]{:S(2)}) collective-permute-start(bf16[512,1024]{1,0:T(8,128)(2,1)} %get-tuple-element.44), channel_id=1, source_target_pairs={{0,16},{1,113},{2,18},{3,115},{4,20},{5,117},{6,22},{7,119},{8,24}... | collective-permute-start | bytes 3145736 | tf_op jit(solution)/shard_map/ppermute | solution.py:531
  16.8 24.4 %collective-permute-start = (bf16[512,1024]{1,0:T(8,128)(2,1)}, bf16[512,1024]{1,0:T(8,128)(2,1)}, u32[]{:S(2)}, u32[]{:S(2)}) collective-permute-start(bf16[512,1024]{1,0:T(8,128)(2,1)} %bitcast.11), channel_id=1, source_target_pairs={{0,16},{1,113},{2,18},{3,115},{4,20},{5,117},{6,22},{7,119},{8,24}... | collective-permute-start | bytes 3145736 | tf_op jit(solution)/shard_map/ppermute | solution.py:529
  31.6 1.2 copy-start.9
  41.3 1.2 copy-start.4
  46.8 9.5 %copy-start.20 = (s32[4]{0:T(128)S(1)}, s32[4]{0:T(128)}, u32[]{:S(2)}) copy-start(s32[4]{0:T(128)} %constant.141.clone) | copy-start | bytes 52
  46.8 58.8 %all-to-all-start.2 = ((bf16[16,128,512]{2,1,0:T(8,128)(2,1)}), bf16[16,128,512]{2,1,0:T(8,128)(2,1)}, u32[]{:S(2)}, u32[]{:S(2)}) async-start(bf16[16,128,512]{2,1,0:T(8,128)(2,1)} %get-tuple-element.54), calls=%async_computation.2 | async-start | bytes 4194304 | tf_op jit(solution)/shard_map/all_to_all | solution.py:524
  56.4 1.2 copy-start.13
  57.6 1.2 copy-start.14
  58.8 9.2 %copy-start.5 = (bf16[1024,512]{1,0:T(8,128)(2,1)S(1)}, bf16[1024,512]{1,0:T(8,128)(2,1)}, u32[]{:S(2)}) copy-start(bf16[1024,512]{1,0:T(8,128)(2,1)} %right_transposed.1.right_ref) | copy-start | bytes 3145732
  105.7 6.1 %copy-start.1 = (bf16[8,1024,128]{2,1,0:T(8,128)(2,1)S(1)}, bf16[8,1024,128]{2,1,0:T(8,128)(2,1)}, u32[]{:S(2)}) copy-start(bf16[8,1024,128]{2,1,0:T(8,128)(2,1)} %get-tuple-element.52.refs_0_.refs_1_.refs_2_.refs_3_) | copy-start | bytes 6291460
  105.7 54.9 %all-to-all-start.1 = ((bf16[16,128,512]{2,1,0:T(8,128)(2,1)}), bf16[16,128,512]{2,1,0:T(8,128)(2,1)}, u32[]{:S(2)}, u32[]{:S(2)}) async-start(bf16[16,128,512]{2,1,0:T(8,128)(2,1)} %get-tuple-element.51), calls=%async_computation.1 | async-start | bytes 4194304 | tf_op jit(solution)/shard_map/all_to_all | solution.py:524
  111.8 2.2 copy-start.2
  114.0 38.4 %copy-start.12 = (f32[8,1024,128]{2,1,0:T(8,128)S(1)}, f32[8,1024,128]{2,1,0:T(8,128)}, u32[]{:S(2)}) copy-start(f32[8,1024,128]{2,1,0:T(8,128)} %get-tuple-element.53.targets_ref) | copy-start | bytes 12582916
  120.4 19.0 %collective-permute-start.2 = (s16[528,128]{1,0:T(8,128)(2,1)}, s16[528,128]{1,0:T(8,128)(2,1)S(1)}, u32[]{:S(2)}, u32[]{:S(2)}) collective-permute-start(s16[528,128]{1,0:T(8,128)(2,1)} %get-tuple-element.55), channel_id=1, source_target_pairs={{0,8},{1,9},{2,10},{3,11},{4,12},{5,13},{6,14},{7,15},{8,0},{9,1},... | collective-permute-start | bytes 405512 | tf_op jit(solution)/shard_map/ppermute | solution.py:521
  121.2 20.7 %collective-permute-start.3 = (s16[528,128]{1,0:T(8,128)(2,1)}, s16[528,128]{1,0:T(8,128)(2,1)S(1)}, u32[]{:S(2)}, u32[]{:S(2)}) collective-permute-start(s16[528,128]{1,0:T(8,128)(2,1)} %get-tuple-element.56), channel_id=1, source_target_pairs={{0,9},{1,8},{2,11},{3,10},{4,13},{5,12},{6,15},{7,14},{8,1},{9,0},... | collective-permute-start | bytes 405512 | tf_op jit(solution)/shard_map/ppermute | solution.py:521
  123.0 21.6 %collective-permute-start.4 = (s16[528,128]{1,0:T(8,128)(2,1)}, s16[528,128]{1,0:T(8,128)(2,1)S(1)}, u32[]{:S(2)}, u32[]{:S(2)}) collective-permute-start(s16[528,128]{1,0:T(8,128)(2,1)} %get-tuple-element.57), channel_id=1, source_target_pairs={{0,10},{1,11},{2,8},{3,9},{4,14},{5,15},{6,12},{7,13},{8,2},{9,3},... | collective-permute-start | bytes 405512 | tf_op jit(solution)/shard_map/ppermute | solution.py:521
  124.8 23.3 %collective-permute-start.5 = (s16[528,128]{1,0:T(8,128)(2,1)}, s16[528,128]{1,0:T(8,128)(2,1)S(1)}, u32[]{:S(2)}, u32[]{:S(2)}) collective-permute-start(s16[528,128]{1,0:T(8,128)(2,1)} %get-tuple-element.58), channel_id=1, source_target_pairs={{0,11},{1,10},{2,9},{3,8},{4,15},{5,14},{6,13},{7,12},{8,3},{9,2},... | collective-permute-start | bytes 405512 | tf_op jit(solution)/shard_map/ppermute | solution.py:521
  127.8 20.4 %collective-permute-start.6 = (s16[528,128]{1,0:T(8,128)(2,1)}, s16[528,128]{1,0:T(8,128)(2,1)S(1)}, u32[]{:S(2)}, u32[]{:S(2)}) collective-permute-start(s16[528,128]{1,0:T(8,128)(2,1)} %get-tuple-element.59), channel_id=1, source_target_pairs={{0,4},{1,5},{2,6},{3,7},{4,0},{5,1},{6,2},{7,3},{8,12},{9,13},{10,... | collective-permute-start | bytes 405512 | tf_op jit(solution)/shard_map/ppermute | solution.py:521
  139.3 8.8 %collective-permute-start.7 = (s16[528,128]{1,0:T(8,128)(2,1)}, s16[528,128]{1,0:T(8,128)(2,1)S(1)}, u32[]{:S(2)}, u32[]{:S(2)}) collective-permute-start(s16[528,128]{1,0:T(8,128)(2,1)} %get-tuple-element.60), channel_id=1, source_target_pairs={{0,5},{1,4},{2,7},{3,6},{4,1},{5,0},{6,3},{7,2},{8,13},{9,12},{10,... | collective-permute-start | bytes 405512 | tf_op jit(solution)/shard_map/ppermute | solution.py:521
  141.9 6.4 %collective-permute-start.8 = (s16[528,128]{1,0:T(8,128)(2,1)}, s16[528,128]{1,0:T(8,128)(2,1)S(1)}, u32[]{:S(2)}, u32[]{:S(2)}) collective-permute-start(s16[528,128]{1,0:T(8,128)(2,1)} %get-tuple-element.61), channel_id=1, source_target_pairs={{0,6},{1,7},{2,4},{3,5},{4,2},{5,3},{6,0},{7,1},{8,14},{9,15},{10,... | collective-permute-start | bytes 405512 | tf_op jit(solution)/shard_map/ppermute | solution.py:521
  144.6 7.8 %collective-permute-start.9 = (s16[528,128]{1,0:T(8,128)(2,1)}, s16[528,128]{1,0:T(8,128)(2,1)S(1)}, u32[]{:S(2)}, u32[]{:S(2)}) collective-permute-start(s16[528,128]{1,0:T(8,128)(2,1)} %get-tuple-element.62), channel_id=1, source_target_pairs={{0,7},{1,6},{2,5},{3,4},{4,3},{5,2},{6,1},{7,0},{8,15},{9,14},{10,... | collective-permute-start | bytes 405512 | tf_op jit(solution)/shard_map/ppermute | solution.py:521
  160.6 2.2 copy-start.3
  162.8 24.2 %copy-start.11 = (f32[8,1024,128]{2,1,0:T(8,128)S(1)}, f32[8,1024,128]{2,1,0:T(8,128)}, u32[]{:S(2)}) copy-start(f32[8,1024,128]{2,1,0:T(8,128)} %get-tuple-element.49.targets_ref) | copy-start | bytes 12582916
  162.8 24.2 %copy-start.16 = (f32[16,64,512]{2,1,0:T(8,128)S(1)}, f32[16,64,512]{2,1,0:T(8,128)}, u32[]{:S(2)}) copy-start(f32[16,64,512]{2,1,0:T(8,128)} %get-tuple-element.72.refs_8_) | copy-start | bytes 6291460
  169.2 11.2 %collective-permute-start.10 = (s16[528,128]{1,0:T(8,128)(2,1)}, s16[528,128]{1,0:T(8,128)(2,1)S(1)}, u32[]{:S(2)}, u32[]{:S(2)}) collective-permute-start(s16[528,128]{1,0:T(8,128)(2,1)} %get-tuple-element.64), channel_id=1, source_target_pairs={{0,12},{1,13},{2,14},{3,15},{4,8},{5,9},{6,10},{7,11},{8,4},{9,5},... | collective-permute-start | bytes 405512 | tf_op jit(solution)/shard_map/ppermute | solution.py:521
  171.8 9.4 %collective-permute-start.11 = (s16[528,128]{1,0:T(8,128)(2,1)}, s16[528,128]{1,0:T(8,128)(2,1)S(1)}, u32[]{:S(2)}, u32[]{:S(2)}) collective-permute-start(s16[528,128]{1,0:T(8,128)(2,1)} %get-tuple-element.65), channel_id=1, source_target_pairs={{0,13},{1,12},{2,15},{3,14},{4,9},{5,8},{6,11},{7,10},{8,5},{9,4},... | collective-permute-start | bytes 405512 | tf_op jit(solution)/shard_map/ppermute | solution.py:521
  173.5 10.2 %collective-permute-start.12 = (s16[528,128]{1,0:T(8,128)(2,1)}, s16[528,128]{1,0:T(8,128)(2,1)S(1)}, u32[]{:S(2)}, u32[]{:S(2)}) collective-permute-start(s16[528,128]{1,0:T(8,128)(2,1)} %get-tuple-element.66), channel_id=1, source_target_pairs={{0,14},{1,15},{2,12},{3,13},{4,10},{5,11},{6,8},{7,9},{8,6},{9,7},... | collective-permute-start | bytes 405512 | tf_op jit(solution)/shard_map/ppermute | solution.py:521
  175.6 11.3 %collective-permute-start.13 = (s16[528,128]{1,0:T(8,128)(2,1)}, s16[528,128]{1,0:T(8,128)(2,1)S(1)}, u32[]{:S(2)}, u32[]{:S(2)}) collective-permute-start(s16[528,128]{1,0:T(8,128)(2,1)} %get-tuple-element.67), channel_id=1, source_target_pairs={{0,15},{1,14},{2,13},{3,12},{4,11},{5,10},{6,9},{7,8},{8,7},{9,6},... | collective-permute-start | bytes 405512 | tf_op jit(solution)/shard_map/ppermute | solution.py:521
  180.2 6.8 %collective-permute-start.14 = (s16[528,128]{1,0:T(8,128)(2,1)}, s16[528,128]{1,0:T(8,128)(2,1)S(1)}, u32[]{:S(2)}, u32[]{:S(2)}) collective-permute-start(s16[528,128]{1,0:T(8,128)(2,1)} %get-tuple-element.68), channel_id=1, source_target_pairs={{0,2},{1,3},{2,0},{3,1},{4,6},{5,7},{6,4},{7,5},{8,10},{9,11},{10,... | collective-permute-start | bytes 405512 | tf_op jit(solution)/shard_map/ppermute | solution.py:521
  180.4 6.6 %collective-permute-start.15 = (s16[528,128]{1,0:T(8,128)(2,1)}, s16[528,128]{1,0:T(8,128)(2,1)S(1)}, u32[]{:S(2)}, u32[]{:S(2)}) collective-permute-start(s16[528,128]{1,0:T(8,128)(2,1)} %get-tuple-element.69), channel_id=1, source_target_pairs={{0,3},{1,2},{2,1},{3,0},{4,7},{5,6},{6,5},{7,4},{8,11},{9,10},{10,... | collective-permute-start | bytes 405512 | tf_op jit(solution)/shard_map/ppermute | solution.py:521
  181.2 5.8 %collective-permute-start.16 = (s16[528,128]{1,0:T(8,128)(2,1)}, s16[528,128]{1,0:T(8,128)(2,1)S(1)}, u32[]{:S(2)}, u32[]{:S(2)}) collective-permute-start(s16[528,128]{1,0:T(8,128)(2,1)} %get-tuple-element.71), channel_id=1, source_target_pairs={{0,1},{1,0},{2,3},{3,2},{4,5},{5,4},{6,7},{7,6},{8,9},{9,8},{10,11... | collective-permute-start | bytes 405512 | tf_op jit(solution)/shard_map/ppermute | solution.py:521
  187.0 0.9 copy-start.15
  193.8 8.6 %copy-start.19 = (s32[8]{0:T(128)S(1)}, s32[8]{0:T(128)}, u32[]{:S(2)}) copy-start(s32[8]{0:T(128)} %constant.139.clone) | copy-start | bytes 100
  193.8 8.6 %copy-start.7 = (bf16[4,2,512,128]{3,2,1,0:T(8,128)(2,1)S(1)}, bf16[4,2,512,128]{3,2,1,0:T(8,128)(2,1)}, u32[]{:S(2)}) copy-start(bf16[4,2,512,128]{3,2,1,0:T(8,128)(2,1)} %get-tuple-element.45.refs_0_) | copy-start | bytes 3145732
  193.8 8.6 %copy-start.8 = (bf16[4,2,512,128]{3,2,1,0:T(8,128)(2,1)S(1)}, bf16[4,2,512,128]{3,2,1,0:T(8,128)(2,1)}, u32[]{:S(2)}) copy-start(bf16[4,2,512,128]{3,2,1,0:T(8,128)(2,1)} %get-tuple-element.48.refs_1_) | copy-start | bytes 3145732
  193.8 36.0 %all-to-all-start.3 = ((bf16[16,64,512]{2,1,0:T(8,128)(2,1)}), bf16[16,64,512]{2,1,0:T(8,128)(2,1)S(1)}, u32[]{:S(2)}, u32[]{:S(2)}) async-start(bf16[16,64,512]{2,1,0:T(8,128)(2,1)} %get-tuple-element.73), calls=%async_computation.3 | async-start | bytes 2097152 | tf_op jit(solution)/shard_map/all_to_all | solution.py:524

commit v4 on v3

--- a/solution.py
+++ b/solution.py
@@ -14,7 +14,7 @@
 EXP_ROWS = 16
 RING = 8
 BATCH = 4
-TILE_BATCH = 4
+TILE_BATCH = 8
 CODE_BITS = 14
 MIB = 1024 * 1024
 
@@ -53,7 +53,7 @@
 
 def groups_of(count):
     if count == 8:
-        return [[4, 5, 2, 3], [6, 7, 1, 0]]
+        return [[4, 6, 2, 3], [5, 7, 1, 0]]
     return [list(range(count // 2, count)), list(range(count // 2))]
 
 
@@ -340,13 +340,16 @@
     out_refs = refs[-2 * count :]
     joint, width = left_ref.shape
     rows = joint // 2
-    part = projected_ref[...].reshape(width, count * CW)
-    product = jnp.dot(left_ref[...], part, preferred_element_type=jnp.float32)
-    for step in range(count):
-        reduced = contribs[step][0].astype(jnp.float32) - product[:, step * CW : (step + 1) * CW]
-        sides = swapped(odd_ref[0] > 0, *halves(reduced[:rows], reduced[rows:]))
-        coded_rows(sides[0], out_refs[2 * step])
-        coded_rows(sides[1], out_refs[2 * step + 1])
+    for start in range(0, count, 2):
+        span = min(2, count - start)
+        part = projected_ref[:, :, start * CW : (start + span) * CW].reshape(width, span * CW)
+        product = jnp.dot(left_ref[...], part, preferred_element_type=jnp.float32)
+        for step in range(start, start + span):
+            reduced = contribs[step][0].astype(jnp.float32)
+            reduced = reduced - product[:, (step - start) * CW : (step - start + 1) * CW]
+            sides = swapped(odd_ref[0] > 0, *halves(reduced[:rows], reduced[rows:]))
+            coded_rows(sides[0], out_refs[2 * step])
+            coded_rows(sides[1], out_refs[2 * step + 1])
 
 
 def update_group(odd, pairs, left, projected, place, contrib, earlier):

time: 233 us -> 230 us (0.987)
  waiting for transfers between devices: 87 us -> 76.3 us
  starting transfers between devices: 62.2 us -> 71.1 us
    ppermute x15, waiting for transfers between devices: 20.6 us -> 8.89 us  [exchange(): lax.ppermute(v, 'blk', p)]
    ppermute x15, starting transfers between devices: 28.7 us -> 38.9 us  [exchange(): lax.ppermute(v, 'blk', p)]
  transfers between devices with their start and end apart: 21 -> 21, of which waited for: 11 -> 7; matrix products, arithmetic and copies ran while one was open for 4% -> 4% of each run, Pallas kernels for 17% -> 17%
where the time goes in v4:
time: 230 us; the launch traced here: 229 us
  waiting for transfers between devices  76.3 us (33%)
  starting transfers between devices  71.1 us (31%)
  Pallas kernels  61.6 us (27%)
  local copies, waits for them, and re-layouts  11.7 us (5%)
  other arithmetic  7.42 us (3%)
    all_to_all x3, waiting for transfers between devices, over_owner(): lax.all_to_all(value, 'owner', split_axis=0, concat_axis=0, tiled=True)  60.4 us
    ppermute x15, starting transfers between devices, exchange(): lax.ppermute(v, 'blk', p)  38.9 us
    all_to_all x3, starting transfers between devices, over_owner(): lax.all_to_all(value, 'owner', split_axis=0, concat_axis=0, tiled=True)  22.8 us
    pallas_call x2, Pallas kernels, update_group(): pl.pallas_call(functools.partial(update_body, count), out_shape=[pltpu.HB...  12.8 us
    pallas_call x2, Pallas kernels, scatter_rows(): pl.pallas_call(functools.partial(scatter_body, count, has_partial), out_s...  11.1 us
    unnamed x44, local copies, waits for them, and re-layouts  10.2 us
    pallas_call x1, Pallas kernels, sort_rows(): pl.pallas_call(sort_body, out_shape=[pltpu.HBM((joint, 2 * width), jnp.bf...  9.2 us
    ppermute x15, waiting for transfers between devices, exchange(): lax.ppermute(v, 'blk', p)  8.89 us
  transfers between devices with their start and end apart: 21, of which 7 were waited for; matrix products, arithmetic and copies ran while one was open for 4% of the time, Pallas kernels for 17%

profile of v4, /device:TPU:16, one launch (start us, length us, event | category | flops | bytes accessed | tf_op | source)
XLA Modules:
  0.0 229.1 jit_solution(11410722222986737041)
XLA Ops:
  0.6 0.0 copy-start
  0.6 3.9 %mask_all.1 = (bf16[16,512,128]{2,1,0:T(8,128)(2,1)}, f32[8,128]{1,0:T(8,128)}) custom-call(s32[16]{0:T(128)} %bitcast.14, bf16[16,512,128]{2,1,0:T(8,128)(2,1)} %rhs_ref.1), custom_call_target="tpu_custom_call" | custom-call | flops 1048576 | bytes 4194304 | tf_op jit(solution)/shard_map/mask_all/pallas_call | solution.py:81
  4.6 7.3 %all-to-all-start = ((bf16[16,512,128]{2,1,0:T(8,128)(2,1)}), bf16[16,512,128]{2,1,0:T(8,128)(2,1)S(1)}, u32[]{:S(2)}, u32[]{:S(2)}) async-start(bf16[16,512,128]{2,1,0:T(8,128)(2,1)} %get-tuple-element.39), calls=%async_computation | async-start | bytes 4194304 | tf_op jit(solution)/shard_map/all_to_all | solution.py:531
  11.8 0.0 copy-start.18
  11.9 3.0 %pack_contrib.1 = (bf16[512,1024]{1,0:T(8,128)(2,1)}, bf16[512,1024]{1,0:T(8,128)(2,1)}) custom-call(s32[1]{0:T(128)} %bitcast.5.high_ref, bf16[512,2048]{1,0:T(8,128)(2,1)} %bitcast.13, f32[8,128]{1,0:T(8,128)} %get-tuple-element.41.after_ref), custom_call_target="tpu_custom_call" | custom-call | bytes 1048576 | tf_op jit(solution)/shard_map/pack_contrib/pallas_call | solution.py:225
  14.9 1.9 collective-permute-start.1
  16.8 0.1 collective-permute-start
  16.9 0.9 constant_dynamic-slice_fusion
  17.9 5.8 %sort.15 = (f32[16,1024]{1,0:T(8,128)S(1)}, s32[16,1024]{1,0:T(8,128)}) sort(f32[16,1024]{1,0:T(8,128)S(1)} %fusion, s32[16,1024]{1,0:T(8,128)S(1)} %iota.20), dimensions={1}, to_apply=%region_0.1 | sort | flops 229376 | bytes 262144 | tf_op jit(solution)/shard_map/jit(sort)/sort | solution.py:548
  23.7 0.6 gather_fusion.1
  24.3 0.1 broadcast_select_fusion
  24.4 3.0 %sorted_targets.3 = (f32[8,1024,128]{2,1,0:T(8,128)}, f32[8,128]{1,0:T(8,128)S(1)}) custom-call(f32[8,1,1024]{2,1,0:T(1,128)S(1)} %reshape.78.keys_ref, f32[8,128]{1,0:T(8,128)S(1)} %copy-done.10), custom_call_target="tpu_custom_call" | custom-call | bytes 1048576 | tf_op jit(solution)/shard_map/sorted_targets/pallas_call | solution.py:317
  27.4 0.6 gather_fusion
  28.0 0.1 broadcast_select_fusion.1
  28.1 3.1 %sorted_targets.2 = (f32[8,1024,128]{2,1,0:T(8,128)}, f32[8,128]{1,0:T(8,128)S(1)}) custom-call(f32[8,1,1024]{2,1,0:T(1,128)S(1)} %reshape.77.keys_ref, f32[8,128]{1,0:T(8,128)S(1)} %copy-done.10), custom_call_target="tpu_custom_call" | custom-call | bytes 1048576 | tf_op jit(solution)/shard_map/sorted_targets/pallas_call | solution.py:317
  31.2 0.2 dynamic-slice_reduce_fusion
  31.4 0.1 fusion.1
  31.5 0.1 reshape.81.keep_ref
  31.6 1.2 copy-done.9
  32.8 1.4 right_transposed.1.right_ref
  34.2 7.0 %collective-permute-done.refs_6_.other_ref = bf16[512,1024]{1,0:T(8,128)(2,1)} collective-permute-done((bf16[512,1024]{1,0:T(8,128)(2,1)}, bf16[512,1024]{1,0:T(8,128)(2,1)}, u32[]{:S(2)}, u32[]{:S(2)}) %collective-permute-start) | collective-permute-done | bytes 1048608 | tf_op jit(solution)/shard_map/ppermute | solution.py:532
  41.3 0.0 all-to-all-done.refs_0_.refs_1_.refs_2_.refs_3_
  41.3 1.2 copy-done.4
  42.5 4.3 %solve_group.2 = (bf16[4,2,512,128]{3,2,1,0:T(8,128)(2,1)}, bf16[16,128,512]{2,1,0:T(8,128)(2,1)}, f32[8,128]{1,0:T(8,128)}) custom-call(s32[4]{0:T(128)S(1)} %broadcast_xor_fusion.1.pairs_ref, s32[1]{0:T(128)} %bitcast.odd_ref, bf16[512,512]{1,0:T(8,128)(2,1)S(1)} %bitcast.8, bf16[1024,512]{1,0:T(8,128)(2,1)S(1)} %copy-done.4, ...), custom_call_target="tpu_custom_call" | custom-call | flops 1610612736 | bytes 4194304 | tf_op jit(solution)/shard_map/solve_group/pallas_call | solution.py:150
  46.8 9.5 %all-to-all-start.2 = ((bf16[16,128,512]{2,1,0:T(8,128)(2,1)}), bf16[16,128,512]{2,1,0:T(8,128)(2,1)}, u32[]{:S(2)}, u32[]{:S(2)}) async-start(bf16[16,128,512]{2,1,0:T(8,128)(2,1)} %get-tuple-element.54), calls=%async_computation.2 | async-start | bytes 4194304 | tf_op jit(solution)/shard_map/all_to_all | solution.py:527
  56.4 0.0 copy-start.13
  56.4 1.2 copy-done.13
  57.6 1.2 copy-done.14
  58.8 9.2 %sort_rows.1 = (bf16[1024,2048]{1,0:T(8,128)(2,1)}, bf16[8,1024,128]{2,1,0:T(8,128)(2,1)}, f32[8,128]{1,0:T(8,128)S(1)}) custom-call(s32[1]{0:T(128)} %bitcast.7.high_ref, f32[1,1024]{1,0:T(1,128)S(1)} %fusion.3.keys_ref, bf16[512,1024]{1,0:T(8,128)(2,1)S(1)} %bitcast.12, bf16[512,1024]{1,0:T(8,128)(2,1)} %collective-permute-done.refs_6_.other_ref, ...), custom_call_target="tpu_custom_call" | custom-call | flops 4294967296 | bytes 8388608 | tf_op jit(solution)/shard_map/sort_rows/pallas_call | solution.py:279
  68.0 4.3 %solve_group.3 = (bf16[4,2,512,128]{3,2,1,0:T(8,128)(2,1)}, bf16[16,128,512]{2,1,0:T(8,128)(2,1)}, f32[8,128]{1,0:T(8,128)}) custom-call(s32[4]{0:T(128)S(1)} %broadcast_xor_fusion.pairs_ref, s32[1]{0:T(128)} %bitcast.odd_ref, bf16[512,512]{1,0:T(8,128)(2,1)S(1)} %bitcast.9, bf16[1024,512]{1,0:T(8,128)(2,1)S(1)} %copy-done.5, ...), custom_call_target="tpu_custom_call" | custom-call | flops 1610612736 | bytes 4194304 | tf_op jit(solution)/shard_map/solve_group/pallas_call | solution.py:150
  72.3 33.3 %all-to-all-done.2.projected_ref = bf16[16,128,512]{2,1,0:T(8,128)(2,1)} async-done(((bf16[16,128,512]{2,1,0:T(8,128)(2,1)}), bf16[16,128,512]{2,1,0:T(8,128)(2,1)}, u32[]{:S(2)}, u32[]{:S(2)}) %all-to-all-start.2) | async-done | bytes 2097184 | tf_op jit(solution)/shard_map/all_to_all | solution.py:527
  105.7 6.1 %all-to-all-start.1 = ((bf16[16,128,512]{2,1,0:T(8,128)(2,1)}), bf16[16,128,512]{2,1,0:T(8,128)(2,1)}, u32[]{:S(2)}, u32[]{:S(2)}) async-start(bf16[16,128,512]{2,1,0:T(8,128)(2,1)} %get-tuple-element.51), calls=%async_computation.1 | async-start | bytes 4194304 | tf_op jit(solution)/shard_map/all_to_all | solution.py:527
  111.8 2.2 copy-done.2
  114.0 6.4 %update_group.2 = (s16[528,128]{1,0:T(8,128)(2,1)}, s16[528,128]{1,0:T(8,128)(2,1)}, s16[528,128]{1,0:T(8,128)(2,1)}, s16[528,128]{1,0:T(8,128)(2,1)}, s16[528,1...) custom-call(s32[4]{0:T(128)S(1)} %broadcast_xor_fusion.1.pairs_ref, ...), custom_call_target="tpu_custom_call" | custom-call | flops 2147483648 | bytes 4194304 | tf_op jit(solution)/shard_map/update_group/pallas_call | solution.py:364
  120.4 0.8 collective-permute-start.2
  121.2 1.8 collective-permute-start.3
  123.0 3.3 %collective-permute-start.4 = (s16[528,128]{1,0:T(8,128)(2,1)}, s16[528,128]{1,0:T(8,128)(2,1)S(1)}, u32[]{:S(2)}, u32[]{:S(2)}) collective-permute-start(s16[528,128]{1,0:T(8,128)(2,1)} %get-tuple-element.57), channel_id=1, source_target_pairs={{0,12},{1,13},{2,14},{3,15},{4,8},{5,9},{6,10},{7,11},{8,4},{9,5},... | collective-permute-start | bytes 405512 | tf_op jit(solution)/shard_map/ppermute | solution.py:524
  126.3 3.0 %collective-permute-start.5 = (s16[528,128]{1,0:T(8,128)(2,1)}, s16[528,128]{1,0:T(8,128)(2,1)S(1)}, u32[]{:S(2)}, u32[]{:S(2)}) collective-permute-start(s16[528,128]{1,0:T(8,128)(2,1)} %get-tuple-element.58), channel_id=1, source_target_pairs={{0,13},{1,12},{2,15},{3,14},{4,9},{5,8},{6,11},{7,10},{8,5},{9,4},... | collective-permute-start | bytes 405512 | tf_op jit(solution)/shard_map/ppermute | solution.py:524
  129.3 3.0 %collective-permute-start.6 = (s16[528,128]{1,0:T(8,128)(2,1)}, s16[528,128]{1,0:T(8,128)(2,1)S(1)}, u32[]{:S(2)}, u32[]{:S(2)}) collective-permute-start(s16[528,128]{1,0:T(8,128)(2,1)} %get-tuple-element.59), channel_id=1, source_target_pairs={{0,4},{1,5},{2,6},{3,7},{4,0},{5,1},{6,2},{7,3},{8,12},{9,13},{10,... | collective-permute-start | bytes 405512 | tf_op jit(solution)/shard_map/ppermute | solution.py:524
  132.2 0.0 collective-permute-done.3.refs_1_
  132.3 8.4 %collective-permute-start.8 = (s16[528,128]{1,0:T(8,128)(2,1)}, s16[528,128]{1,0:T(8,128)(2,1)S(1)}, u32[]{:S(2)}, u32[]{:S(2)}) collective-permute-start(s16[528,128]{1,0:T(8,128)(2,1)} %get-tuple-element.61), channel_id=1, source_target_pairs={{0,6},{1,7},{2,4},{3,5},{4,2},{5,3},{6,0},{7,1},{8,14},{9,15},{10,... | collective-permute-start | bytes 405512 | tf_op jit(solution)/shard_map/ppermute | solution.py:524
  140.7 0.0 collective-permute-done.4.refs_2_
  140.7 7.0 %collective-permute-start.9 = (s16[528,128]{1,0:T(8,128)(2,1)}, s16[528,128]{1,0:T(8,128)(2,1)S(1)}, u32[]{:S(2)}, u32[]{:S(2)}) collective-permute-start(s16[528,128]{1,0:T(8,128)(2,1)} %get-tuple-element.62), channel_id=1, source_target_pairs={{0,7},{1,6},{2,5},{3,4},{4,3},{5,2},{6,1},{7,0},{8,15},{9,14},{10,... | collective-permute-start | bytes 405512 | tf_op jit(solution)/shard_map/ppermute | solution.py:524
  147.7 0.4 convert_reduce_fusion
  148.1 0.0 collective-permute-done.5.refs_3_
  148.2 4.2 %collective-permute-done.9.refs_7_ = s16[528,128]{1,0:T(8,128)(2,1)S(1)} collective-permute-done((s16[528,128]{1,0:T(8,128)(2,1)}, s16[528,128]{1,0:T(8,128)(2,1)S(1)}, u32[]{:S(2)}, u32[]{:S(2)}) %collective-permute-start.9) | collective-permute-done | bytes 135200 | tf_op jit(solution)/shard_map/ppermute | solution.py:524
  152.4 5.6 %scatter_rows.2 = (f32[16,64,512]{2,1,0:T(8,128)}, f32[8,128]{1,0:T(8,128)S(1)}) custom-call(s32[8,16]{1,0:T(8,128)S(1)} %get-tuple-element.74.starts_ref, f32[8,1024,128]{2,1,0:T(8,128)S(1)} %copy-done.12, s16[528,128]{1,0:T(8,128)(2,1)S(1)} %collective-permute-done.2.refs_0_, s16[528,128]{1,0:T(8,128)(2,1)S(1)} %collective-permute-done.3.refs_1_, ...), custom_call_target="tpu_custom_call" | custom-call | flops 2415919104 | bytes 4194304 | tf_op jit(solution)/shard_map/scatter_rows/pallas_call | solution.py:439
  158.0 3.0 %all-to-all-done.1.projected_ref = bf16[16,128,512]{2,1,0:T(8,128)(2,1)} async-done(((bf16[16,128,512]{2,1,0:T(8,128)(2,1)}), bf16[16,128,512]{2,1,0:T(8,128)(2,1)}, u32[]{:S(2)}, u32[]{:S(2)}) %all-to-all-start.1) | async-done | bytes 2097184 | tf_op jit(solution)/shard_map/all_to_all | solution.py:527
  161.0 2.2 copy-done.3
  163.2 6.4 %update_group.3 = (s16[528,128]{1,0:T(8,128)(2,1)}, s16[528,128]{1,0:T(8,128)(2,1)}, s16[528,128]{1,0:T(8,128)(2,1)}, s16[528,128]{1,0:T(8,128)(2,1)}, s16[528,1...) custom-call(s32[4]{0:T(128)S(1)} %broadcast_xor_fusion.pairs_ref, ...), custom_call_target="tpu_custom_call" | custom-call | flops 2147483648 | bytes 4194304 | tf_op jit(solution)/shard_map/update_group/pallas_call | solution.py:364
  169.6 0.6 collective-permute-start.10
  170.2 1.8 collective-permute-start.11
  172.0 3.6 %collective-permute-start.12 = (s16[528,128]{1,0:T(8,128)(2,1)}, s16[528,128]{1,0:T(8,128)(2,1)S(1)}, u32[]{:S(2)}, u32[]{:S(2)}) collective-permute-start(s16[528,128]{1,0:T(8,128)(2,1)} %get-tuple-element.66), channel_id=1, source_target_pairs={{0,14},{1,15},{2,12},{3,13},{4,10},{5,11},{6,8},{7,9},{8,6},{9,7},... | collective-permute-start | bytes 405512 | tf_op jit(solution)/shard_map/ppermute | solution.py:524
  175.6 3.5 %collective-permute-start.13 = (s16[528,128]{1,0:T(8,128)(2,1)}, s16[528,128]{1,0:T(8,128)(2,1)S(1)}, u32[]{:S(2)}, u32[]{:S(2)}) collective-permute-start(s16[528,128]{1,0:T(8,128)(2,1)} %get-tuple-element.67), channel_id=1, source_target_pairs={{0,15},{1,14},{2,13},{3,12},{4,11},{5,10},{6,9},{7,8},{8,7},{9,6},... | collective-permute-start | bytes 405512 | tf_op jit(solution)/shard_map/ppermute | solution.py:524
  179.1 0.3 collective-permute-start.14
  179.5 1.8 collective-permute-start.16
  181.3 0.6 collective-permute-done.12.refs_2_
  181.9 4.1 %collective-permute-done.13.refs_3_ = s16[528,128]{1,0:T(8,128)(2,1)S(1)} collective-permute-done((s16[528,128]{1,0:T(8,128)(2,1)}, s16[528,128]{1,0:T(8,128)(2,1)S(1)}, u32[]{:S(2)}, u32[]{:S(2)}) %collective-permute-start.13) | collective-permute-done | bytes 135200 | tf_op jit(solution)/shard_map/ppermute | solution.py:524
  186.0 0.9 copy-done.15
  186.9 5.5 %scatter_rows.3 = (bf16[16,64,512]{2,1,0:T(8,128)(2,1)}, f32[8,128]{1,0:T(8,128)}) custom-call(s32[8,16]{1,0:T(8,128)S(1)} %get-tuple-element.75.starts_ref, f32[8,1024,128]{2,1,0:T(8,128)S(1)} %copy-done.11, s16[528,128]{1,0:T(8,128)(2,1)S(1)} %collective-permute-done.10.refs_0_, s16[528,128]{1,0:T(8,128)(2,1)S(1)} %collective-permute-done.11.refs_1_, ...), custom_call_target="tpu_custom_call" | custom-call | flops 2415919104 | bytes 4194304 | tf_op jit(solution)/shard_map/scatter_rows/pallas_call | solution.py:439
  192.4 7.2 %all-to-all-start.3 = ((bf16[16,64,512]{2,1,0:T(8,128)(2,1)}), bf16[16,64,512]{2,1,0:T(8,128)(2,1)S(1)}, u32[]{:S(2)}, u32[]{:S(2)}) async-start(bf16[16,64,512]{2,1,0:T(8,128)(2,1)} %get-tuple-element.73), calls=%async_computation.3 | async-start | bytes 2097152 | tf_op jit(solution)/shard_map/all_to_all | solution.py:527
  199.6 3.7 %place_blocks.1 = bf16[1,512,2048]{2,1,0:T(8,128)(2,1)} custom-call(s32[8]{0:T(128)S(1)} %broadcast_xor_fusion.2.pairs_ref, bf16[4,2,512,128]{3,2,1,0:T(8,128)(2,1)S(1)} %copy-done.7, bf16[4,2,512,128]{3,2,1,0:T(8,128)(2,1)S(1)} %copy-done.8), custom_call_target="tpu_custom_call" | custom-call | bytes 4194304 | tf_op jit(solution)/shard_map/place_blocks/pallas_call | solution.py:195
  203.3 24.0 %all-to-all-done.3.parts_ref = bf16[16,64,512]{2,1,0:T(8,128)(2,1)S(1)} async-done(((bf16[16,64,512]{2,1,0:T(8,128)(2,1)}), bf16[16,64,512]{2,1,0:T(8,128)(2,1)S(1)}, u32[]{:S(2)}, u32[]{:S(2)}) %all-to-all-start.3) | async-done | bytes 1048608 | tf_op jit(solution)/shard_map/all_to_all | solution.py:527
  227.3 1.7 total_rows.1
  (59 shorter events, 0.2 us)
Async XLA Ops:
  0.6 30.6 %copy-start = (s32[1,16,16]{2,1,0:T(8,128)S(1)}, s32[1,16,16]{2,1,0:T(8,128)}, u32[]{:S(2)}) copy-start(s32[1,16,16]{2,1,0:T(8,128)} %param.22) | copy-start | bytes 3076
  4.6 36.7 %all-to-all-start = ((bf16[16,512,128]{2,1,0:T(8,128)(2,1)}), bf16[16,512,128]{2,1,0:T(8,128)(2,1)S(1)}, u32[]{:S(2)}, u32[]{:S(2)}) async-start(bf16[16,512,128]{2,1,0:T(8,128)(2,1)} %get-tuple-element.39), calls=%async_computation | async-start | bytes 4194304 | tf_op jit(solution)/shard_map/all_to_all | solution.py:531
  11.8 6.0 %copy-start.17 = (s32[8]{0:T(128)S(1)}, s32[8]{0:T(128)}, u32[]{:S(2)}) copy-start(s32[8]{0:T(128)} %constant.142.clone) | copy-start | bytes 100
  11.8 6.0 %copy-start.18 = (s32[8]{0:T(128)S(1)}, s32[8]{0:T(128)}, u32[]{:S(2)}) copy-start(s32[8]{0:T(128)} %constant.143.clone) | copy-start | bytes 100
  11.9 12.5 %copy-start.10 = (f32[8,128]{1,0:T(8,128)S(1)}, f32[8,128]{1,0:T(8,128)}, u32[]{:S(2)}) copy-start(f32[8,128]{1,0:T(8,128)} %get-tuple-element.41.after_ref) | copy-start | bytes 12292
  14.9 19.3 %copy-start.21 = (s32[4]{0:T(128)S(1)}, s32[4]{0:T(128)}, u32[]{:S(2)}) copy-start(s32[4]{0:T(128)} %constant.140.clone) | copy-start | bytes 52
  14.9 26.4 %copy-start.6 = (bf16[1,512,512]{2,1,0:T(8,128)(2,1)S(1)}, bf16[1,512,512]{2,1,0:T(8,128)(2,1)}, u32[]{:S(2)}) copy-start(bf16[1,512,512]{2,1,0:T(8,128)(2,1)} %param.19) | copy-start | bytes 1572868
  14.9 19.3 %collective-permute-start.1 = (bf16[512,1024]{1,0:T(8,128)(2,1)}, bf16[512,1024]{1,0:T(8,128)(2,1)}, u32[]{:S(2)}, u32[]{:S(2)}) collective-permute-start(bf16[512,1024]{1,0:T(8,128)(2,1)} %get-tuple-element.44), channel_id=1, source_target_pairs={{0,16},{1,113},{2,18},{3,115},{4,20},{5,117},{6,22},{7,119},{8,24}... | collective-permute-start | bytes 3145736 | tf_op jit(solution)/shard_map/ppermute | solution.py:534
  16.8 24.4 %collective-permute-start = (bf16[512,1024]{1,0:T(8,128)(2,1)}, bf16[512,1024]{1,0:T(8,128)(2,1)}, u32[]{:S(2)}, u32[]{:S(2)}) collective-permute-start(bf16[512,1024]{1,0:T(8,128)(2,1)} %bitcast.11), channel_id=1, source_target_pairs={{0,16},{1,113},{2,18},{3,115},{4,20},{5,117},{6,22},{7,119},{8,24}... | collective-permute-start | bytes 3145736 | tf_op jit(solution)/shard_map/ppermute | solution.py:532
  31.6 1.2 copy-start.9
  41.3 1.2 copy-start.4
  46.8 9.5 %copy-start.20 = (s32[4]{0:T(128)S(1)}, s32[4]{0:T(128)}, u32[]{:S(2)}) copy-start(s32[4]{0:T(128)} %constant.141.clone) | copy-start | bytes 52
  46.8 58.8 %all-to-all-start.2 = ((bf16[16,128,512]{2,1,0:T(8,128)(2,1)}), bf16[16,128,512]{2,1,0:T(8,128)(2,1)}, u32[]{:S(2)}, u32[]{:S(2)}) async-start(bf16[16,128,512]{2,1,0:T(8,128)(2,1)} %get-tuple-element.54), calls=%async_computation.2 | async-start | bytes 4194304 | tf_op jit(solution)/shard_map/all_to_all | solution.py:527
  56.4 1.2 copy-start.13
  57.6 1.2 copy-start.14
  58.8 9.2 %copy-start.5 = (bf16[1024,512]{1,0:T(8,128)(2,1)S(1)}, bf16[1024,512]{1,0:T(8,128)(2,1)}, u32[]{:S(2)}) copy-start(bf16[1024,512]{1,0:T(8,128)(2,1)} %right_transposed.1.right_ref) | copy-start | bytes 3145732
  105.7 6.1 %copy-start.1 = (bf16[8,1024,128]{2,1,0:T(8,128)(2,1)S(1)}, bf16[8,1024,128]{2,1,0:T(8,128)(2,1)}, u32[]{:S(2)}) copy-start(bf16[8,1024,128]{2,1,0:T(8,128)(2,1)} %get-tuple-element.52.refs_0_.refs_1_.refs_2_.refs_3_) | copy-start | bytes 6291460
  105.7 55.4 %all-to-all-start.1 = ((bf16[16,128,512]{2,1,0:T(8,128)(2,1)}), bf16[16,128,512]{2,1,0:T(8,128)(2,1)}, u32[]{:S(2)}, u32[]{:S(2)}) async-start(bf16[16,128,512]{2,1,0:T(8,128)(2,1)} %get-tuple-element.51), calls=%async_computation.1 | async-start | bytes 4194304 | tf_op jit(solution)/shard_map/all_to_all | solution.py:527
  111.8 2.2 copy-start.2
  114.0 38.4 %copy-start.12 = (f32[8,1024,128]{2,1,0:T(8,128)S(1)}, f32[8,1024,128]{2,1,0:T(8,128)}, u32[]{:S(2)}) copy-start(f32[8,1024,128]{2,1,0:T(8,128)} %get-tuple-element.53.targets_ref) | copy-start | bytes 12582916
  120.4 11.9 %collective-permute-start.2 = (s16[528,128]{1,0:T(8,128)(2,1)}, s16[528,128]{1,0:T(8,128)(2,1)S(1)}, u32[]{:S(2)}, u32[]{:S(2)}) collective-permute-start(s16[528,128]{1,0:T(8,128)(2,1)} %get-tuple-element.55), channel_id=1, source_target_pairs={{0,8},{1,9},{2,10},{3,11},{4,12},{5,13},{6,14},{7,15},{8,0},{9,1},... | collective-permute-start | bytes 405512 | tf_op jit(solution)/shard_map/ppermute | solution.py:524
  121.2 11.1 %collective-permute-start.3 = (s16[528,128]{1,0:T(8,128)(2,1)}, s16[528,128]{1,0:T(8,128)(2,1)S(1)}, u32[]{:S(2)}, u32[]{:S(2)}) collective-permute-start(s16[528,128]{1,0:T(8,128)(2,1)} %get-tuple-element.56), channel_id=1, source_target_pairs={{0,9},{1,8},{2,11},{3,10},{4,13},{5,12},{6,15},{7,14},{8,1},{9,0},... | collective-permute-start | bytes 405512 | tf_op jit(solution)/shard_map/ppermute | solution.py:524
  123.0 17.8 %collective-permute-start.4 = (s16[528,128]{1,0:T(8,128)(2,1)}, s16[528,128]{1,0:T(8,128)(2,1)S(1)}, u32[]{:S(2)}, u32[]{:S(2)}) collective-permute-start(s16[528,128]{1,0:T(8,128)(2,1)} %get-tuple-element.57), channel_id=1, source_target_pairs={{0,12},{1,13},{2,14},{3,15},{4,8},{5,9},{6,10},{7,11},{8,4},{9,5},... | collective-permute-start | bytes 405512 | tf_op jit(solution)/shard_map/ppermute | solution.py:524
  126.3 21.8 %collective-permute-start.5 = (s16[528,128]{1,0:T(8,128)(2,1)}, s16[528,128]{1,0:T(8,128)(2,1)S(1)}, u32[]{:S(2)}, u32[]{:S(2)}) collective-permute-start(s16[528,128]{1,0:T(8,128)(2,1)} %get-tuple-element.58), channel_id=1, source_target_pairs={{0,13},{1,12},{2,15},{3,14},{4,9},{5,8},{6,11},{7,10},{8,5},{9,4},... | collective-permute-start | bytes 405512 | tf_op jit(solution)/shard_map/ppermute | solution.py:524
  129.3 18.9 %collective-permute-start.6 = (s16[528,128]{1,0:T(8,128)(2,1)}, s16[528,128]{1,0:T(8,128)(2,1)S(1)}, u32[]{:S(2)}, u32[]{:S(2)}) collective-permute-start(s16[528,128]{1,0:T(8,128)(2,1)} %get-tuple-element.59), channel_id=1, source_target_pairs={{0,4},{1,5},{2,6},{3,7},{4,0},{5,1},{6,2},{7,3},{8,12},{9,13},{10,... | collective-permute-start | bytes 405512 | tf_op jit(solution)/shard_map/ppermute | solution.py:524
  132.2 15.9 %collective-permute-start.7 = (s16[528,128]{1,0:T(8,128)(2,1)}, s16[528,128]{1,0:T(8,128)(2,1)S(1)}, u32[]{:S(2)}, u32[]{:S(2)}) collective-permute-start(s16[528,128]{1,0:T(8,128)(2,1)} %get-tuple-element.60), channel_id=1, source_target_pairs={{0,5},{1,4},{2,7},{3,6},{4,1},{5,0},{6,3},{7,2},{8,13},{9,12},{10,... | collective-permute-start | bytes 405512 | tf_op jit(solution)/shard_map/ppermute | solution.py:524
  132.3 15.9 %collective-permute-start.8 = (s16[528,128]{1,0:T(8,128)(2,1)}, s16[528,128]{1,0:T(8,128)(2,1)S(1)}, u32[]{:S(2)}, u32[]{:S(2)}) collective-permute-start(s16[528,128]{1,0:T(8,128)(2,1)} %get-tuple-element.61), channel_id=1, source_target_pairs={{0,6},{1,7},{2,4},{3,5},{4,2},{5,3},{6,0},{7,1},{8,14},{9,15},{10,... | collective-permute-start | bytes 405512 | tf_op jit(solution)/shard_map/ppermute | solution.py:524
  140.7 11.7 %collective-permute-start.9 = (s16[528,128]{1,0:T(8,128)(2,1)}, s16[528,128]{1,0:T(8,128)(2,1)S(1)}, u32[]{:S(2)}, u32[]{:S(2)}) collective-permute-start(s16[528,128]{1,0:T(8,128)(2,1)} %get-tuple-element.62), channel_id=1, source_target_pairs={{0,7},{1,6},{2,5},{3,4},{4,3},{5,2},{6,1},{7,0},{8,15},{9,14},{10,... | collective-permute-start | bytes 405512 | tf_op jit(solution)/shard_map/ppermute | solution.py:524
  161.0 2.2 copy-start.3
  163.2 22.7 %copy-start.11 = (f32[8,1024,128]{2,1,0:T(8,128)S(1)}, f32[8,1024,128]{2,1,0:T(8,128)}, u32[]{:S(2)}) copy-start(f32[8,1024,128]{2,1,0:T(8,128)} %get-tuple-element.49.targets_ref) | copy-start | bytes 12582916
  163.2 22.7 %copy-start.16 = (f32[16,64,512]{2,1,0:T(8,128)S(1)}, f32[16,64,512]{2,1,0:T(8,128)}, u32[]{:S(2)}) copy-start(f32[16,64,512]{2,1,0:T(8,128)} %get-tuple-element.72.refs_8_) | copy-start | bytes 6291460
  169.6 9.9 %collective-permute-start.10 = (s16[528,128]{1,0:T(8,128)(2,1)}, s16[528,128]{1,0:T(8,128)(2,1)S(1)}, u32[]{:S(2)}, u32[]{:S(2)}) collective-permute-start(s16[528,128]{1,0:T(8,128)(2,1)} %get-tuple-element.64), channel_id=1, source_target_pairs={{0,10},{1,11},{2,8},{3,9},{4,14},{5,15},{6,12},{7,13},{8,2},{9,3},... | collective-permute-start | bytes 405512 | tf_op jit(solution)/shard_map/ppermute | solution.py:524
  170.2 9.3 %collective-permute-start.11 = (s16[528,128]{1,0:T(8,128)(2,1)}, s16[528,128]{1,0:T(8,128)(2,1)S(1)}, u32[]{:S(2)}, u32[]{:S(2)}) collective-permute-start(s16[528,128]{1,0:T(8,128)(2,1)} %get-tuple-element.65), channel_id=1, source_target_pairs={{0,11},{1,10},{2,9},{3,8},{4,15},{5,14},{6,13},{7,12},{8,3},{9,2},... | collective-permute-start | bytes 405512 | tf_op jit(solution)/shard_map/ppermute | solution.py:524
  172.0 9.8 %collective-permute-start.12 = (s16[528,128]{1,0:T(8,128)(2,1)}, s16[528,128]{1,0:T(8,128)(2,1)S(1)}, u32[]{:S(2)}, u32[]{:S(2)}) collective-permute-start(s16[528,128]{1,0:T(8,128)(2,1)} %get-tuple-element.66), channel_id=1, source_target_pairs={{0,14},{1,15},{2,12},{3,13},{4,10},{5,11},{6,8},{7,9},{8,6},{9,7},... | collective-permute-start | bytes 405512 | tf_op jit(solution)/shard_map/ppermute | solution.py:524
  175.6 10.3 %collective-permute-start.13 = (s16[528,128]{1,0:T(8,128)(2,1)}, s16[528,128]{1,0:T(8,128)(2,1)S(1)}, u32[]{:S(2)}, u32[]{:S(2)}) collective-permute-start(s16[528,128]{1,0:T(8,128)(2,1)} %get-tuple-element.67), channel_id=1, source_target_pairs={{0,15},{1,14},{2,13},{3,12},{4,11},{5,10},{6,9},{7,8},{8,7},{9,6},... | collective-permute-start | bytes 405512 | tf_op jit(solution)/shard_map/ppermute | solution.py:524
  179.1 6.8 %collective-permute-start.14 = (s16[528,128]{1,0:T(8,128)(2,1)}, s16[528,128]{1,0:T(8,128)(2,1)S(1)}, u32[]{:S(2)}, u32[]{:S(2)}) collective-permute-start(s16[528,128]{1,0:T(8,128)(2,1)} %get-tuple-element.68), channel_id=1, source_target_pairs={{0,2},{1,3},{2,0},{3,1},{4,6},{5,7},{6,4},{7,5},{8,10},{9,11},{10,... | collective-permute-start | bytes 405512 | tf_op jit(solution)/shard_map/ppermute | solution.py:524
  179.5 6.5 %collective-permute-start.15 = (s16[528,128]{1,0:T(8,128)(2,1)}, s16[528,128]{1,0:T(8,128)(2,1)S(1)}, u32[]{:S(2)}, u32[]{:S(2)}) collective-permute-start(s16[528,128]{1,0:T(8,128)(2,1)} %get-tuple-element.69), channel_id=1, source_target_pairs={{0,3},{1,2},{2,1},{3,0},{4,7},{5,6},{6,5},{7,4},{8,11},{9,10},{10,... | collective-permute-start | bytes 405512 | tf_op jit(solution)/shard_map/ppermute | solution.py:524
  179.5 6.5 %collective-permute-start.16 = (s16[528,128]{1,0:T(8,128)(2,1)}, s16[528,128]{1,0:T(8,128)(2,1)S(1)}, u32[]{:S(2)}, u32[]{:S(2)}) collective-permute-start(s16[528,128]{1,0:T(8,128)(2,1)} %get-tuple-element.71), channel_id=1, source_target_pairs={{0,1},{1,0},{2,3},{3,2},{4,5},{5,4},{6,7},{7,6},{8,9},{9,8},{10,11... | collective-permute-start | bytes 405512 | tf_op jit(solution)/shard_map/ppermute | solution.py:524
  186.0 0.9 copy-start.15
  192.4 7.2 %copy-start.19 = (s32[8]{0:T(128)S(1)}, s32[8]{0:T(128)}, u32[]{:S(2)}) copy-start(s32[8]{0:T(128)} %constant.139.clone) | copy-start | bytes 100
  192.4 7.3 %copy-start.7 = (bf16[4,2,512,128]{3,2,1,0:T(8,128)(2,1)S(1)}, bf16[4,2,512,128]{3,2,1,0:T(8,128)(2,1)}, u32[]{:S(2)}) copy-start(bf16[4,2,512,128]{3,2,1,0:T(8,128)(2,1)} %get-tuple-element.45.refs_0_) | copy-start | bytes 3145732
  192.4 7.3 %copy-start.8 = (bf16[4,2,512,128]{3,2,1,0:T(8,128)(2,1)S(1)}, bf16[4,2,512,128]{3,2,1,0:T(8,128)(2,1)}, u32[]{:S(2)}) copy-start(bf16[4,2,512,128]{3,2,1,0:T(8,128)(2,1)} %get-tuple-element.48.refs_1_) | copy-start | bytes 3145732
  192.4 35.0 %all-to-all-start.3 = ((bf16[16,64,512]{2,1,0:T(8,128)(2,1)}), bf16[16,64,512]{2,1,0:T(8,128)(2,1)S(1)}, u32[]{:S(2)}, u32[]{:S(2)}) async-start(bf16[16,64,512]{2,1,0:T(8,128)(2,1)} %get-tuple-element.73), calls=%async_computation.3 | async-start | bytes 2097152 | tf_op jit(solution)/shard_map/all_to_all | solution.py:527

commit v5 on v4

--- a/solution.py
+++ b/solution.py
@@ -166,7 +166,7 @@
                 token_spec(),
             ],
         ),
-        compiler_params=params(20),
+        compiler_params=params(60),
         cost_estimate=cost(4 * rows * (rows + width) * count * CW, 4 * count * CW * (2 * rows + width)),
         name="solve_group",
     )(pairs, odd, inverse, right, *([blocks] * count), *earlier)
@@ -375,7 +375,7 @@
             + untouched(len(earlier)),
             out_specs=[pl.BlockSpec(coded, lambda i, a, b: (0, 0))] * (2 * count),
         ),
-        compiler_params=params(28),
+        compiler_params=params(60),
         cost_estimate=cost(2 * joint * width * count * CW, 2 * count * CW * (width + 2 * joint)),
         name="update_group",
     )(pairs, odd, left, projected, *([contrib] * count), *earlier)

time: 230 us -> 237 us (1.030)
  starting transfers between devices: 71.1 us -> 63.5 us
  waiting for transfers between devices: 76.3 us -> 83.1 us
  Pallas kernels: 61.6 us -> 67.1 us
    ppermute x15, starting transfers between devices: 38.9 us -> 28.3 us  [exchange(): lax.ppermute(v, 'blk', p)]
    ppermute x15, waiting for transfers between devices: 8.89 us -> 18.7 us  [exchange(): lax.ppermute(v, 'blk', p)]
    pallas_call x2, Pallas kernels: 8.63 us -> 11.9 us  [solve_group(): pl.pallas_call(functools.partial(solve_body, count, ring), out_shape=[plt...]
    all_to_all x3, starting transfers between devices: 22.8 us -> 25.9 us  [over_owner(): lax.all_to_all(value, 'owner', split_axis=0, concat_axis=0, tiled=True)]
    pallas_call x2, Pallas kernels: 12.8 us -> 15.5 us  [update_group(): pl.pallas_call(functools.partial(update_body, count), out_shape=[pltpu.HB...]
    unnamed x44 -> x50, local copies, waits for them, and re-layouts: 10.2 us -> 11.3 us
  transfers between devices with their start and end apart: 21 -> 21, of which waited for: 7 -> 9; matrix products, arithmetic and copies ran while one was open for 4% -> 4% of each run, Pallas kernels for 17% -> 18%
where the time goes in v5:
time: 237 us; the launch traced here: 236 us
  waiting for transfers between devices  83.1 us (35%)
  Pallas kernels  67.1 us (28%)
  starting transfers between devices  63.5 us (27%)
  local copies, waits for them, and re-layouts  12.7 us (5%)
  other arithmetic  8.5 us (4%)
    all_to_all x3, waiting for transfers between devices, over_owner(): lax.all_to_all(value, 'owner', split_axis=0, concat_axis=0, tiled=True)  58 us
    ppermute x15, starting transfers between devices, exchange(): lax.ppermute(v, 'blk', p)  28.3 us
    all_to_all x3, starting transfers between devices, over_owner(): lax.all_to_all(value, 'owner', split_axis=0, concat_axis=0, tiled=True)  25.9 us
    ppermute x15, waiting for transfers between devices, exchange(): lax.ppermute(v, 'blk', p)  18.7 us
    pallas_call x2, Pallas kernels, update_group(): pl.pallas_call(functools.partial(update_body, count), out_shape=[pltpu.HB...  15.5 us
    pallas_call x2, Pallas kernels, solve_group(): pl.pallas_call(functools.partial(solve_body, count, ring), out_shape=[plt...  11.9 us
    unnamed x50, local copies, waits for them, and re-layouts  11.3 us
    pallas_call x2, Pallas kernels, scatter_rows(): pl.pallas_call(functools.partial(scatter_body, count, has_partial), out_s...  11.1 us
  transfers between devices with their start and end apart: 21, of which 9 were waited for; matrix products, arithmetic and copies ran while one was open for 4% of the time, Pallas kernels for 18%

profile of v5, /device:TPU:16, one launch (start us, length us, event | category | flops | bytes accessed | tf_op | source)
XLA Modules:
  0.0 235.9 jit_solution(646176162031761988)
XLA Ops:
  0.6 3.9 %mask_all.1 = (bf16[16,512,128]{2,1,0:T(8,128)(2,1)}, f32[8,128]{1,0:T(8,128)}) custom-call(s32[16]{0:T(128)} %bitcast.14, bf16[16,512,128]{2,1,0:T(8,128)(2,1)} %rhs_ref.1), custom_call_target="tpu_custom_call" | custom-call | flops 1048576 | bytes 4194304 | tf_op jit(solution)/shard_map/mask_all/pallas_call | solution.py:81
  4.6 7.3 %all-to-all-start = ((bf16[16,512,128]{2,1,0:T(8,128)(2,1)}), bf16[16,512,128]{2,1,0:T(8,128)(2,1)}, u32[]{:S(2)}, u32[]{:S(2)}) async-start(bf16[16,512,128]{2,1,0:T(8,128)(2,1)} %get-tuple-element.39), calls=%async_computation | async-start | bytes 4194304 | tf_op jit(solution)/shard_map/all_to_all | solution.py:531
  11.9 3.2 %pack_contrib.1 = (bf16[512,1024]{1,0:T(8,128)(2,1)}, bf16[512,1024]{1,0:T(8,128)(2,1)}) custom-call(s32[1]{0:T(128)} %bitcast.5.high_ref, bf16[512,2048]{1,0:T(8,128)(2,1)} %bitcast.13, f32[8,128]{1,0:T(8,128)} %get-tuple-element.41.after_ref), custom_call_target="tpu_custom_call" | custom-call | bytes 1048576 | tf_op jit(solution)/shard_map/pack_contrib/pallas_call | solution.py:225
  15.1 1.9 collective-permute-start.1
  17.0 0.1 collective-permute-start
  17.1 0.9 constant_dynamic-slice_fusion
  18.1 5.8 %sort.15 = (f32[16,1024]{1,0:T(8,128)S(1)}, s32[16,1024]{1,0:T(8,128)}) sort(f32[16,1024]{1,0:T(8,128)S(1)} %fusion, s32[16,1024]{1,0:T(8,128)S(1)} %iota.20), dimensions={1}, to_apply=%region_0.1 | sort | flops 229376 | bytes 262144 | tf_op jit(solution)/shard_map/jit(sort)/sort | solution.py:548
  23.9 0.6 gather_fusion.1
  24.5 0.1 broadcast_select_fusion
  24.6 3.0 %sorted_targets.3 = (f32[8,1024,128]{2,1,0:T(8,128)}, f32[8,128]{1,0:T(8,128)S(1)}) custom-call(f32[8,1,1024]{2,1,0:T(1,128)S(1)} %reshape.78.keys_ref, f32[8,128]{1,0:T(8,128)S(1)} %copy-done.8), custom_call_target="tpu_custom_call" | custom-call | bytes 1048576 | tf_op jit(solution)/shard_map/sorted_targets/pallas_call | solution.py:317
  27.6 0.6 copy-done.9
  28.2 0.6 gather_fusion
  28.8 0.1 broadcast_select_fusion.1
  28.9 3.1 %sorted_targets.2 = (f32[8,1024,128]{2,1,0:T(8,128)}, f32[8,128]{1,0:T(8,128)S(1)}) custom-call(f32[8,1,1024]{2,1,0:T(1,128)S(1)} %reshape.77.keys_ref, f32[8,128]{1,0:T(8,128)S(1)} %copy-done.8), custom_call_target="tpu_custom_call" | custom-call | bytes 1048576 | tf_op jit(solution)/shard_map/sorted_targets/pallas_call | solution.py:317
  32.0 0.6 copy-done.10
  32.6 0.2 dynamic-slice_reduce_fusion
  32.8 0.1 fusion.1
  32.9 0.1 reshape.81.keep_ref
  32.9 1.4 right_transposed.1.right_ref
  34.4 0.5 broadcast_xor_fusion.1.pairs_ref
  34.9 6.4 %collective-permute-done.refs_6_.other_ref = bf16[512,1024]{1,0:T(8,128)(2,1)S(1)} collective-permute-done((bf16[512,1024]{1,0:T(8,128)(2,1)}, bf16[512,1024]{1,0:T(8,128)(2,1)S(1)}, u32[]{:S(2)}, u32[]{:S(2)}) %collective-permute-start) | collective-permute-done | bytes 1048608 | tf_op jit(solution)/shard_map/ppermute | solution.py:532
  41.3 1.0 copy-done.6
  42.3 6.0 %solve_group.2 = (bf16[4,2,512,128]{3,2,1,0:T(8,128)(2,1)}, bf16[16,128,512]{2,1,0:T(8,128)(2,1)}, f32[8,128]{1,0:T(8,128)}) custom-call(s32[4]{0:T(128)} %broadcast_xor_fusion.1.pairs_ref, s32[1]{0:T(128)} %bitcast.odd_ref, bf16[512,512]{1,0:T(8,128)(2,1)} %bitcast.11, bf16[1024,512]{1,0:T(8,128)(2,1)} %right_transposed.1.right_ref, ...), custom_call_target="tpu_custom_call" | custom-call | flops 1610612736 | bytes 4194304 | tf_op jit(solution)/shard_map/solve_group/pallas_call | solution.py:150
  48.3 9.6 %all-to-all-start.2 = ((bf16[16,128,512]{2,1,0:T(8,128)(2,1)}), bf16[16,128,512]{2,1,0:T(8,128)(2,1)}, u32[]{:S(2)}, u32[]{:S(2)}) async-start(bf16[16,128,512]{2,1,0:T(8,128)(2,1)} %get-tuple-element.54), calls=%async_computation.2 | async-start | bytes 4194304 | tf_op jit(solution)/shard_map/all_to_all | solution.py:527
  58.0 0.5 broadcast_xor_fusion.pairs_ref
  58.5 1.2 copy-done.16
  59.8 8.5 %sort_rows.1 = (bf16[1024,2048]{1,0:T(8,128)(2,1)}, bf16[8,1024,128]{2,1,0:T(8,128)(2,1)}, f32[8,128]{1,0:T(8,128)S(1)}) custom-call(s32[1]{0:T(128)} %bitcast.7.high_ref, f32[1,1024]{1,0:T(1,128)S(1)} %fusion.3.keys_ref, bf16[512,1024]{1,0:T(8,128)(2,1)S(1)} %bitcast.10, bf16[512,1024]{1,0:T(8,128)(2,1)S(1)} %copy-done.7, bf16[512,1024]{1,0:T(8,128)(2,1)S(1)} %copy-done.16, ...), custom_call_target="tpu_custom_call" | custom-call | flops 4294967296 | bytes 8388608 | tf_op jit(solution)/shard_map/sort_rows/pallas_call | solution.py:279
  68.3 0.6 copy-done.12
  68.9 6.0 %solve_group.3 = (bf16[4,2,512,128]{3,2,1,0:T(8,128)(2,1)}, bf16[16,128,512]{2,1,0:T(8,128)(2,1)}, f32[8,128]{1,0:T(8,128)}) custom-call(s32[4]{0:T(128)} %broadcast_xor_fusion.pairs_ref, s32[1]{0:T(128)} %bitcast.odd_ref, bf16[512,512]{1,0:T(8,128)(2,1)} %bitcast.12, bf16[1024,512]{1,0:T(8,128)(2,1)} %right_transposed.1.right_ref, ...), custom_call_target="tpu_custom_call" | custom-call | flops 1610612736 | bytes 4194304 | tf_op jit(solution)/shard_map/solve_group/pallas_call | solution.py:150
  74.8 32.4 %all-to-all-done.2.projected_ref = bf16[16,128,512]{2,1,0:T(8,128)(2,1)} async-done(((bf16[16,128,512]{2,1,0:T(8,128)(2,1)}), bf16[16,128,512]{2,1,0:T(8,128)(2,1)}, u32[]{:S(2)}, u32[]{:S(2)}) %all-to-all-start.2) | async-done | bytes 2097184 | tf_op jit(solution)/shard_map/all_to_all | solution.py:527
  107.3 5.9 %all-to-all-start.1 = ((bf16[16,128,512]{2,1,0:T(8,128)(2,1)}), bf16[16,128,512]{2,1,0:T(8,128)(2,1)S(1)}, u32[]{:S(2)}, u32[]{:S(2)}) async-start(bf16[16,128,512]{2,1,0:T(8,128)(2,1)} %get-tuple-element.51), calls=%async_computation.1 | async-start | bytes 4194304 | tf_op jit(solution)/shard_map/all_to_all | solution.py:527
  113.2 7.7 %update_group.2 = (s16[528,128]{1,0:T(8,128)(2,1)}, s16[528,128]{1,0:T(8,128)(2,1)}, s16[528,128]{1,0:T(8,128)(2,1)}, s16[528,128]{1,0:T(8,128)(2,1)}, s16[528,1...) custom-call(s32[4]{0:T(128)} %broadcast_xor_fusion.1.pairs_ref, ...), custom_call_target="tpu_custom_call" | custom-call | flops 2147483648 | bytes 4194304 | tf_op jit(solution)/shard_map/update_group/pallas_call | solution.py:364
  120.9 0.6 collective-permute-start.2
  121.5 2.0 collective-permute-start.3
  123.5 3.3 %collective-permute-start.4 = (s16[528,128]{1,0:T(8,128)(2,1)}, s16[528,128]{1,0:T(8,128)(2,1)S(1)}, u32[]{:S(2)}, u32[]{:S(2)}) collective-permute-start(s16[528,128]{1,0:T(8,128)(2,1)} %get-tuple-element.57), channel_id=1, source_target_pairs={{0,12},{1,13},{2,14},{3,15},{4,8},{5,9},{6,10},{7,11},{8,4},{9,5},... | collective-permute-start | bytes 405512 | tf_op jit(solution)/shard_map/ppermute | solution.py:524
  126.8 3.0 %collective-permute-start.5 = (s16[528,128]{1,0:T(8,128)(2,1)}, s16[528,128]{1,0:T(8,128)(2,1)S(1)}, u32[]{:S(2)}, u32[]{:S(2)}) collective-permute-start(s16[528,128]{1,0:T(8,128)(2,1)} %get-tuple-element.58), channel_id=1, source_target_pairs={{0,13},{1,12},{2,15},{3,14},{4,9},{5,8},{6,11},{7,10},{8,5},{9,4},... | collective-permute-start | bytes 405512 | tf_op jit(solution)/shard_map/ppermute | solution.py:524
  129.8 3.0 %collective-permute-start.6 = (s16[528,128]{1,0:T(8,128)(2,1)}, s16[528,128]{1,0:T(8,128)(2,1)S(1)}, u32[]{:S(2)}, u32[]{:S(2)}) collective-permute-start(s16[528,128]{1,0:T(8,128)(2,1)} %get-tuple-element.59), channel_id=1, source_target_pairs={{0,4},{1,5},{2,6},{3,7},{4,0},{5,1},{6,2},{7,3},{8,12},{9,13},{10,... | collective-permute-start | bytes 405512 | tf_op jit(solution)/shard_map/ppermute | solution.py:524
  132.8 9.5 %collective-permute-done.3.refs_1_ = s16[528,128]{1,0:T(8,128)(2,1)S(1)} collective-permute-done((s16[528,128]{1,0:T(8,128)(2,1)}, s16[528,128]{1,0:T(8,128)(2,1)S(1)}, u32[]{:S(2)}, u32[]{:S(2)}) %collective-permute-start.3) | collective-permute-done | bytes 135200 | tf_op jit(solution)/shard_map/ppermute | solution.py:524
  142.2 4.7 %collective-permute-start.9 = (s16[528,128]{1,0:T(8,128)(2,1)}, s16[528,128]{1,0:T(8,128)(2,1)S(1)}, u32[]{:S(2)}, u32[]{:S(2)}) collective-permute-start(s16[528,128]{1,0:T(8,128)(2,1)} %get-tuple-element.62), channel_id=1, source_target_pairs={{0,7},{1,6},{2,5},{3,4},{4,3},{5,2},{6,1},{7,0},{8,15},{9,14},{10,... | collective-permute-start | bytes 405512 | tf_op jit(solution)/shard_map/ppermute | solution.py:524
  147.0 0.4 convert_reduce_fusion
  147.4 1.4 collective-permute-done.8.refs_6_
  148.9 3.3 %collective-permute-done.9.refs_7_ = s16[528,128]{1,0:T(8,128)(2,1)S(1)} collective-permute-done((s16[528,128]{1,0:T(8,128)(2,1)}, s16[528,128]{1,0:T(8,128)(2,1)S(1)}, u32[]{:S(2)}, u32[]{:S(2)}) %collective-permute-start.9) | collective-permute-done | bytes 135200 | tf_op jit(solution)/shard_map/ppermute | solution.py:524
  152.2 2.2 copy-done.14
  154.4 5.6 %scatter_rows.2 = (f32[16,64,512]{2,1,0:T(8,128)}, f32[8,128]{1,0:T(8,128)S(1)}) custom-call(s32[8,16]{1,0:T(8,128)S(1)} %get-tuple-element.74.starts_ref, f32[8,1024,128]{2,1,0:T(8,128)S(1)} %copy-done.14, s16[528,128]{1,0:T(8,128)(2,1)S(1)} %collective-permute-done.2.refs_0_, s16[528,128]{1,0:T(8,128)(2,1)S(1)} %collective-permute-done.3.refs_1_, ...), custom_call_target="tpu_custom_call" | custom-call | flops 2415919104 | bytes 4194304 | tf_op jit(solution)/shard_map/scatter_rows/pallas_call | solution.py:439
  160.0 0.6 copy-done.11
  160.6 1.9 all-to-all-done.1.projected_ref
  162.5 1.3 copy-done.19
  163.8 7.8 %update_group.3 = (s16[528,128]{1,0:T(8,128)(2,1)}, s16[528,128]{1,0:T(8,128)(2,1)}, s16[528,128]{1,0:T(8,128)(2,1)}, s16[528,128]{1,0:T(8,128)(2,1)}, s16[528,1...) custom-call(s32[4]{0:T(128)} %broadcast_xor_fusion.pairs_ref, ...), custom_call_target="tpu_custom_call" | custom-call | flops 2147483648 | bytes 4194304 | tf_op jit(solution)/shard_map/update_group/pallas_call | solution.py:364
  171.6 0.7 collective-permute-start.10
  172.4 2.1 collective-permute-start.11
  174.4 3.2 %collective-permute-start.12 = (s16[528,128]{1,0:T(8,128)(2,1)}, s16[528,128]{1,0:T(8,128)(2,1)S(1)}, u32[]{:S(2)}, u32[]{:S(2)}) collective-permute-start(s16[528,128]{1,0:T(8,128)(2,1)} %get-tuple-element.66), channel_id=1, source_target_pairs={{0,14},{1,15},{2,12},{3,13},{4,10},{5,11},{6,8},{7,9},{8,6},{9,7},... | collective-permute-start | bytes 405512 | tf_op jit(solution)/shard_map/ppermute | solution.py:524
  177.7 3.5 %collective-permute-start.13 = (s16[528,128]{1,0:T(8,128)(2,1)}, s16[528,128]{1,0:T(8,128)(2,1)S(1)}, u32[]{:S(2)}, u32[]{:S(2)}) collective-permute-start(s16[528,128]{1,0:T(8,128)(2,1)} %get-tuple-element.67), channel_id=1, source_target_pairs={{0,15},{1,14},{2,13},{3,12},{4,11},{5,10},{6,9},{7,8},{8,7},{9,6},... | collective-permute-start | bytes 405512 | tf_op jit(solution)/shard_map/ppermute | solution.py:524
  181.1 0.3 collective-permute-start.14
  181.4 0.1 collective-permute-start.15
  181.6 1.7 collective-permute-start.16
  183.3 1.0 collective-permute-done.12.refs_2_
  184.3 3.4 %collective-permute-done.13.refs_3_ = s16[528,128]{1,0:T(8,128)(2,1)S(1)} collective-permute-done((s16[528,128]{1,0:T(8,128)(2,1)}, s16[528,128]{1,0:T(8,128)(2,1)S(1)}, u32[]{:S(2)}, u32[]{:S(2)}) %collective-permute-start.13) | collective-permute-done | bytes 135200 | tf_op jit(solution)/shard_map/ppermute | solution.py:524
  187.7 2.2 copy-done.13
  189.9 0.9 copy-done.17
  190.8 5.5 %scatter_rows.3 = (bf16[16,64,512]{2,1,0:T(8,128)(2,1)}, f32[8,128]{1,0:T(8,128)}) custom-call(s32[8,16]{1,0:T(8,128)S(1)} %get-tuple-element.75.starts_ref, f32[8,1024,128]{2,1,0:T(8,128)S(1)} %copy-done.13, s16[528,128]{1,0:T(8,128)(2,1)S(1)} %collective-permute-done.10.refs_0_, s16[528,128]{1,0:T(8,128)(2,1)S(1)} %collective-permute-done.11.refs_1_, ...), custom_call_target="tpu_custom_call" | custom-call | flops 2415919104 | bytes 4194304 | tf_op jit(solution)/shard_map/scatter_rows/pallas_call | solution.py:439
  196.3 10.4 %all-to-all-start.3 = ((bf16[16,64,512]{2,1,0:T(8,128)(2,1)}), bf16[16,64,512]{2,1,0:T(8,128)(2,1)S(1)}, u32[]{:S(2)}, u32[]{:S(2)}) async-start(bf16[16,64,512]{2,1,0:T(8,128)(2,1)} %get-tuple-element.73), calls=%async_computation.3 | async-start | bytes 2097152 | tf_op jit(solution)/shard_map/all_to_all | solution.py:527
  206.8 3.7 %place_blocks.1 = bf16[1,512,2048]{2,1,0:T(8,128)(2,1)} custom-call(s32[8]{0:T(128)S(1)} %broadcast_xor_fusion.2.pairs_ref, bf16[4,2,512,128]{3,2,1,0:T(8,128)(2,1)S(1)} %copy-done.1, bf16[4,2,512,128]{3,2,1,0:T(8,128)(2,1)S(1)} %copy-done.2), custom_call_target="tpu_custom_call" | custom-call | bytes 4194304 | tf_op jit(solution)/shard_map/place_blocks/pallas_call | solution.py:195
  210.4 23.7 %all-to-all-done.3.parts_ref = bf16[16,64,512]{2,1,0:T(8,128)(2,1)S(1)} async-done(((bf16[16,64,512]{2,1,0:T(8,128)(2,1)}), bf16[16,64,512]{2,1,0:T(8,128)(2,1)S(1)}, u32[]{:S(2)}, u32[]{:S(2)}) %all-to-all-start.3) | async-done | bytes 1048608 | tf_op jit(solution)/shard_map/all_to_all | solution.py:527
  234.2 1.7 total_rows.1
  (65 shorter events, 0.2 us)
Async XLA Ops:
  0.6 32.0 %copy-start = (s32[1,16,16]{2,1,0:T(8,128)S(1)}, s32[1,16,16]{2,1,0:T(8,128)}, u32[]{:S(2)}) copy-start(s32[1,16,16]{2,1,0:T(8,128)} %param.22) | copy-start | bytes 3076
  4.6 36.8 %all-to-all-start = ((bf16[16,512,128]{2,1,0:T(8,128)(2,1)}), bf16[16,512,128]{2,1,0:T(8,128)(2,1)}, u32[]{:S(2)}, u32[]{:S(2)}) async-start(bf16[16,512,128]{2,1,0:T(8,128)(2,1)} %get-tuple-element.39), calls=%async_computation | async-start | bytes 4194304 | tf_op jit(solution)/shard_map/all_to_all | solution.py:531
  11.8 6.1 %copy-start.20 = (s32[8]{0:T(128)S(1)}, s32[8]{0:T(128)}, u32[]{:S(2)}) copy-start(s32[8]{0:T(128)} %constant.142.clone) | copy-start | bytes 100
  11.8 6.1 %copy-start.21 = (s32[8]{0:T(128)S(1)}, s32[8]{0:T(128)}, u32[]{:S(2)}) copy-start(s32[8]{0:T(128)} %constant.143.clone) | copy-start | bytes 100
  11.9 12.7 %copy-start.8 = (f32[8,128]{1,0:T(8,128)S(1)}, f32[8,128]{1,0:T(8,128)}, u32[]{:S(2)}) copy-start(f32[8,128]{1,0:T(8,128)} %get-tuple-element.41.after_ref) | copy-start | bytes 12292
  11.9 21.1 %copy-start.3 = (bf16[1,512,1024]{2,1,0:T(8,128)(2,1)S(1)}, bf16[1,512,1024]{2,1,0:T(8,128)(2,1)}, u32[]{:S(2)}) copy-start(bf16[1,512,1024]{2,1,0:T(8,128)(2,1)} %param.20) | copy-start | bytes 3145732
  15.1 19.3 %copy-start.24 = (s32[4]{0:T(128)S(1)}, s32[4]{0:T(128)}, u32[]{:S(2)}) copy-start(s32[4]{0:T(128)} %constant.140.clone) | copy-start | bytes 52
  15.1 19.8 %collective-permute-start.1 = (bf16[512,1024]{1,0:T(8,128)(2,1)}, bf16[512,1024]{1,0:T(8,128)(2,1)S(1)}, u32[]{:S(2)}, u32[]{:S(2)}) collective-permute-start(bf16[512,1024]{1,0:T(8,128)(2,1)} %get-tuple-element.44), channel_id=1, source_target_pairs={{0,16},{1,113},{2,18},{3,115},{4,20},{5,117},{6,22},{7,119},{8,24}... | collective-permute-start | bytes 3145736 | tf_op jit(solution)/shard_map/ppermute | solution.py:534
  17.0 24.3 %collective-permute-start = (bf16[512,1024]{1,0:T(8,128)(2,1)}, bf16[512,1024]{1,0:T(8,128)(2,1)S(1)}, u32[]{:S(2)}, u32[]{:S(2)}) collective-permute-start(bf16[512,1024]{1,0:T(8,128)(2,1)} %bitcast.9), channel_id=1, source_target_pairs={{0,16},{1,113},{2,18},{3,115},{4,20},{5,117},{6,22},{7,119},{8,24}... | collective-permute-start | bytes 3145736 | tf_op jit(solution)/shard_map/ppermute | solution.py:532
  27.6 0.6 copy-start.9
  32.0 0.6 copy-start.10
  34.9 6.4 %copy-start.4 = (bf16[512,1024]{1,0:T(8,128)(2,1)}, bf16[512,1024]{1,0:T(8,128)(2,1)S(1)}, u32[]{:S(2)}) copy-start(bf16[512,1024]{1,0:T(8,128)(2,1)S(1)} %collective-permute-done.1.refs_7_.got_ref) | copy-start | bytes 3145732
  41.3 1.0 copy-start.6
  48.3 9.7 %copy-start.23 = (s32[4]{0:T(128)S(1)}, s32[4]{0:T(128)}, u32[]{:S(2)}) copy-start(s32[4]{0:T(128)} %constant.141.clone) | copy-start | bytes 52
  48.3 10.2 %copy-start.5 = (bf16[512,1024]{1,0:T(8,128)(2,1)S(1)}, bf16[512,1024]{1,0:T(8,128)(2,1)}, u32[]{:S(2)}) copy-start(bf16[512,1024]{1,0:T(8,128)(2,1)} %copy-done.4) | copy-start | bytes 3145732
  48.3 10.2 %copy-start.7 = (bf16[512,1024]{1,0:T(8,128)(2,1)S(1)}, bf16[512,1024]{1,0:T(8,128)(2,1)}, u32[]{:S(2)}) copy-start(bf16[512,1024]{1,0:T(8,128)(2,1)} %copy-done.6) | copy-start | bytes 3145732
  48.3 10.2 %copy-start.15 = (bf16[1,512,1024]{2,1,0:T(8,128)(2,1)S(1)}, bf16[1,512,1024]{2,1,0:T(8,128)(2,1)}, u32[]{:S(2)}) copy-start(bf16[1,512,1024]{2,1,0:T(8,128)(2,1)} %param.21) | copy-start | bytes 3145732
  48.3 59.0 %all-to-all-start.2 = ((bf16[16,128,512]{2,1,0:T(8,128)(2,1)}), bf16[16,128,512]{2,1,0:T(8,128)(2,1)}, u32[]{:S(2)}, u32[]{:S(2)}) async-start(bf16[16,128,512]{2,1,0:T(8,128)(2,1)} %get-tuple-element.54), calls=%async_computation.2 | async-start | bytes 4194304 | tf_op jit(solution)/shard_map/all_to_all | solution.py:527
  58.5 1.2 copy-start.16
  68.3 0.6 copy-start.12
  107.3 55.2 %all-to-all-start.1 = ((bf16[16,128,512]{2,1,0:T(8,128)(2,1)}), bf16[16,128,512]{2,1,0:T(8,128)(2,1)S(1)}, u32[]{:S(2)}, u32[]{:S(2)}) async-start(bf16[16,128,512]{2,1,0:T(8,128)(2,1)} %get-tuple-element.51), calls=%async_computation.1 | async-start | bytes 4194304 | tf_op jit(solution)/shard_map/all_to_all | solution.py:527
  120.9 11.9 %collective-permute-start.2 = (s16[528,128]{1,0:T(8,128)(2,1)}, s16[528,128]{1,0:T(8,128)(2,1)S(1)}, u32[]{:S(2)}, u32[]{:S(2)}) collective-permute-start(s16[528,128]{1,0:T(8,128)(2,1)} %get-tuple-element.55), channel_id=1, source_target_pairs={{0,8},{1,9},{2,10},{3,11},{4,12},{5,13},{6,14},{7,15},{8,0},{9,1},... | collective-permute-start | bytes 405512 | tf_op jit(solution)/shard_map/ppermute | solution.py:524
  121.5 20.7 %collective-permute-start.3 = (s16[528,128]{1,0:T(8,128)(2,1)}, s16[528,128]{1,0:T(8,128)(2,1)S(1)}, u32[]{:S(2)}, u32[]{:S(2)}) collective-permute-start(s16[528,128]{1,0:T(8,128)(2,1)} %get-tuple-element.56), channel_id=1, source_target_pairs={{0,9},{1,8},{2,11},{3,10},{4,13},{5,12},{6,15},{7,14},{8,1},{9,0},... | collective-permute-start | bytes 405512 | tf_op jit(solution)/shard_map/ppermute | solution.py:524
  123.5 18.7 %collective-permute-start.4 = (s16[528,128]{1,0:T(8,128)(2,1)}, s16[528,128]{1,0:T(8,128)(2,1)S(1)}, u32[]{:S(2)}, u32[]{:S(2)}) collective-permute-start(s16[528,128]{1,0:T(8,128)(2,1)} %get-tuple-element.57), channel_id=1, source_target_pairs={{0,12},{1,13},{2,14},{3,15},{4,8},{5,9},{6,10},{7,11},{8,4},{9,5},... | collective-permute-start | bytes 405512 | tf_op jit(solution)/shard_map/ppermute | solution.py:524
  126.8 20.6 %collective-permute-start.5 = (s16[528,128]{1,0:T(8,128)(2,1)}, s16[528,128]{1,0:T(8,128)(2,1)S(1)}, u32[]{:S(2)}, u32[]{:S(2)}) collective-permute-start(s16[528,128]{1,0:T(8,128)(2,1)} %get-tuple-element.58), channel_id=1, source_target_pairs={{0,13},{1,12},{2,15},{3,14},{4,9},{5,8},{6,11},{7,10},{8,5},{9,4},... | collective-permute-start | bytes 405512 | tf_op jit(solution)/shard_map/ppermute | solution.py:524
  129.8 17.6 %collective-permute-start.6 = (s16[528,128]{1,0:T(8,128)(2,1)}, s16[528,128]{1,0:T(8,128)(2,1)S(1)}, u32[]{:S(2)}, u32[]{:S(2)}) collective-permute-start(s16[528,128]{1,0:T(8,128)(2,1)} %get-tuple-element.59), channel_id=1, source_target_pairs={{0,4},{1,5},{2,6},{3,7},{4,0},{5,1},{6,2},{7,3},{8,12},{9,13},{10,... | collective-permute-start | bytes 405512 | tf_op jit(solution)/shard_map/ppermute | solution.py:524
  132.8 14.7 %collective-permute-start.7 = (s16[528,128]{1,0:T(8,128)(2,1)}, s16[528,128]{1,0:T(8,128)(2,1)S(1)}, u32[]{:S(2)}, u32[]{:S(2)}) collective-permute-start(s16[528,128]{1,0:T(8,128)(2,1)} %get-tuple-element.60), channel_id=1, source_target_pairs={{0,5},{1,4},{2,7},{3,6},{4,1},{5,0},{6,3},{7,2},{8,13},{9,12},{10,... | collective-permute-start | bytes 405512 | tf_op jit(solution)/shard_map/ppermute | solution.py:524
  142.2 6.7 %collective-permute-start.8 = (s16[528,128]{1,0:T(8,128)(2,1)}, s16[528,128]{1,0:T(8,128)(2,1)S(1)}, u32[]{:S(2)}, u32[]{:S(2)}) collective-permute-start(s16[528,128]{1,0:T(8,128)(2,1)} %get-tuple-element.61), channel_id=1, source_target_pairs={{0,6},{1,7},{2,4},{3,5},{4,2},{5,3},{6,0},{7,1},{8,14},{9,15},{10,... | collective-permute-start | bytes 405512 | tf_op jit(solution)/shard_map/ppermute | solution.py:524
  142.2 10.0 %collective-permute-start.9 = (s16[528,128]{1,0:T(8,128)(2,1)}, s16[528,128]{1,0:T(8,128)(2,1)S(1)}, u32[]{:S(2)}, u32[]{:S(2)}) collective-permute-start(s16[528,128]{1,0:T(8,128)(2,1)} %get-tuple-element.62), channel_id=1, source_target_pairs={{0,7},{1,6},{2,5},{3,4},{4,3},{5,2},{6,1},{7,0},{8,15},{9,14},{10,... | collective-permute-start | bytes 405512 | tf_op jit(solution)/shard_map/ppermute | solution.py:524
  152.2 2.2 copy-start.14
  160.0 0.6 copy-start.11
  162.5 1.3 copy-start.19
  163.8 23.9 %copy-start.18 = (f32[16,64,512]{2,1,0:T(8,128)S(1)}, f32[16,64,512]{2,1,0:T(8,128)}, u32[]{:S(2)}) copy-start(f32[16,64,512]{2,1,0:T(8,128)} %get-tuple-element.72.refs_8_) | copy-start | bytes 6291460
  171.6 9.8 %collective-permute-start.10 = (s16[528,128]{1,0:T(8,128)(2,1)}, s16[528,128]{1,0:T(8,128)(2,1)S(1)}, u32[]{:S(2)}, u32[]{:S(2)}) collective-permute-start(s16[528,128]{1,0:T(8,128)(2,1)} %get-tuple-element.64), channel_id=1, source_target_pairs={{0,10},{1,11},{2,8},{3,9},{4,14},{5,15},{6,12},{7,13},{8,2},{9,3},... | collective-permute-start | bytes 405512 | tf_op jit(solution)/shard_map/ppermute | solution.py:524
  172.4 9.2 %collective-permute-start.11 = (s16[528,128]{1,0:T(8,128)(2,1)}, s16[528,128]{1,0:T(8,128)(2,1)S(1)}, u32[]{:S(2)}, u32[]{:S(2)}) collective-permute-start(s16[528,128]{1,0:T(8,128)(2,1)} %get-tuple-element.65), channel_id=1, source_target_pairs={{0,11},{1,10},{2,9},{3,8},{4,15},{5,14},{6,13},{7,12},{8,3},{9,2},... | collective-permute-start | bytes 405512 | tf_op jit(solution)/shard_map/ppermute | solution.py:524
  174.4 9.9 %collective-permute-start.12 = (s16[528,128]{1,0:T(8,128)(2,1)}, s16[528,128]{1,0:T(8,128)(2,1)S(1)}, u32[]{:S(2)}, u32[]{:S(2)}) collective-permute-start(s16[528,128]{1,0:T(8,128)(2,1)} %get-tuple-element.66), channel_id=1, source_target_pairs={{0,14},{1,15},{2,12},{3,13},{4,10},{5,11},{6,8},{7,9},{8,6},{9,7},... | collective-permute-start | bytes 405512 | tf_op jit(solution)/shard_map/ppermute | solution.py:524
  177.7 10.0 %collective-permute-start.13 = (s16[528,128]{1,0:T(8,128)(2,1)}, s16[528,128]{1,0:T(8,128)(2,1)S(1)}, u32[]{:S(2)}, u32[]{:S(2)}) collective-permute-start(s16[528,128]{1,0:T(8,128)(2,1)} %get-tuple-element.67), channel_id=1, source_target_pairs={{0,15},{1,14},{2,13},{3,12},{4,11},{5,10},{6,9},{7,8},{8,7},{9,6},... | collective-permute-start | bytes 405512 | tf_op jit(solution)/shard_map/ppermute | solution.py:524
  181.1 6.6 %collective-permute-start.14 = (s16[528,128]{1,0:T(8,128)(2,1)}, s16[528,128]{1,0:T(8,128)(2,1)S(1)}, u32[]{:S(2)}, u32[]{:S(2)}) collective-permute-start(s16[528,128]{1,0:T(8,128)(2,1)} %get-tuple-element.68), channel_id=1, source_target_pairs={{0,2},{1,3},{2,0},{3,1},{4,6},{5,7},{6,4},{7,5},{8,10},{9,11},{10,... | collective-permute-start | bytes 405512 | tf_op jit(solution)/shard_map/ppermute | solution.py:524
  181.4 6.3 %collective-permute-start.15 = (s16[528,128]{1,0:T(8,128)(2,1)}, s16[528,128]{1,0:T(8,128)(2,1)S(1)}, u32[]{:S(2)}, u32[]{:S(2)}) collective-permute-start(s16[528,128]{1,0:T(8,128)(2,1)} %get-tuple-element.69), channel_id=1, source_target_pairs={{0,3},{1,2},{2,1},{3,0},{4,7},{5,6},{6,5},{7,4},{8,11},{9,10},{10,... | collective-permute-start | bytes 405512 | tf_op jit(solution)/shard_map/ppermute | solution.py:524
  181.6 6.2 %collective-permute-start.16 = (s16[528,128]{1,0:T(8,128)(2,1)}, s16[528,128]{1,0:T(8,128)(2,1)S(1)}, u32[]{:S(2)}, u32[]{:S(2)}) collective-permute-start(s16[528,128]{1,0:T(8,128)(2,1)} %get-tuple-element.71), channel_id=1, source_target_pairs={{0,1},{1,0},{2,3},{3,2},{4,5},{5,4},{6,7},{7,6},{8,9},{9,8},{10,11... | collective-permute-start | bytes 405512 | tf_op jit(solution)/shard_map/ppermute | solution.py:524
  187.7 2.2 copy-start.13
  189.9 0.9 copy-start.17
  196.3 10.4 %copy-start.22 = (s32[8]{0:T(128)S(1)}, s32[8]{0:T(128)}, u32[]{:S(2)}) copy-start(s32[8]{0:T(128)} %constant.139.clone) | copy-start | bytes 100
  196.3 10.4 %copy-start.1 = (bf16[4,2,512,128]{3,2,1,0:T(8,128)(2,1)S(1)}, bf16[4,2,512,128]{3,2,1,0:T(8,128)(2,1)}, u32[]{:S(2)}) copy-start(bf16[4,2,512,128]{3,2,1,0:T(8,128)(2,1)} %get-tuple-element.45.refs_0_) | copy-start | bytes 3145732
  196.3 10.5 %copy-start.2 = (bf16[4,2,512,128]{3,2,1,0:T(8,128)(2,1)S(1)}, bf16[4,2,512,128]{3,2,1,0:T(8,128)(2,1)}, u32[]{:S(2)}) copy-start(bf16[4,2,512,128]{3,2,1,0:T(8,128)(2,1)} %get-tuple-element.48.refs_1_) | copy-start | bytes 3145732
  196.3 37.8 %all-to-all-start.3 = ((bf16[16,64,512]{2,1,0:T(8,128)(2,1)}), bf16[16,64,512]{2,1,0:T(8,128)(2,1)S(1)}, u32[]{:S(2)}, u32[]{:S(2)}) async-start(bf16[16,64,512]{2,1,0:T(8,128)(2,1)} %get-tuple-element.73), calls=%async_computation.3 | async-start | bytes 2097152 | tf_op jit(solution)/shard_map/all_to_all | solution.py:527
